TPU v7x, 32 devices: a whole 2x2x4 slice. The times are simulated.
32 devices in a mesh: groups: 2 (over y), adapter: 4 (over z), mp: 2 (over x), kv: 2 (over core).
Axes of the slice: x: 2, y: 2, z: 4, core: 2. Of those that a mesh axis runs over, the one named last changes fastest.
Arguments:
- queries: bfloat16 [384, 8192], P(('groups', 'adapter'), 'mp'), parts along dimension 0
- keys: bfloat16 [384, 128, 1024], P(('groups', 'adapter'), 'kv', 'mp'), parts along dimension 0
- values: bfloat16 [384, 128, 1024], P(('groups', 'adapter'), 'kv', 'mp'), parts along dimension 0, may hold values from -6 to 6
- lengths: int32 [384], P(('groups', 'adapter')), parts along dimension 0, may hold values from 1 to 128, as said below
- row_adapter_index: int32 [384], P('groups'), parts along dimension 0, may hold values from 0 to 31, as said below
- residual: bfloat16 [384, 8192], P(('groups', 'mp'), ('adapter', 'kv')), parts along dimension 0, may hold values from -4 to 4
- output_weight: bfloat16 [8192, 8192], P('mp', ('adapter', 'kv')), may hold values from -0.0625 to 0.0625
- adapter_down_weight: bfloat16 [32, 8192, 64], P('adapter', ('mp', 'kv')), may hold values from -0.0625 to 0.0625
- adapter_up_weight: bfloat16 [32, 64, 8192], P('mp', None, ('adapter', 'kv')), may hold values from -0.75 to 0.75
Outputs:
- layer_out: bfloat16 [384, 8192], P(('groups', 'mp'), ('adapter', 'kv')), parts along dimension 0
There are 2 independent parts, one for each index of `groups`. A program takes and returns all parts, laid end to end along the dimension named above; an argument that names none is the same for every part. Nothing has to cross between parts.
Inputs may be any that keep to these rules, and one draw needn't show every extreme that they name: `row_adapter_index`: among the 48 rows of each device (aligned blocks of the row order), the adapters of one owner (adapter // 8) are named by at most 24 rows, and by exactly 24 rows for some owner in every block. `lengths`: in every aligned block of 48 rows some row has 128 positions.
All inputs are finite; a program needn't handle non-finite values.
Results may differ from a plain program's by a relative error of at most 0.0053.
Values may be sent and summed in bfloat16 or wider, within the bound.
No kernel may reach another device: no remote copies, remote signals or barrier semaphores. Data moves between devices by JAX's collectives and lax.ppermute only.
A program may use at most 64 MiB of HBM per device.

v0:
```python
import math

import jax
import jax.numpy as jnp
from jax import lax
from jax.sharding import PartitionSpec as P

HD = 128


neg_big = -1e30
adapter_scale = 2.0


def merged_2(part, axis, combine):
    gathered = jax.tree.map(lambda a: lax.all_gather(a, axis), part)

    def take(source):
        return jax.tree.map(lambda a: lax.dynamic_index_in_dim(a, source, 0, False), gathered)

    return lax.fori_loop(
        1, lax.axis_size(axis), lambda source, state: combine(state, take(source)), take(0)
    )


def combine(first, second):
    top_first, sum_first, val_first = first
    top_second, sum_second, val_second = second
    joined = jnp.maximum(top_first, top_second)
    scale_first = jnp.exp(top_first - joined)
    scale_second = jnp.exp(top_second - joined)
    return (
        joined,
        sum_first * scale_first + sum_second * scale_second,
        val_first * scale_first[..., None] + val_second * scale_second[..., None],
    )


def attend(queries, keys, values, lengths):
    rows_dev = queries.shape[0]
    kv_local = keys.shape[2] // HD
    heads_local = queries.shape[1] // HD
    group = heads_local // kv_local
    local_len = keys.shape[1]
    offset = lax.axis_index("kv") * local_len
    query_heads = queries.reshape(rows_dev, kv_local, group, HD)
    key_heads = keys.reshape(rows_dev, local_len, kv_local, HD)
    value_heads = values.reshape(rows_dev, local_len, kv_local, HD)
    scores = jnp.einsum(
        "rgjd,rpgd->rgjp", query_heads, key_heads, preferred_element_type=jnp.float32
    ) * (1.0 / math.sqrt(HD))
    position = offset + lax.broadcasted_iota(jnp.int32, (rows_dev, local_len), 1)
    valid = (position < lengths[:, None])[:, None, None, :]
    masked = jnp.where(valid, scores, neg_big)
    row_top = jnp.max(masked, axis=3)
    weights = jnp.where(valid, jnp.exp(masked - row_top[..., None]), 0.0)
    weight_sum = jnp.sum(weights, axis=3)
    weighted = jnp.einsum(
        "rgjp,rpgd->rgjd", weights, value_heads.astype(jnp.float32), precision=lax.Precision.HIGHEST
    )
    merged = merged_2((row_top, weight_sum, weighted), "kv", combine)
    return (
        (merged[2] / merged[1][..., None]).reshape(rows_dev, heads_local * HD).astype(jnp.bfloat16)
    )


def slot_layout(row_adapter_index, rows_dev, adapter_placed):
    sources = row_adapter_index.shape[0] // rows_dev
    owner = row_adapter_index // adapter_placed
    blocked = owner.reshape(sources, rows_dev)
    same = blocked[:, :, None] == blocked[:, None, :]
    before = lax.broadcasted_iota(jnp.int32, (rows_dev, rows_dev), 1) < lax.broadcasted_iota(
        jnp.int32, (rows_dev, rows_dev), 0
    )
    rank = jnp.sum(jnp.where(same & before[None], 1, 0), axis=2).reshape(-1).astype(jnp.int32)
    source = jnp.arange(row_adapter_index.shape[0], dtype=jnp.int32) // rows_dev
    return (owner, source, rank)


def local(
    queries,
    keys,
    values,
    lengths,
    row_adapter_index,
    residual,
    output_weight,
    adapter_down_weight,
    adapter_up_weight,
):
    rows_dev = queries.shape[0]
    owners = lax.axis_size("adapter")
    capacity = 2 * rows_dev // owners
    adapter_placed = adapter_down_weight.shape[0]
    feature_portion = adapter_down_weight.shape[1]
    adapter_rank_width = adapter_down_weight.shape[2]
    entire_rows = row_adapter_index.shape[0]
    holder = lax.axis_index("adapter")
    half = lax.axis_index("kv")
    attention_output = attend(queries, keys, values, lengths)
    owner, source, rank = slot_layout(row_adapter_index, rows_dev, adapter_placed)
    member = row_adapter_index % adapter_placed
    slot_index = source * capacity + rank
    down_concat = jnp.transpose(adapter_down_weight, (1, 0, 2)).reshape(
        feature_portion, adapter_placed * adapter_rank_width
    )
    slot_iota = lax.broadcasted_iota(jnp.int32, (entire_rows, owners * capacity), 1)
    own_place = ((owner == holder)[:, None] & (slot_index[:, None] == slot_iota)).astype(
        jnp.float32
    )
    base_output = jnp.dot(
        lax.all_gather(attention_output, "adapter", axis=0, tiled=True),
        output_weight,
        preferred_element_type=jnp.float32,
    )
    my_feats = lax.dynamic_slice_in_dim(
        attention_output, half * feature_portion, feature_portion, 1
    )
    my_owner = lax.dynamic_slice_in_dim(owner, holder * rows_dev, rows_dev)
    my_rank = lax.dynamic_slice_in_dim(rank, holder * rows_dev, rows_dev)
    my_member = lax.dynamic_slice_in_dim(member, holder * rows_dev, rows_dev)
    columns = my_owner * capacity + my_rank
    place = columns[:, None] == lax.broadcasted_iota(jnp.int32, (rows_dev, owners * capacity), 1)
    outgoing = jnp.dot(place.T.astype(jnp.bfloat16), my_feats, preferred_element_type=jnp.float32)
    outgoing = outgoing.astype(jnp.bfloat16).reshape(owners, capacity, feature_portion)
    tags = jnp.sum(jnp.where(place, (my_member + 1)[:, None], 0), axis=0)
    tags = tags.astype(jnp.bfloat16).reshape(owners, capacity)
    rows_in = lax.all_to_all(outgoing, "adapter", split_axis=0, concat_axis=0, tiled=True)
    tags_in = lax.all_to_all(tags, "adapter", split_axis=0, concat_axis=0, tiled=True)
    flat = rows_in.reshape(-1, feature_portion)
    product = jnp.dot(flat, down_concat, preferred_element_type=jnp.float32).reshape(
        -1, adapter_placed, adapter_rank_width
    )
    member_iota = lax.broadcasted_iota(jnp.float32, (flat.shape[0], adapter_placed), 1)
    pick = (tags_in.astype(jnp.float32).reshape(-1, 1) - 1.0 == member_iota).astype(jnp.float32)
    slots = jnp.sum(product * pick[:, :, None], axis=1).reshape(
        rows_in.shape[0], rows_in.shape[1], adapter_rank_width
    )
    row_vectors = jnp.dot(
        own_place, slots.reshape(-1, adapter_rank_width), precision=lax.Precision.HIGHEST
    )
    lookup_table = lax.psum(row_vectors, ("adapter", "mp", "kv"))
    adapter_middle = lookup_table.astype(jnp.bfloat16)
    up_weight_count = adapter_up_weight.shape[0]
    local_id = row_adapter_index - lax.axis_index("mp") * up_weight_count
    selected_adapter = (
        local_id[:, None] == lax.broadcasted_iota(jnp.int32, (entire_rows, up_weight_count), 1)
    ).astype(jnp.bfloat16)
    spread_rows = (selected_adapter[:, :, None] * adapter_middle[:, None, :]).reshape(
        entire_rows, up_weight_count * adapter_rank_width
    )
    up_weight_flattened = adapter_up_weight.reshape(
        up_weight_count * adapter_rank_width, adapter_up_weight.shape[2]
    )
    partial_terms = base_output + adapter_scale * jnp.dot(
        spread_rows, up_weight_flattened, preferred_element_type=jnp.float32
    )
    summed = lax.psum_scatter(partial_terms, "mp", scatter_dimension=0, tiled=True)
    return (residual.astype(jnp.float32) + summed).astype(jnp.bfloat16)


def solution(mesh):
    placed = (
        P(("groups", "adapter"), "mp"),
        P(("groups", "adapter"), "kv", "mp"),
        P(("groups", "adapter"), "kv", "mp"),
        P(("groups", "adapter")),
        P("groups"),
        P(("groups", "mp"), ("adapter", "kv")),
        P("mp", ("adapter", "kv")),
        P("adapter", ("mp", "kv"), None),
        P("mp", None, ("adapter", "kv")),
    )
    return jax.shard_map(
        local,
        mesh=mesh,
        in_specs=placed,
        out_specs=P(("groups", "mp"), ("adapter", "kv")),
        check_vma=False,
    )
```

profile of v0, /device:TPU:0, one launch (start us, length us, event | category | flops | bytes accessed | tf_op | source)
XLA Modules:
  0.0 162.9 jit_solution(9968124663326220083)
XLA Ops:
  6.5 1.2 copy.20
  7.8 0.7 broadcast_compare_fusion
  8.5 3.7 %fusion.50 = (f32[48,4,8]{2,1,0:T(4,128)S(1)}, f32[48,4,8,64]{3,2,1,0:T(8,128)S(1)}) fusion(bf16[48,4,8,128]{3,2,1,0:T(8,128)(2,1)S(1)} %bitcast.60, pred[48,64]{1,0:T(8,128)(4,1)S(1)} %broadcast_compare_fusion, bf16[48,64,512]{2,1,0:T(8,128)(2,1)} %param.10), kind=kOutput, calls=%fused_computation.75 | convolution fusion | flops 25459200 | bytes 3941376 | tf_op jit(solution)/shard_map/rgjd,rpgd->rgjp/dot_general | solution.py:49
  12.2 0.9 copy-done.1
  13.1 3.5 %fusion = f32[48,4,8,128]{3,2,1,0:T(8,128)} fusion(f32[48,4,8,64]{3,2,1,0:T(8,128)S(1)} %get-tuple-element.37, f32[48,4,8]{2,1,0:T(4,128)S(1)} %get-tuple-element.36, pred[48,64]{1,0:T(8,128)(4,1)S(1)} %broadcast_compare_fusion, bf16[48,64,512]{2,1,0:T(8,128)(2,1)S(1)} %copy-done), kind=kOutput, calls=%fused_computation | convolution fusion | flops 151191552 | bytes 4334592 | tf_op jit(solution)/shard_map/rgjp,rpgd->rgjd/dot_general | solution.py:58
  16.8 2.0 %all-gather.1 = f32[96,4,8]{2,1,0:T(4,128)S(1)} all-gather(f32[48,4,8]{2,1,0:T(4,128)S(1)} %get-tuple-element.36), channel_id=3, replica_groups=mesh['groups'=2,'adapter'=4,'mp'=2,'kv'=2] {'kv'}, dimensions={0}, use_global_device_ids=true | all-gather | bytes 18432 | tf_op jit(solution)/shard_map/all_gather | solution.py:16
  18.8 1.7 %fusion.25 = f32[48,4,8]{2,1,0:T(4,128)S(1)} fusion(f32[48,4,8,64]{3,2,1,0:T(8,128)} %copy-done.1, f32[48,4,8]{2,1,0:T(4,128)S(1)} %get-tuple-element.36, pred[48,64]{1,0:T(8,128)(4,1)S(1)} %broadcast_compare_fusion), kind=kLoop, calls=%fused_computation.22 | loop fusion | flops 293376 | bytes 408576 | tf_op jit(solution)/shard_map/reduce_sum | solution.py:57
  20.5 1.9 %all-gather.2 = f32[96,4,8]{2,1,0:T(4,128)S(1)} all-gather(f32[48,4,8]{2,1,0:T(4,128)S(1)} %fusion.25), channel_id=4, replica_groups=mesh['groups'=2,'adapter'=4,'mp'=2,'kv'=2] {'kv'}, dimensions={0}, use_global_device_ids=true | all-gather | bytes 18432 | tf_op jit(solution)/shard_map/all_gather | solution.py:16
  22.5 6.9 %all-gather.8.cloned.1.call-done = f32[96,4,8,128]{3,2,1,0:T(8,128)} async-done(((f32[48,4,8,128]{3,2,1,0:T(8,128)}), f32[96,4,8,128]{3,2,1,0:T(8,128)}) %all-gather.8.cloned.1.call-update) | async-done | bytes 1572880 | tf_op jit(solution)/shard_map/all_gather | solution.py:16
  29.4 1.9 %fusion.24 = bf16[48,4,8,128]{3,2,1,0:T(8,128)(2,1)S(1)} fusion(f32[96,4,8,128]{3,2,1,0:T(8,128)} %all-gather.8.cloned.1.call-done, f32[48,4,8]{2,1,0:T(4,128)S(1)} %get-tuple-element.21, f32[48,4,8]{2,1,0:T(4,128)S(1)} %get-tuple-element.23, f32[48,4,8]{2,1,0:T(4,128)S(1)} %get-tuple-element.22), kind=kLoop, calls=%fused_computation.21 | loop fusion | flops 983040 | bytes 1984512 | tf_op jit(solution)/shard_map/convert_element_type | solution.py:63
  31.3 0.9 copy.37
  33.8 0.7 convert_element_type.66
  34.5 4.9 %all-to-all-start.1 = ((bf16[4,1,24]{2,1,0:T(2,128)(2,1)}), bf16[4,1,24]{2,1,0:T(2,128)(2,1)S(1)}, u32[]{:S(2)}, u32[]{:S(2)}) async-start(bf16[4,1,24]{2,1,0:T(2,128)(2,1)} %convert_element_type.66), calls=%async_computation.1 | async-start | bytes 4096 | tf_op jit(solution)/shard_map/all_to_all | solution.py:129
  39.4 2.1 %convolution_convert_fusion = bf16[96,2048]{1,0:T(8,128)(2,1)} fusion(bf16[48,4096]{1,0:T(8,128)(2,1)} %bitcast.58, s32[]{:T(128)S(6)} %select_n.60, s32[48]{0:T(128)S(1)} %get-tuple-element.39), kind=kOutput, calls=%fused_computation.6 | convolution fusion | flops 19075584 | bytes 590020 | tf_op jit(solution)/shard_map/dot_general | solution.py:124
  41.4 3.4 %all-to-all-done.1 = bf16[4,1,24]{2,1,0:T(2,128)(2,1)S(1)} async-done(((bf16[4,1,24]{2,1,0:T(2,128)(2,1)}), bf16[4,1,24]{2,1,0:T(2,128)(2,1)S(1)}, u32[]{:S(2)}, u32[]{:S(2)}) %all-to-all-start.1) | async-done | bytes 224 | tf_op jit(solution)/shard_map/all_to_all | solution.py:129
  44.8 3.5 %all-to-all-start = ((bf16[4,24,2048]{2,1,0:T(8,128)(2,1)}), bf16[4,24,2048]{2,1,0:T(8,128)(2,1)S(1)}, u32[]{:S(2)}, u32[]{:S(2)}) async-start(bf16[4,24,2048]{2,1,0:T(8,128)(2,1)} %bitcast), calls=%async_computation | async-start | bytes 786432 | tf_op jit(solution)/shard_map/all_to_all | solution.py:128
  49.6 20.9 %all-to-all-done = bf16[4,24,2048]{2,1,0:T(8,128)(2,1)S(1)} async-done(((bf16[4,24,2048]{2,1,0:T(8,128)(2,1)}), bf16[4,24,2048]{2,1,0:T(8,128)(2,1)S(1)}, u32[]{:S(2)}, u32[]{:S(2)}) %all-to-all-start) | async-done | bytes 393248 | tf_op jit(solution)/shard_map/all_to_all | solution.py:128
  70.6 2.3 %fusion.19 = f32[96,64]{0,1:T(8,128)S(1)} fusion(bf16[96,2048,1]{1,0,2:T(8,128)(2,1)S(1)} %bitcast.59, bf16[8,2048,64]{1,2,0:T(8,128)(2,1)} %param.16, f32[96,8]{0,1:T(8,128)S(1)} %fusion.43), kind=kOutput, calls=%fused_computation.15 | convolution fusion | flops 201418752 | bytes 2518016 | tf_op jit(solution)/shard_map/dot_general | solution.py:131
  72.9 1.0 fusion.37
  73.9 58.5 %psum.7 = bf16[192,64]{0,1:T(8,128)(2,1)S(1)} all-reduce(f32[192,64]{0,1:T(8,128)S(1)} %fusion.37), channel_id=1, replica_groups=mesh['groups'=2,'adapter'=4,'mp'=2,'kv'=2] {'adapter','mp','kv'}, use_global_device_ids=true, to_apply=%region_5.6 | all-reduce | flops 12288 | bytes 73728 | tf_op jit(solution)/shard_map/psum | solution.py:142
  132.5 5.8 %fusion.51 = f32[192,1024]{1,0:T(8,128)S(1)} fusion(bf16[192,4096]{1,0:T(8,128)(2,1)} %all-gather.6.cloned.1.call-done, bf16[4096,1024]{1,0:T(8,128)(2,1)} %param.15), kind=kOutput, calls=%fused_computation.76 | convolution fusion | flops 1610612736 | bytes 10747904 | tf_op jit(solution)/shard_map/dot_general | solution.py:111
  138.3 1.5 fusion.15
  139.8 14.8 %reduce-scatter.2.cloned.1.call-done = f32[96,1024]{1,0:T(8,128)} async-done(((f32[192,1024]{1,0:T(8,128)}), f32[96,1024]{1,0:T(8,128)}) %reduce-scatter.2.cloned.1.call-update) | async-done | bytes 393232 | tf_op jit(solution)/shard_map/reduce_scatter | solution.py:158
  154.6 1.7 %add_convert_fusion = bf16[96,1024]{1,0:T(8,128)(2,1)} fusion(f32[96,1024]{1,0:T(8,128)} %reduce-scatter.2.cloned.1.call-done, bf16[96,1024]{1,0:T(8,128)(2,1)S(1)} %copy-done.2), kind=kLoop, calls=%fused_computation.25 | loop fusion | flops 294912 | bytes 786432 | tf_op jit(solution)/shard_map/convert_element_type | solution.py:159
  (32 shorter events, 3.2 us)
Async XLA Ops:
  6.5 6.6 %copy-start = (bf16[48,64,512]{2,1,0:T(8,128)(2,1)S(1)}, bf16[48,64,512]{2,1,0:T(8,128)(2,1)}, u32[]{:S(2)}) copy-start(bf16[48,64,512]{2,1,0:T(8,128)(2,1)} %param.11) | copy-start | bytes 9437188
  6.5 22.8 %all-gather.8.cloned.1.call-start = ((), (), s32[]{:S(2)}) async-start(), calls=%async_computation.5 | async-start | bytes 2359296 | tf_op jit(solution)/shard_map/all_gather | solution.py:16
  12.2 0.9 copy-start.1
  16.7 15.5 %copy-start.3 = (s32[192]{0:T(256)S(1)}, s32[192]{0:T(256)}, u32[]{:S(2)}) copy-start(s32[192]{0:T(256)} %param.13) | copy-start | bytes 2308
  16.7 115.8 %all-gather.6.cloned.1.call-start = ((), (), s32[]{:S(2)}) async-start(), calls=%async_computation.3 | async-start | bytes 1966080 | tf_op jit(solution)/shard_map/all_gather | solution.py:112
  34.5 10.3 %all-to-all-start.1 = ((bf16[4,1,24]{2,1,0:T(2,128)(2,1)}), bf16[4,1,24]{2,1,0:T(2,128)(2,1)S(1)}, u32[]{:S(2)}, u32[]{:S(2)}) async-start(bf16[4,1,24]{2,1,0:T(2,128)(2,1)} %convert_element_type.66), calls=%async_computation.1 | async-start | bytes 4096 | tf_op jit(solution)/shard_map/all_to_all | solution.py:129
  44.8 25.8 %all-to-all-start = ((bf16[4,24,2048]{2,1,0:T(8,128)(2,1)}), bf16[4,24,2048]{2,1,0:T(8,128)(2,1)S(1)}, u32[]{:S(2)}, u32[]{:S(2)}) async-start(bf16[4,24,2048]{2,1,0:T(8,128)(2,1)} %bitcast), calls=%async_computation | async-start | bytes 786432 | tf_op jit(solution)/shard_map/all_to_all | solution.py:128
  48.3 106.3 %reduce-scatter.2.cloned.1.call-start = ((), (), s32[]{:S(2)}) async-start(), calls=%async_computation.4 | async-start | bytes 1179648 | tf_op jit(solution)/shard_map/reduce_scatter | solution.py:158
  132.5 5.8 %copy-start.4 = (bf16[16,64,1024]{2,1,0:T(8,128)(2,1)S(1)}, bf16[16,64,1024]{2,1,0:T(8,128)(2,1)}, u32[]{:S(2)}) copy-start(bf16[16,64,1024]{2,1,0:T(8,128)(2,1)} %param.17) | copy-start | bytes 6291460
  138.3 16.4 %copy-start.2 = (bf16[96,1024]{1,0:T(8,128)(2,1)S(1)}, bf16[96,1024]{1,0:T(8,128)(2,1)}, u32[]{:S(2)}) copy-start(bf16[96,1024]{1,0:T(8,128)(2,1)} %param.14) | copy-start | bytes 589828
Sparse Core Ops, SparseCore 0:
  16.8 12.4 all-gather.7
  32.3 46.7 all-gather.5
  139.9 14.6 reduce-scatter.1
where the time goes:
time: 163 us
  blocking collectives  62.5 us (38%)
  waiting for transfers between devices  46 us (28%)
  matrix products  20 us (12%)
  between operations  13.2 us (8%)
  other arithmetic  8.77 us (5%)
  starting transfers between devices  8.4 us (5%)
  local copies, waits for them, and re-layouts  3.93 us (2%)
    psum x1, blocking collectives, local(): lookup_table = lax.psum(row_vectors, ('adapter', 'mp', 'kv'))  58.5 us
    all_to_all x1, waiting for transfers between devices, local(): lax.all_to_all(outgoing, 'adapter', split_axis=0, concat_axis=0, tiled=True)  20.9 us
    reduce_scatter x1, waiting for transfers between devices, local(): lax.psum_scatter(partial_terms, 'mp', scatter_dimension=0, tiled=True)  14.8 us
    all_gather x1, waiting for transfers between devices, merged_2(): gathered = jax.tree.map(lambda a: lax.all_gather(a, axis), part)  6.86 us
    dot_general x1, matrix products, local(): jnp.dot(lax.all_gather(attention_output, 'adapter', axis=0, tiled=True),...  5.79 us
    all_to_all x1, starting transfers between devices, local(): lax.all_to_all(tags, 'adapter', split_axis=0, concat_axis=0, tiled=True)  4.86 us
    all_gather x2, blocking collectives, merged_2(): gathered = jax.tree.map(lambda a: lax.all_gather(a, axis), part)  3.99 us
    dot_general x1, matrix products, attend(): jnp.einsum('rgjd,rpgd->rgjp', query_heads, key_heads, preferred_element_t...  3.73 us
  transfers between devices with their start and end apart: 5, of which 4 were waited for; matrix products, arithmetic and copies ran while one was open for 7% of the time, Pallas kernels for 0%

commit v1 on v0

v1 whole, which is shorter than its diff:
```python
import functools
import math

import jax
import jax.numpy as jnp
from jax import lax
from jax.experimental import pallas as pl
from jax.experimental.pallas import tpu as pltpu
from jax.sharding import PartitionSpec as P

HD = 128
LANES = 128
MIB = 1 << 20

neg_big = -1e30
adapter_scale = 2.0
score_scale = 1.0 / math.sqrt(HD)
log2_e = 1.4426950408889634


vmem_spec = pl.BlockSpec(memory_space=pltpu.VMEM)


def whole(shape):
    return pl.BlockSpec(shape, lambda *_: (0,) * len(shape))


def attend_body(group, away, lengths, q_hbm, k_hbm, v_hbm, o_ref, s_ref, q_ref, k_ref, v_ref, sems):
    core = lax.axis_index("kv")
    half = 1 - core if away else core
    steps, positions = k_ref.shape[0], k_ref.shape[2]
    rows, features = q_ref.shape[1], q_ref.shape[2]
    kv_features = k_ref.shape[3]
    kv_heads = kv_features // HD
    offset = core * positions

    def copies(i):
        at = pl.ds(i * rows, rows)
        wide_at = pl.ds(pl.multiple_of(half * features, features), features)
        narrow_at = pl.ds(pl.multiple_of(half * kv_features, kv_features), kv_features)
        return (
            pltpu.make_async_copy(q_hbm.at[at, wide_at], q_ref.at[i], sems.at[0, i]),
            pltpu.make_async_copy(k_hbm.at[at, :, narrow_at], k_ref.at[i], sems.at[1, i]),
            pltpu.make_async_copy(v_hbm.at[at, :, narrow_at], v_ref.at[i], sems.at[2, i]),
        )

    for i in range(steps):
        for copy in copies(i):
            copy.start()

    wide = 8 * positions
    row_id = lax.broadcasted_iota(jnp.int32, (8, wide), 0)
    column = lax.broadcasted_iota(jnp.int32, (8, wide), 1)
    own_row = column // positions == row_id
    position = column % positions + offset
    lane = lax.broadcasted_iota(jnp.int32, (8, LANES), 1)
    ones = jnp.ones((wide, LANES), jnp.bfloat16)
    for i in range(steps):
        for copy in copies(i):
            copy.wait()
        queries = q_ref[i].astype(jnp.float32)
        outs = {}
        stats = []
        for sub in range(rows // 8):
            limit = jnp.zeros((8, wide), jnp.int32)
            for t in range(8):
                limit = jnp.where(row_id == t, lengths[i * rows + sub * 8 + t], limit)
            valid = own_row & (position < limit)
            stat = jnp.zeros((8, LANES), jnp.float32)
            for g in range(kv_heads):
                q = jnp.concatenate(
                    [
                        queries[sub * 8 : sub * 8 + 8, j * HD : (j + 1) * HD]
                        for j in range(g * group, (g + 1) * group)
                    ],
                    axis=0,
                ).astype(jnp.bfloat16)
                k = k_ref[i, sub * 8 : sub * 8 + 8, :, g * HD : (g + 1) * HD].reshape(wide, HD)
                v = v_ref[i, sub * 8 : sub * 8 + 8, :, g * HD : (g + 1) * HD].reshape(wide, HD)
                scores = lax.dot_general(
                    q, k, (((1,), (1,)), ((), ())), preferred_element_type=jnp.float32
                ).reshape(group, 8, wide)
                scores = jnp.where(valid[None], scores, neg_big)
                top = jnp.max(scores, axis=2, keepdims=True)
                weights = jnp.exp2((scores - top) * (score_scale * log2_e))
                weights = weights.astype(jnp.bfloat16).reshape(group * 8, wide)
                both = jnp.dot(
                    weights,
                    jnp.concatenate([v, ones], axis=1),
                    preferred_element_type=jnp.float32,
                )
                total = both[:, HD:]
                out = both[:, :HD] / total
                level = jnp.log2(total) + top.reshape(group * 8, 1) * (score_scale * log2_e)
                for j in range(group):
                    outs[sub, g * group + j] = out[j * 8 : j * 8 + 8]
                    stat = jnp.where(lane == g * group + j, level[j * 8 : j * 8 + 8], stat)
            stats.append(stat)
        at = slice(i * rows, (i + 1) * rows)
        for j in range(kv_heads * group):
            o_ref[at, j * HD : (j + 1) * HD] = jnp.concatenate(
                [outs[sub, j] for sub in range(rows // 8)], axis=0
            ).astype(o_ref.dtype)
        s_ref[at, :] = jnp.concatenate(stats, axis=0)


def attend(queries, keys, values, lengths, away, out_type):
    rows, features = queries.shape[0], queries.shape[1] // 2
    positions, kv_features = keys.shape[1], keys.shape[2] // 2
    block = 16
    steps = rows // block
    group = features // kv_features
    hbm = pl.BlockSpec(memory_space=pltpu.HBM)
    return pl.pallas_call(
        functools.partial(attend_body, group, away),
        in_specs=[pl.BlockSpec(memory_space=pltpu.SMEM), hbm, hbm, hbm],
        out_specs=[vmem_spec, vmem_spec],
        out_shape=[
            jax.ShapeDtypeStruct((rows, features), out_type),
            jax.ShapeDtypeStruct((rows, LANES), jnp.float32),
        ],
        scratch_shapes=[
            pltpu.VMEM((steps, block, features), jnp.bfloat16),
            pltpu.VMEM((steps, block, positions, kv_features), jnp.bfloat16),
            pltpu.VMEM((steps, block, positions, kv_features), jnp.bfloat16),
            pltpu.SemaphoreType.DMA((3, steps)),
        ],
        compiler_params=pltpu.CompilerParams(vmem_limit_bytes=12 * MIB),
        cost_estimate=pl.CostEstimate(
            flops=2_000_000_000, bytes_accessed=4_000_000, transcendentals=1_000_000
        ),
        name="attend",
    )(
        lengths,
        *(pltpu.with_memory_space_constraint(a, pltpu.HBM) for a in (queries, keys, values)),
    )


def merge_body(own_ref, own_level, other_ref, other_level, out_ref):
    share = 1.0 / (1.0 + jnp.exp2(own_level[...] - other_level[...]))
    for j in range(own_ref.shape[1] // HD):
        at = slice(j * HD, (j + 1) * HD)
        own = own_ref[:, at]
        other = other_ref[:, at].astype(jnp.float32)
        out_ref[:, at] = (own + (other - own) * share[:, j : j + 1]).astype(out_ref.dtype)


def merge(own, own_level, other, other_level):
    return pl.pallas_call(
        merge_body,
        out_shape=jax.ShapeDtypeStruct(own.shape, jnp.bfloat16),
        compiler_params=pltpu.CompilerParams(vmem_limit_bytes=8 * MIB),
        cost_estimate=pl.CostEstimate(
            flops=1_000_000, bytes_accessed=800_000, transcendentals=6_000
        ),
        name="merge",
    )(own, own_level, other, other_level)


def down_body(count, rank, ids_ref, d_ref, *refs):
    xs, out_ref = refs[:count], refs[count]
    picked_ref = refs[count + 1]
    me = lax.axis_index("adapter")
    rows = xs[0].shape[0]
    width = d_ref.shape[0]
    x = jnp.concatenate([r[...] for r in xs], axis=0) if count > 1 else xs[0][...]
    product = lax.dot_general(
        x, d_ref[...], (((1,), (1,)), ((), ())), preferred_element_type=jnp.float32
    )
    lane = lax.broadcasted_iota(jnp.int32, (rows, LANES), 1)
    per_tile = LANES // rank
    for j in range(count):
        source = lax.bitwise_xor(me, j) if count > 1 else 0
        at = pl.ds(pl.multiple_of(source * rows, 16), rows)
        member = ids_ref[at, :] - me * (width // rank)
        picked = jnp.zeros((rows, LANES), jnp.float32)
        for t in range(width // LANES):
            part = product[j * rows : (j + 1) * rows, t * LANES : (t + 1) * LANES]
            picked += jnp.where(member == t * per_tile + lane // rank, part, 0.0)
        picked_ref[at, :] = picked + pltpu.roll(picked, rank, 1)
    packed = out_ref.shape[0]
    left = lax.broadcasted_iota(jnp.int32, (packed, LANES), 1) < rank
    out_ref[...] = jnp.where(left, picked_ref[:packed, :], picked_ref[packed:, :])


def down(ids, weight, blocks):
    count, rows = len(blocks), len(blocks) * blocks[0].shape[0]
    rank = weight.shape[2]
    flat = jnp.transpose(weight, (0, 2, 1)).reshape(-1, weight.shape[1])
    return pl.pallas_call(
        functools.partial(down_body, count, rank),
        in_specs=[vmem_spec] * (2 + count),
        out_specs=vmem_spec,
        out_shape=jax.ShapeDtypeStruct((rows // 2, LANES), jnp.float32),
        scratch_shapes=[pltpu.VMEM((rows, LANES), jnp.float32)],
        compiler_params=pltpu.CompilerParams(vmem_limit_bytes=16 * MIB),
        cost_estimate=pl.CostEstimate(
            flops=2 * rows * flat.shape[0] * flat.shape[1],
            bytes_accessed=4_000_000,
            transcendentals=0,
        ),
        name="down",
    )(ids, flat, *blocks)


def up_body(count, rank, which, with_residual, ids_ref, base_ref, up_ref, *refs):
    mids, out_ref = refs[:count], refs[-1]
    side = lax.axis_index("mp")
    packed = mids[0][...]
    for r in mids[1:]:
        packed += r[...]
    packed = packed.astype(jnp.bfloat16).astype(jnp.float32)
    turned = pltpu.roll(packed, rank, 1)
    rows = out_ref.shape[0]
    left = lax.broadcasted_iota(jnp.int32, packed.shape, 1) < rank
    if which == "all":
        at = pl.ds(0, rows)
        total = jnp.concatenate(
            [jnp.where(left, packed, turned), jnp.where(left, turned, packed)], axis=0
        )
    else:
        part = side if which == "mine" else 1 - side
        at = pl.ds(pl.multiple_of(part * rows, 16), rows)
        total = jnp.where(left == (part == 0), packed, turned)
    lane = lax.broadcasted_iota(jnp.int32, (rows, LANES), 1)
    per_tile = LANES // rank
    local = ids_ref[at, :] - side * (up_ref.shape[0] // rank)
    spread = jnp.concatenate(
        [
            jnp.where(local == t * per_tile + lane // rank, total, 0.0)
            for t in range(up_ref.shape[0] // LANES)
        ],
        axis=1,
    ).astype(jnp.bfloat16)
    delta = jnp.dot(spread, up_ref[...], preferred_element_type=jnp.float32)
    out = base_ref[at, :] + adapter_scale * delta
    if with_residual:
        out += refs[count][...].astype(jnp.float32)
    out_ref[...] = out.astype(out_ref.dtype)


def up(ids, base, weight, mids, which, rows, residual, out_type):
    rank = weight.shape[1]
    flat = weight.reshape(-1, weight.shape[2])
    extra = [] if residual is None else [residual]
    return pl.pallas_call(
        functools.partial(up_body, len(mids), rank, which, residual is not None),
        in_specs=[vmem_spec] * (3 + len(mids) + len(extra)),
        out_specs=vmem_spec,
        out_shape=jax.ShapeDtypeStruct((rows, base.shape[1]), out_type),
        compiler_params=pltpu.CompilerParams(
            vmem_limit_bytes=(24 if which == "all" else 10) * MIB
        ),
        cost_estimate=pl.CostEstimate(
            flops=2 * rows * flat.shape[0] * flat.shape[1],
            bytes_accessed=3_000_000,
            transcendentals=0,
        ),
        name="up",
    )(ids, base, flat, *mids, *extra)


def last_body(kept_ref, back_ref, out_ref):
    out_ref[...] = (kept_ref[...] + back_ref[...].astype(jnp.float32)).astype(out_ref.dtype)


def last(kept, back):
    return pl.pallas_call(
        last_body,
        in_specs=[vmem_spec] * 2,
        out_specs=vmem_spec,
        out_shape=jax.ShapeDtypeStruct(kept.shape, jnp.bfloat16),
        compiler_params=pltpu.CompilerParams(vmem_limit_bytes=4 * MIB),
        name="last",
    )(kept, back)


def base_body(count, w_ref, *refs):
    xs, ys, out_ref = refs[:count], refs[count : 2 * count], refs[-1]
    me, half = lax.axis_index("adapter"), lax.axis_index("kv")
    rows, depth = xs[0].shape
    own = w_ref[pl.ds(pl.multiple_of(half * depth, depth), depth), :]
    other = w_ref[pl.ds(pl.multiple_of((1 - half) * depth, depth), depth), :]
    x = jnp.concatenate([r[...] for r in xs], axis=0) if count > 1 else xs[0][...]
    y = jnp.concatenate([r[...] for r in ys], axis=0) if count > 1 else ys[0][...]
    out = jnp.dot(x, own, preferred_element_type=jnp.float32)
    out += jnp.dot(y, other, preferred_element_type=jnp.float32)
    for j in range(count):
        source = lax.bitwise_xor(me, j) if count > 1 else 0
        at = pl.ds(pl.multiple_of(source * rows, 16), rows)
        out_ref[at, :] = out[j * rows : (j + 1) * rows]


def base_projection(weight, own, other):
    count = len(own)
    rows, depth = own[0].shape
    columns = weight.shape[1]
    tile = min(256, columns)
    return pl.pallas_call(
        functools.partial(base_body, count),
        grid=(columns // tile,),
        in_specs=[pl.BlockSpec((2 * depth, tile), lambda i: (0, i))]
        + [whole((rows, depth))] * (2 * count),
        out_specs=pl.BlockSpec((count * rows, tile), lambda i: (0, i)),
        out_shape=jax.ShapeDtypeStruct((count * rows, columns), jnp.float32),
        compiler_params=pltpu.CompilerParams(vmem_limit_bytes=24 * MIB),
        cost_estimate=pl.CostEstimate(
            flops=4 * count * rows * depth * columns,
            bytes_accessed=10_000_000,
            transcendentals=0,
        ),
        name="base",
    )(weight, *own, *other)


def swapped(x, axis, other=1):
    return lax.ppermute(x, axis, [(i, i ^ other) for i in range(lax.axis_size(axis))])


def local(
    queries,
    keys,
    values,
    lengths,
    row_adapter_index,
    residual,
    output_weight,
    adapter_down_weight,
    adapter_up_weight,
):
    owners, splits = lax.axis_size("adapter"), lax.axis_size("mp")
    entire_rows = row_adapter_index.shape[0]
    kept_rows = entire_rows // splits
    direct = owners == 4 and splits == 2
    ids = jnp.broadcast_to(row_adapter_index[:, None], (entire_rows, LANES))

    sent, sent_level = attend(queries, keys, values, lengths, True, jnp.float32)
    got, got_level = swapped(sent, "kv"), swapped(sent_level, "kv")
    own, own_level = attend(queries, keys, values, lengths, False, jnp.float32)
    attended = merge(own, own_level, got, got_level)

    if direct:
        blocks = [attended] + [swapped(attended, "adapter", j) for j in range(1, owners)]
    else:
        blocks = [lax.all_gather(attended, "adapter", axis=0, tiled=True)]
    others = [swapped(b, "kv") for b in blocks]
    part = down(ids, adapter_down_weight, blocks)
    base = base_projection(output_weight, blocks, others)

    if direct:
        part = part + swapped(part, "kv")
        part = part + swapped(part, "mp")
        mids = [part] + [swapped(part, "adapter", j) for j in range(1, owners)]
        away = up(
            ids, base, adapter_up_weight, mids, "theirs", kept_rows, None, jnp.bfloat16
        )
        back = swapped(away, "mp")
        kept = up(
            ids, base, adapter_up_weight, mids, "mine", kept_rows, residual, jnp.float32
        )
        return last(kept, back)
    mids = [lax.psum(part, ("adapter", "mp", "kv"))]
    terms = up(ids, base, adapter_up_weight, mids, "all", entire_rows, None, jnp.float32)
    summed = lax.psum_scatter(terms, "mp", scatter_dimension=0, tiled=True)
    return (residual.astype(jnp.float32) + summed).astype(jnp.bfloat16)


def solution(mesh):
    placed = (
        P(("groups", "adapter"), "mp"),
        P(("groups", "adapter"), "kv", "mp"),
        P(("groups", "adapter"), "kv", "mp"),
        P(("groups", "adapter")),
        P("groups"),
        P(("groups", "mp"), ("adapter", "kv")),
        P("mp", ("adapter", "kv")),
        P("adapter", ("mp", "kv"), None),
        P("mp", None, ("adapter", "kv")),
    )
    return jax.shard_map(
        local,
        mesh=mesh,
        in_specs=placed,
        out_specs=P(("groups", "mp"), ("adapter", "kv")),
        check_vma=False,
    )
```

time: 163 us -> 54.6 us (0.33)
  blocking collectives: 62.5 us -> 0 us
  waiting for transfers between devices: 46 us -> 22.9 us
  matrix products: 20 us -> 0 us
  Pallas kernels: 0 us -> 14.8 us
  between operations: 13.2 us -> 0.14 us
  other arithmetic: 8.77 us -> 0.01 us
  starting transfers between devices: 8.4 us -> 15.8 us
  local copies, waits for them, and re-layouts: 3.93 us -> 0.76 us
    psum x1 -> x0, blocking collectives: 58.5 us -> none  [local(): lookup_table = lax.psum(row_vectors, ('adapter', 'mp', 'kv'))]
    all_to_all x2 -> x0, waiting for transfers between devices: 24.3 us -> none  [the longest x1 20.9 us: local(): lax.all_to_all(outgoing, 'adapter', split_axis=0, concat_axis=0, tiled=True)]
    ppermute x0 -> x15, waiting for transfers between devices: none -> 22.9 us  [swapped(): lax.ppermute(x, axis, [(i, i ^ other) for i in range(lax.axis_size(axis))])]
    dot_general x7 -> x0, matrix products: 20 us -> none  [the longest x1 5.79 us: local(): jnp.dot(lax.all_gather(attention_output, 'adapter', axis=0, tiled=True),...]
    ppermute x0 -> x15, starting transfers between devices: none -> 15.8 us  [swapped(): lax.ppermute(x, axis, [(i, i ^ other) for i in range(lax.axis_size(axis))])]
    reduce_scatter x1 -> x0, waiting for transfers between devices: 14.8 us -> none  [local(): lax.psum_scatter(partial_terms, 'mp', scatter_dimension=0, tiled=True)]
    pallas_call x0 -> x8, Pallas kernels: none -> 14.8 us  [the longest x2 8.29 us: attend(): pl.pallas_call(functools.partial(attend_body, group, away), in_specs=[pl....]
    all_to_all x2 -> x0, starting transfers between devices: 8.32 us -> none  [the longest x1 4.86 us: local(): lax.all_to_all(tags, 'adapter', split_axis=0, concat_axis=0, tiled=True)]
  transfers between devices with their start and end apart: 5 -> 15, of which waited for: 4 -> 6; matrix products, arithmetic and copies ran while one was open for 7% -> 0% of each run, Pallas kernels for 0% -> 17%
where the time goes in v1:
time: 54.6 us; the launch traced here: 54.4 us
  waiting for transfers between devices  22.9 us (42%)
  starting transfers between devices  15.8 us (29%)
  Pallas kernels  14.8 us (27%)
  local copies, waits for them, and re-layouts  0.76 us (1%)
    ppermute x15, waiting for transfers between devices, swapped(): lax.ppermute(x, axis, [(i, i ^ other) for i in range(lax.axis_size(axis))])  22.9 us
    ppermute x15, starting transfers between devices, swapped(): lax.ppermute(x, axis, [(i, i ^ other) for i in range(lax.axis_size(axis))])  15.8 us
    pallas_call x2, Pallas kernels, attend(): pl.pallas_call(functools.partial(attend_body, group, away), in_specs=[pl....  8.29 us
    pallas_call x1, Pallas kernels, base_projection(): pl.pallas_call(functools.partial(base_body, count), grid=(columns // tile...  3.57 us
  transfers between devices with their start and end apart: 15, of which 6 were waited for; matrix products, arithmetic and copies ran while one was open for 0% of the time, Pallas kernels for 17%

profile of v1, /device:TPU:0, one launch (start us, length us, event | category | flops | bytes accessed | tf_op | source)
XLA Modules:
  0.0 54.4 jit_solution(1732290886524207200)
XLA Ops:
  0.0 0.7 %copy-done.3 = s32[48]{0:T(128)S(1)} copy-done((s32[48]{0:T(128)S(1)}, s32[48]{0:T(128)}, u32[]{:S(2)}) %copy-start.3) | copy-done | bytes 216
  0.7 4.2 %attend.3 = (f32[48,2048]{1,0:T(8,128)S(1)}, f32[48,128]{1,0:T(8,128)S(1)}) custom-call(s32[48]{0:T(128)S(1)} %copy-done.3, bf16[48,4096]{1,0:T(8,128)(2,1)} %q_hbm.3, bf16[48,64,512]{2,1,0:T(8,128)(2,1)} %k_hbm.3, bf16[48,64,512]{2,1,0:T(8,128)(2,1)} %v_hbm.3), custom_call_target="tpu_custom_call" | custom-call | flops 2000000000 | bytes 4000000 | tf_op jit(solution)/shard_map/attend/pallas_call | solution.py:114
  4.9 0.5 collective-permute-start
  5.5 4.1 %attend.2 = (f32[48,2048]{1,0:T(8,128)S(1)}, f32[48,128]{1,0:T(8,128)S(1)}) custom-call(s32[48]{0:T(128)S(1)} %copy-done.3, bf16[48,4096]{1,0:T(8,128)(2,1)} %q_hbm.3, bf16[48,64,512]{2,1,0:T(8,128)(2,1)} %k_hbm.3, bf16[48,64,512]{2,1,0:T(8,128)(2,1)} %v_hbm.3), custom_call_target="tpu_custom_call" | custom-call | flops 2000000000 | bytes 4000000 | tf_op jit(solution)/shard_map/attend/pallas_call | solution.py:114
  9.6 0.2 merge.1.refs_0_
  9.8 3.1 %collective-permute-start.2 = (bf16[48,2048]{1,0:T(8,128)(2,1)S(1)}, bf16[48,2048]{1,0:T(8,128)(2,1)S(1)}, u32[]{:S(2)}, u32[]{:S(2)}) collective-permute-start(bf16[48,2048]{1,0:T(8,128)(2,1)S(1)} %merge.1.refs_0_), channel_id=1, source_target_pairs={{0,4},{4,0},{8,12},{12,8},{1,5},{5,1},{9,13},{13,9},{2,6},{6,2},{1... | collective-permute-start | bytes 589832 | tf_op jit(solution)/shard_map/ppermute | solution.py:317
  13.0 2.6 %collective-permute-start.3 = (bf16[48,2048]{1,0:T(8,128)(2,1)S(1)}, bf16[48,2048]{1,0:T(8,128)(2,1)S(1)}, u32[]{:S(2)}, u32[]{:S(2)}) collective-permute-start(bf16[48,2048]{1,0:T(8,128)(2,1)S(1)} %merge.1.refs_0_), channel_id=1, source_target_pairs={{0,8},{4,12},{8,0},{12,4},{1,9},{5,13},{9,1},{13,5},{2,10},{6,14},... | collective-permute-start | bytes 589832 | tf_op jit(solution)/shard_map/ppermute | solution.py:317
  15.6 6.1 %collective-permute-done.2.refs_1_ = bf16[48,2048]{1,0:T(8,128)(2,1)S(1)} collective-permute-done((bf16[48,2048]{1,0:T(8,128)(2,1)S(1)}, bf16[48,2048]{1,0:T(8,128)(2,1)S(1)}, u32[]{:S(2)}, u32[]{:S(2)}) %collective-permute-start.2) | collective-permute-done | bytes 196640 | tf_op jit(solution)/shard_map/ppermute | solution.py:317
  21.6 8.5 %collective-permute-done.3.refs_2_ = bf16[48,2048]{1,0:T(8,128)(2,1)S(1)} collective-permute-done((bf16[48,2048]{1,0:T(8,128)(2,1)S(1)}, bf16[48,2048]{1,0:T(8,128)(2,1)S(1)}, u32[]{:S(2)}, u32[]{:S(2)}) %collective-permute-start.3) | collective-permute-done | bytes 196640 | tf_op jit(solution)/shard_map/ppermute | solution.py:317
  30.1 0.5 collective-permute-start.8
  30.7 0.9 %down.1 = f32[96,128]{1,0:T(8,128)S(1)} custom-call(s32[192,128]{1,0:T(8,128)S(1)} %broadcast_in_dim.2.ids_ref, bf16[512,2048]{1,0:T(8,128)(2,1)S(1)} %bitcast.8, bf16[48,2048]{1,0:T(8,128)(2,1)S(1)} %merge.1.refs_0_, bf16[48,2048]{1,0:T(8,128)(2,1)S(1)} %collective-permute-done.2.refs_1_, bf16[48,2048]{1,0:T(8,128)(2,1)S(1)} %collective-permute-done.3.refs_2_, ...), custom_call_target="tpu_custom_call" | custom-call | flops 402653184 | bytes 4000000 | tf_op jit(solution)/shard_map/down/pallas_call | solution.py:190
  31.7 1.2 %collective-permute-done.9 = f32[96,128]{1,0:T(8,128)S(1)} collective-permute-done((f32[96,128]{1,0:T(8,128)S(1)}, f32[96,128]{1,0:T(8,128)S(1)}, u32[]{:S(2)}, u32[]{:S(2)}) %collective-permute-start.9) | collective-permute-done | bytes 49184 | tf_op jit(solution)/shard_map/ppermute | solution.py:317
  32.9 1.5 %collective-permute-start.10 = (f32[96,128]{1,0:T(8,128)S(1)}, f32[96,128]{1,0:T(8,128)S(1)}, u32[]{:S(2)}, u32[]{:S(2)}) collective-permute-start(f32[96,128]{1,0:T(8,128)S(1)} %add.6), channel_id=1, source_target_pairs={{0,2},{2,0},{1,3},{3,1},{4,6},{6,4},{5,7},{7,5},{8,10},{10,8},{9,1... | collective-permute-start | bytes 147464 | tf_op jit(solution)/shard_map/ppermute | solution.py:317
  34.5 2.6 %collective-permute-done.10 = f32[96,128]{1,0:T(8,128)S(1)} collective-permute-done((f32[96,128]{1,0:T(8,128)S(1)}, f32[96,128]{1,0:T(8,128)S(1)}, u32[]{:S(2)}, u32[]{:S(2)}) %collective-permute-start.10) | collective-permute-done | bytes 49184 | tf_op jit(solution)/shard_map/ppermute | solution.py:317
  37.1 3.2 %collective-permute-start.11 = (f32[96,128]{1,0:T(8,128)S(1)}, f32[96,128]{1,0:T(8,128)S(1)}, u32[]{:S(2)}, u32[]{:S(2)}) collective-permute-start(f32[96,128]{1,0:T(8,128)S(1)} %add.7.refs_0_), channel_id=1, source_target_pairs={{0,4},{4,0},{8,12},{12,8},{1,5},{5,1},{9,13},{13,9},{2,6},{6,2},{1... | collective-permute-start | bytes 147464 | tf_op jit(solution)/shard_map/ppermute | solution.py:317
  40.3 1.1 %collective-permute-start.12 = (f32[96,128]{1,0:T(8,128)S(1)}, f32[96,128]{1,0:T(8,128)S(1)}, u32[]{:S(2)}, u32[]{:S(2)}) collective-permute-start(f32[96,128]{1,0:T(8,128)S(1)} %add.7.refs_0_), channel_id=1, source_target_pairs={{0,8},{4,12},{8,0},{12,4},{1,9},{5,13},{9,1},{13,5},{2,10},{6,14},... | collective-permute-start | bytes 147464 | tf_op jit(solution)/shard_map/ppermute | solution.py:317
  41.4 1.4 %collective-permute-start.13 = (f32[96,128]{1,0:T(8,128)S(1)}, f32[96,128]{1,0:T(8,128)S(1)}, u32[]{:S(2)}, u32[]{:S(2)}) collective-permute-start(f32[96,128]{1,0:T(8,128)S(1)} %add.7.refs_0_), channel_id=1, source_target_pairs={{0,12},{4,8},{8,4},{12,0},{1,13},{5,9},{9,5},{13,1},{2,14},{6,10},... | collective-permute-start | bytes 147464 | tf_op jit(solution)/shard_map/ppermute | solution.py:317
  42.9 3.6 %base.1.base_ref = f32[192,1024]{1,0:T(8,128)S(1)} custom-call(bf16[4096,1024]{1,0:T(8,128)(2,1)S(1)} %bitcast.7, bf16[48,2048]{1,0:T(8,128)(2,1)S(1)} %merge.1.refs_0_, bf16[48,2048]{1,0:T(8,128)(2,1)S(1)} %collective-permute-done.2.refs_1_, bf16[48,2048]{1,0:T(8,128)(2,1)S(1)} %collective-permute-done.3.refs_2_, ...), custom_call_target="tpu_custom_call" | custom-call | flops 1610612736 | bytes 10000000 | tf_op jit(solution)/shard_map/base/pallas_call | solution.py:299
  46.5 0.9 %collective-permute-done.13.refs_3_ = f32[96,128]{1,0:T(8,128)S(1)} collective-permute-done((f32[96,128]{1,0:T(8,128)S(1)}, f32[96,128]{1,0:T(8,128)S(1)}, u32[]{:S(2)}, u32[]{:S(2)}) %collective-permute-start.13) | collective-permute-done | bytes 49184 | tf_op jit(solution)/shard_map/ppermute | solution.py:317
  47.4 0.5 up.3
  48.0 1.6 %collective-permute-start.14 = (bf16[96,1024]{1,0:T(8,128)(2,1)S(1)}, bf16[96,1024]{1,0:T(8,128)(2,1)S(1)}, u32[]{:S(2)}, u32[]{:S(2)}) collective-permute-start(bf16[96,1024]{1,0:T(8,128)(2,1)S(1)} %up.3), channel_id=1, source_target_pairs={{0,2},{2,0},{1,3},{3,1},{4,6},{6,4},{5,7},{7,5},{8,10},{10,8},{9,1... | collective-permute-start | bytes 589832 | tf_op jit(solution)/shard_map/ppermute | solution.py:317
  49.5 0.5 up.2.kept_ref
  50.0 3.6 %collective-permute-done.14.back_ref = bf16[96,1024]{1,0:T(8,128)(2,1)S(1)} collective-permute-done((bf16[96,1024]{1,0:T(8,128)(2,1)S(1)}, bf16[96,1024]{1,0:T(8,128)(2,1)S(1)}, u32[]{:S(2)}, u32[]{:S(2)}) %collective-permute-start.14) | collective-permute-done | bytes 196640 | tf_op jit(solution)/shard_map/ppermute | solution.py:317
  53.7 0.7 %last.1 = bf16[96,1024]{1,0:T(8,128)(2,1)} custom-call(f32[96,1024]{1,0:T(8,128)S(1)} %up.2.kept_ref, bf16[96,1024]{1,0:T(8,128)(2,1)S(1)} %collective-permute-done.14.back_ref), custom_call_target="tpu_custom_call" | custom-call | tf_op jit(solution)/shard_map/last/pallas_call | solution.py:268
  (32 shorter events, 0.3 us)
Async XLA Ops:
  0.0 0.7 %copy-start.3 = (s32[48]{0:T(128)S(1)}, s32[48]{0:T(128)}, u32[]{:S(2)}) copy-start(s32[48]{0:T(128)} %lengths.3) | copy-start | bytes 580
  0.7 42.2 %slice-start = ((s8[8388608]{0:T(1024)(128)(4,1)}), s8[4194304]{0:T(1024)(128)(4,1)S(1)}, s32[]{:S(2)}) async-start(s8[8388608]{0:T(1024)(128)(4,1)} %bitcast.6), calls=%async_computation | async-start | bytes 8388608
  4.9 4.7 %collective-permute-start = (f32[48,2048]{1,0:T(8,128)S(1)}, f32[48,2048]{1,0:T(8,128)S(1)}, u32[]{:S(2)}, u32[]{:S(2)}) collective-permute-start(f32[48,2048]{1,0:T(8,128)S(1)} %get-tuple-element.11), channel_id=1, source_target_pairs={{0,1},{1,0},{2,3},{3,2},{4,5},{5,4},{6,7},{7,6},{8,9},{9,8},{10,11... | collective-permute-start | bytes 1179656 | tf_op jit(solution)/shard_map/ppermute | solution.py:317
  5.4 25.2 %copy-start.4 = (s32[192]{0:T(256)S(1)}, s32[192]{0:T(256)}, u32[]{:S(2)}) copy-start(s32[192]{0:T(256)} %param.13) | copy-start | bytes 2308
  5.4 25.3 %copy-start.1 = (bf16[8,2048,64]{1,2,0:T(8,128)(2,1)S(1)}, bf16[8,2048,64]{1,2,0:T(8,128)(2,1)}, u32[]{:S(2)}) copy-start(bf16[8,2048,64]{1,2,0:T(8,128)(2,1)} %param.16) | copy-start | bytes 6291460
  5.4 37.5 %slice-start.1 = ((s8[8388608]{0:T(1024)(128)(4,1)}), s8[4194304]{0:T(1024)(128)(4,1)S(1)}, s32[]{:S(2)}) async-start(s8[8388608]{0:T(1024)(128)(4,1)} %bitcast.6), calls=%async_computation.1 | async-start | bytes 8388608
  5.4 4.2 %collective-permute-start.1 = (f32[48,128]{1,0:T(8,128)S(1)}, f32[48,128]{1,0:T(8,128)S(1)}, u32[]{:S(2)}, u32[]{:S(2)}) collective-permute-start(f32[48,128]{1,0:T(8,128)S(1)} %get-tuple-element.12), channel_id=1, source_target_pairs={{0,1},{1,0},{2,3},{3,2},{4,5},{5,4},{6,7},{7,6},{8,9},{9,8},{10,11... | collective-permute-start | bytes 73736 | tf_op jit(solution)/shard_map/ppermute | solution.py:317
  9.8 11.8 %collective-permute-start.2 = (bf16[48,2048]{1,0:T(8,128)(2,1)S(1)}, bf16[48,2048]{1,0:T(8,128)(2,1)S(1)}, u32[]{:S(2)}, u32[]{:S(2)}) collective-permute-start(bf16[48,2048]{1,0:T(8,128)(2,1)S(1)} %merge.1.refs_0_), channel_id=1, source_target_pairs={{0,4},{4,0},{8,12},{12,8},{1,5},{5,1},{9,13},{13,9},{2,6},{6,2},{1... | collective-permute-start | bytes 589832 | tf_op jit(solution)/shard_map/ppermute | solution.py:317
  13.0 17.1 %collective-permute-start.3 = (bf16[48,2048]{1,0:T(8,128)(2,1)S(1)}, bf16[48,2048]{1,0:T(8,128)(2,1)S(1)}, u32[]{:S(2)}, u32[]{:S(2)}) collective-permute-start(bf16[48,2048]{1,0:T(8,128)(2,1)S(1)} %merge.1.refs_0_), channel_id=1, source_target_pairs={{0,8},{4,12},{8,0},{12,4},{1,9},{5,13},{9,1},{13,5},{2,10},{6,14},... | collective-permute-start | bytes 589832 | tf_op jit(solution)/shard_map/ppermute | solution.py:317
  15.5 14.5 %collective-permute-start.4 = (bf16[48,2048]{1,0:T(8,128)(2,1)S(1)}, bf16[48,2048]{1,0:T(8,128)(2,1)S(1)}, u32[]{:S(2)}, u32[]{:S(2)}) collective-permute-start(bf16[48,2048]{1,0:T(8,128)(2,1)S(1)} %merge.1.refs_0_), channel_id=1, source_target_pairs={{0,12},{4,8},{8,4},{12,0},{1,13},{5,9},{9,5},{13,1},{2,14},{6,10},... | collective-permute-start | bytes 589832 | tf_op jit(solution)/shard_map/ppermute | solution.py:317
  15.6 24.8 %collective-permute-start.5 = (bf16[48,2048]{1,0:T(8,128)(2,1)S(1)}, bf16[48,2048]{1,0:T(8,128)(2,1)S(1)}, u32[]{:S(2)}, u32[]{:S(2)}) collective-permute-start(bf16[48,2048]{1,0:T(8,128)(2,1)S(1)} %merge.1.refs_0_), channel_id=1, source_target_pairs={{0,1},{1,0},{2,3},{3,2},{4,5},{5,4},{6,7},{7,6},{8,9},{9,8},{10,11... | collective-permute-start | bytes 589832 | tf_op jit(solution)/shard_map/ppermute | solution.py:317
  21.6 19.8 %collective-permute-start.6 = (bf16[48,2048]{1,0:T(8,128)(2,1)S(1)}, bf16[48,2048]{1,0:T(8,128)(2,1)S(1)}, u32[]{:S(2)}, u32[]{:S(2)}) collective-permute-start(bf16[48,2048]{1,0:T(8,128)(2,1)S(1)} %collective-permute-done.2.refs_1_), channel_id=1, source_target_pairs={{0,1},{1,0},{2,3},{3,2},{4,5},{5,4},{6,7},{7,6},{8,9},{9,8},{10,11... | collective-permute-start | bytes 589832 | tf_op jit(solution)/shard_map/ppermute | solution.py:317
  30.1 12.8 %collective-permute-start.7 = (bf16[48,2048]{1,0:T(8,128)(2,1)S(1)}, bf16[48,2048]{1,0:T(8,128)(2,1)S(1)}, u32[]{:S(2)}, u32[]{:S(2)}) collective-permute-start(bf16[48,2048]{1,0:T(8,128)(2,1)S(1)} %collective-permute-done.3.refs_2_), channel_id=1, source_target_pairs={{0,1},{1,0},{2,3},{3,2},{4,5},{5,4},{6,7},{7,6},{8,9},{9,8},{10,11... | collective-permute-start | bytes 589832 | tf_op jit(solution)/shard_map/ppermute | solution.py:317
  30.1 12.8 %collective-permute-start.8 = (bf16[48,2048]{1,0:T(8,128)(2,1)S(1)}, bf16[48,2048]{1,0:T(8,128)(2,1)S(1)}, u32[]{:S(2)}, u32[]{:S(2)}) collective-permute-start(bf16[48,2048]{1,0:T(8,128)(2,1)S(1)} %collective-permute-done.4.refs_3_), channel_id=1, source_target_pairs={{0,1},{1,0},{2,3},{3,2},{4,5},{5,4},{6,7},{7,6},{8,9},{9,8},{10,11... | collective-permute-start | bytes 589832 | tf_op jit(solution)/shard_map/ppermute | solution.py:317
  31.6 1.3 %collective-permute-start.9 = (f32[96,128]{1,0:T(8,128)S(1)}, f32[96,128]{1,0:T(8,128)S(1)}, u32[]{:S(2)}, u32[]{:S(2)}) collective-permute-start(f32[96,128]{1,0:T(8,128)S(1)} %down.1), channel_id=1, source_target_pairs={{0,1},{1,0},{2,3},{3,2},{4,5},{5,4},{6,7},{7,6},{8,9},{9,8},{10,11... | collective-permute-start | bytes 147464 | tf_op jit(solution)/shard_map/ppermute | solution.py:317
  32.9 4.2 %collective-permute-start.10 = (f32[96,128]{1,0:T(8,128)S(1)}, f32[96,128]{1,0:T(8,128)S(1)}, u32[]{:S(2)}, u32[]{:S(2)}) collective-permute-start(f32[96,128]{1,0:T(8,128)S(1)} %add.6), channel_id=1, source_target_pairs={{0,2},{2,0},{1,3},{3,1},{4,6},{6,4},{5,7},{7,5},{8,10},{10,8},{9,1... | collective-permute-start | bytes 147464 | tf_op jit(solution)/shard_map/ppermute | solution.py:317
  37.1 10.3 %copy-start = (bf16[16,64,1024]{2,1,0:T(8,128)(2,1)S(1)}, bf16[16,64,1024]{2,1,0:T(8,128)(2,1)}, u32[]{:S(2)}) copy-start(bf16[16,64,1024]{2,1,0:T(8,128)(2,1)} %param.17) | copy-start | bytes 6291460
  37.1 9.4 %collective-permute-start.11 = (f32[96,128]{1,0:T(8,128)S(1)}, f32[96,128]{1,0:T(8,128)S(1)}, u32[]{:S(2)}, u32[]{:S(2)}) collective-permute-start(f32[96,128]{1,0:T(8,128)S(1)} %add.7.refs_0_), channel_id=1, source_target_pairs={{0,4},{4,0},{8,12},{12,8},{1,5},{5,1},{9,13},{13,9},{2,6},{6,2},{1... | collective-permute-start | bytes 147464 | tf_op jit(solution)/shard_map/ppermute | solution.py:317
  40.3 6.2 %collective-permute-start.12 = (f32[96,128]{1,0:T(8,128)S(1)}, f32[96,128]{1,0:T(8,128)S(1)}, u32[]{:S(2)}, u32[]{:S(2)}) collective-permute-start(f32[96,128]{1,0:T(8,128)S(1)} %add.7.refs_0_), channel_id=1, source_target_pairs={{0,8},{4,12},{8,0},{12,4},{1,9},{5,13},{9,1},{13,5},{2,10},{6,14},... | collective-permute-start | bytes 147464 | tf_op jit(solution)/shard_map/ppermute | solution.py:317
  41.4 6.0 %collective-permute-start.13 = (f32[96,128]{1,0:T(8,128)S(1)}, f32[96,128]{1,0:T(8,128)S(1)}, u32[]{:S(2)}, u32[]{:S(2)}) collective-permute-start(f32[96,128]{1,0:T(8,128)S(1)} %add.7.refs_0_), channel_id=1, source_target_pairs={{0,12},{4,8},{8,4},{12,0},{1,13},{5,9},{9,5},{13,1},{2,14},{6,10},... | collective-permute-start | bytes 147464 | tf_op jit(solution)/shard_map/ppermute | solution.py:317
  46.5 3.0 %copy-start.2 = (bf16[96,1024]{1,0:T(8,128)(2,1)S(1)}, bf16[96,1024]{1,0:T(8,128)(2,1)}, u32[]{:S(2)}) copy-start(bf16[96,1024]{1,0:T(8,128)(2,1)} %refs_4_.1) | copy-start | bytes 589828
  48.0 5.7 %collective-permute-start.14 = (bf16[96,1024]{1,0:T(8,128)(2,1)S(1)}, bf16[96,1024]{1,0:T(8,128)(2,1)S(1)}, u32[]{:S(2)}, u32[]{:S(2)}) collective-permute-start(bf16[96,1024]{1,0:T(8,128)(2,1)S(1)} %up.3), channel_id=1, source_target_pairs={{0,2},{2,0},{1,3},{3,1},{4,6},{6,4},{5,7},{7,5},{8,10},{10,8},{9,1... | collective-permute-start | bytes 589832 | tf_op jit(solution)/shard_map/ppermute | solution.py:317

commit v2 on v1

v2 whole, which is shorter than its diff:
```python
import functools
import math

import jax
import jax.numpy as jnp
from jax import lax
from jax.experimental import pallas as pl
from jax.experimental.pallas import tpu as pltpu
from jax.sharding import PartitionSpec as P

HD = 128
LANES = 128
MIB = 1 << 20

neg_big = -1e30
adapter_scale = 2.0
score_scale = 1.0 / math.sqrt(HD)
log2_e = 1.4426950408889634


vmem_spec = pl.BlockSpec(memory_space=pltpu.VMEM)
light = pl.CostEstimate(flops=1000, bytes_accessed=1000, transcendentals=0)


def attend_away_body(group, lengths_hbm, q_hbm, k_hbm, v_hbm, o_ref, s_ref, *refs):
    own, fetched, (lengths, sems, sem) = refs[:3], refs[3:6], refs[6:]
    core = lax.axis_index("kv")
    steps, rows = own[0].shape[:2]

    def copies(half, dst, first, i):
        at = pl.ds(i * rows, rows)
        for n, (hbm, ref) in enumerate(zip((q_hbm, k_hbm, v_hbm), dst)):
            width = ref.shape[-1]
            columns = pl.ds(pl.multiple_of(half * width, width), width)
            src = hbm.at[at, columns] if n == 0 else hbm.at[at, :, columns]
            yield pltpu.make_async_copy(src, ref.at[i], sems.at[first + n, i])

    number = pltpu.make_async_copy(lengths_hbm, lengths, sem)
    number.start()
    for half, dst, first in ((1 - core, fetched, 0), (core, own, 3)):
        for i in range(steps):
            for copy in copies(half, dst, first, i):
                copy.start()
    number.wait()
    for i in range(steps):
        for copy in copies(1 - core, fetched, 0, i):
            copy.wait()
        attend_block(group, core, i, lengths, *fetched, o_ref, s_ref)
    for i in range(steps):
        for copy in copies(core, own, 3, i):
            copy.wait()


def attend_own_body(group, lengths, q_ref, k_ref, v_ref, o_ref, s_ref):
    for i in range(q_ref.shape[0]):
        attend_block(group, lax.axis_index("kv"), i, lengths, q_ref, k_ref, v_ref, o_ref, s_ref)


def attend_block(group, core, i, lengths, q_ref, k_ref, v_ref, o_ref, s_ref):
    positions = k_ref.shape[2]
    rows, kv_heads = q_ref.shape[1], k_ref.shape[3] // HD
    offset = core * positions
    wide = 8 * positions
    row_id = lax.broadcasted_iota(jnp.int32, (8, wide), 0)
    column = lax.broadcasted_iota(jnp.int32, (8, wide), 1)
    own_row = column // positions == row_id
    position = column % positions + offset
    lane = lax.broadcasted_iota(jnp.int32, (8, LANES), 1)
    ones = jnp.ones((wide, LANES), jnp.bfloat16)
    queries = q_ref[i].astype(jnp.float32)
    outs = {}
    stats = []
    for sub in range(rows // 8):
        limit = jnp.zeros((8, wide), jnp.int32)
        for t in range(8):
            limit = jnp.where(row_id == t, lengths[i * rows + sub * 8 + t], limit)
        valid = own_row & (position < limit)
        stat = jnp.zeros((8, LANES), jnp.float32)
        for g in range(kv_heads):
            q = jnp.concatenate(
                [
                    queries[sub * 8 : sub * 8 + 8, j * HD : (j + 1) * HD]
                    for j in range(g * group, (g + 1) * group)
                ],
                axis=0,
            ).astype(jnp.bfloat16)
            k = k_ref[i, sub * 8 : sub * 8 + 8, :, g * HD : (g + 1) * HD].reshape(wide, HD)
            v = v_ref[i, sub * 8 : sub * 8 + 8, :, g * HD : (g + 1) * HD].reshape(wide, HD)
            scores = lax.dot_general(
                q, k, (((1,), (1,)), ((), ())), preferred_element_type=jnp.float32
            ).reshape(group, 8, wide)
            scores = jnp.where(valid[None], scores, neg_big)
            top = jnp.max(scores, axis=2, keepdims=True)
            weights = jnp.exp2((scores - top) * (score_scale * log2_e))
            weights = weights.astype(jnp.bfloat16).reshape(group * 8, wide)
            both = jnp.dot(
                weights,
                jnp.concatenate([v, ones], axis=1),
                preferred_element_type=jnp.float32,
            )
            total = both[:, HD:]
            out = both[:, :HD] / total
            level = jnp.log2(total) + top.reshape(group * 8, 1) * (score_scale * log2_e)
            for j in range(group):
                outs[sub, g * group + j] = out[j * 8 : j * 8 + 8]
                stat = jnp.where(lane == g * group + j, level[j * 8 : j * 8 + 8], stat)
        stats.append(stat)
    at = slice(i * rows, (i + 1) * rows)
    for j in range(kv_heads * group):
        o_ref[at, j * HD : (j + 1) * HD] = jnp.concatenate(
            [outs[sub, j] for sub in range(rows // 8)], axis=0
        ).astype(o_ref.dtype)
    s_ref[at, :] = jnp.concatenate(stats, axis=0)


def attend_away(queries, keys, values, lengths):
    rows, features = queries.shape[0], queries.shape[1] // 2
    positions, kv_features = keys.shape[1], keys.shape[2] // 2
    block = 16
    steps = rows // block
    hbm = pl.BlockSpec(memory_space=pltpu.HBM)
    pieces = [
        (steps, block, features),
        (steps, block, positions, kv_features),
        (steps, block, positions, kv_features),
    ]
    return pl.pallas_call(
        functools.partial(attend_away_body, features // kv_features),
        in_specs=[hbm] * 4,
        out_specs=[vmem_spec] * 5,
        out_shape=[
            jax.ShapeDtypeStruct((rows, features), jnp.float32),
            jax.ShapeDtypeStruct((rows, LANES), jnp.float32),
        ]
        + [jax.ShapeDtypeStruct(shape, jnp.bfloat16) for shape in pieces],
        scratch_shapes=[pltpu.VMEM(shape, jnp.bfloat16) for shape in pieces]
        + [
            pltpu.SMEM((rows,), jnp.int32),
            pltpu.SemaphoreType.DMA((6, steps)),
            pltpu.SemaphoreType.DMA,
        ],
        compiler_params=pltpu.CompilerParams(vmem_limit_bytes=16 * MIB),
        cost_estimate=light,
        name="attend_away",
    )(
        *(
            pltpu.with_memory_space_constraint(a, pltpu.HBM)
            for a in (lengths, queries, keys, values)
        )
    )


def attend_own(queries, keys, values, lengths):
    steps, block, features = queries.shape
    group = features // keys.shape[3]
    return pl.pallas_call(
        functools.partial(attend_own_body, group),
        in_specs=[pl.BlockSpec(memory_space=pltpu.SMEM)] + [vmem_spec] * 3,
        out_specs=[vmem_spec] * 2,
        out_shape=[
            jax.ShapeDtypeStruct((steps * block, features), jnp.float32),
            jax.ShapeDtypeStruct((steps * block, LANES), jnp.float32),
        ],
        compiler_params=pltpu.CompilerParams(vmem_limit_bytes=12 * MIB),
        cost_estimate=light,
        name="attend_own",
    )(lengths, queries, keys, values)


def places(ids, target, owned_count):
    rows = ids.shape[0]
    member = ids - target * owned_count
    owned = (member >= 0) & (member < owned_count)
    mark = jnp.where(owned, 1.0, 0.0)
    earlier = lax.broadcasted_iota(jnp.int32, (rows, rows), 1) < lax.broadcasted_iota(
        jnp.int32, (rows, rows), 0
    )
    before = jnp.dot(
        jnp.where(earlier, 1.0, 0.0).astype(jnp.bfloat16),
        mark.astype(jnp.bfloat16),
        preferred_element_type=jnp.float32,
    )
    count = jnp.sum(mark, axis=0, keepdims=True)
    row = lax.broadcasted_iota(jnp.int32, ids.shape, 0).astype(jnp.float32)
    return jnp.where(owned, before, count + row - before)


def merge_body(owned_count, own_ref, own_level, other_ref, other_level, ids_ref, out_ref, *fronts):
    rows = own_ref.shape[0]
    share = 1.0 / (1.0 + jnp.exp2(own_level[...] - other_level[...]))
    for j in range(own_ref.shape[1] // HD):
        at = slice(j * HD, (j + 1) * HD)
        own = own_ref[:, at]
        other = other_ref[:, at].astype(jnp.float32)
        out_ref[:, at] = (own + (other - own) * share[:, j : j + 1]).astype(out_ref.dtype)
    for j, ref in enumerate(fronts):
        route_to(j + 1, owned_count, ids_ref, out_ref, ref, 0)


def route_to(shift, owned_count, ids_ref, rows_ref, out_ref, first):
    rows, slots = rows_ref.shape[0], out_ref.shape[0]
    me = lax.axis_index("adapter")
    ids = ids_ref[pl.ds(pl.multiple_of(me * rows, 16), rows), :]
    place = places(ids, lax.bitwise_xor(me, shift), owned_count).T
    slot = lax.broadcasted_iota(jnp.int32, (slots, rows), 0) + first
    take = jnp.where(place[:slots, :] == slot.astype(jnp.float32), 1.0, 0.0)
    out_ref[...] = jnp.dot(
        take.astype(jnp.bfloat16), rows_ref[...], preferred_element_type=jnp.float32
    ).astype(out_ref.dtype)


def merge(own, own_level, other, other_level, ids, owned_count, partners, capacity):
    shapes = [own.shape] + [(capacity, own.shape[1])] * partners
    return pl.pallas_call(
        functools.partial(merge_body, owned_count),
        in_specs=[vmem_spec] * 5,
        out_specs=[vmem_spec] * len(shapes),
        out_shape=[jax.ShapeDtypeStruct(s, jnp.bfloat16) for s in shapes],
        compiler_params=pltpu.CompilerParams(vmem_limit_bytes=10 * MIB),
        cost_estimate=light,
        name="merge",
    )(own, own_level, other, other_level, ids)


def route_rest_body(first, owned_count, ids_ref, rows_ref, _, *outs):
    for j, ref in enumerate(outs):
        route_to(j + 1, owned_count, ids_ref, rows_ref, ref, first)


def route_rest(ids, rows, after, first, owned_count, partners):
    shape = (rows.shape[0] - first, rows.shape[1])
    return pl.pallas_call(
        functools.partial(route_rest_body, first, owned_count),
        in_specs=[vmem_spec] * 2 + [pl.BlockSpec(memory_space=pl.ANY)],
        out_specs=[vmem_spec] * partners,
        out_shape=[jax.ShapeDtypeStruct(shape, jnp.bfloat16)] * partners,
        compiler_params=pltpu.CompilerParams(vmem_limit_bytes=6 * MIB),
        cost_estimate=light,
        name="route_rest",
    )(ids, rows, after)


def put_back(ids, source, part, first, owned_count):
    rows, slots = ids.shape[0], part.shape[0]
    me = lax.axis_index("adapter")
    place = places(ids, me, owned_count)
    slot = lax.broadcasted_iota(jnp.int32, (rows, slots), 1) + first
    put = jnp.where(place[:, :slots] == slot.astype(jnp.float32), 1.0, 0.0)
    return jnp.dot(put.astype(jnp.bfloat16), part, preferred_element_type=jnp.float32)


def restore_body(count, owned_count, ids_ref, *refs):
    fronts, backs, out_ref = refs[:count], refs[count : 2 * count], refs[-1]
    rows = out_ref.shape[0] // count
    for j in range(count):
        source = lax.bitwise_xor(lax.axis_index("adapter"), j + 1)
        ids = ids_ref[pl.ds(pl.multiple_of(source * rows, 16), rows), :]
        front = put_back(ids, source, fronts[j][...], 0, owned_count)
        back = put_back(ids, source, backs[j][...], fronts[j].shape[0], owned_count)
        out_ref[j * rows : (j + 1) * rows, :] = (front + back).astype(out_ref.dtype)


def restore(ids, fronts, backs, after, owned_count):
    count = len(fronts)
    rows, features = fronts[0].shape[0] + backs[0].shape[0], fronts[0].shape[1]
    return pl.pallas_call(
        functools.partial(restore_body, count, owned_count),
        in_specs=[vmem_spec] * (1 + 2 * count) + [pl.BlockSpec(memory_space=pl.ANY)],
        out_specs=vmem_spec,
        out_shape=jax.ShapeDtypeStruct((count * rows, features), jnp.bfloat16),
        compiler_params=pltpu.CompilerParams(vmem_limit_bytes=8 * MIB),
        cost_estimate=light,
        name="restore",
    )(ids, *fronts, *backs, after)


def down_body(count, rank, ids_ref, d_ref, *refs):
    xs, (out_ref, picked_ref) = refs[:count], refs[-2:]
    me = lax.axis_index("adapter")
    rows = xs[0].shape[0]
    width = d_ref.shape[0]
    parts = [xs[0][...]]
    for j in range(1, count):
        source = lax.bitwise_xor(me, j)
        ids = ids_ref[pl.ds(pl.multiple_of(source * rows, 16), rows), :]
        parts.append(put_back(ids, source, xs[j][...], 0, width // rank).astype(jnp.bfloat16))
    x = jnp.concatenate(parts, axis=0) if count > 1 else parts[0]
    product = lax.dot_general(
        x, d_ref[...], (((1,), (1,)), ((), ())), preferred_element_type=jnp.float32
    )
    lane = lax.broadcasted_iota(jnp.int32, (rows, LANES), 1)
    per_tile = LANES // rank
    for j in range(count):
        source = lax.bitwise_xor(me, j) if count > 1 else 0
        at = pl.ds(pl.multiple_of(source * rows, 16), rows)
        member = ids_ref[at, :] - me * (width // rank)
        picked = jnp.zeros((rows, LANES), jnp.float32)
        for t in range(width // LANES):
            part = product[j * rows : (j + 1) * rows, t * LANES : (t + 1) * LANES]
            picked += jnp.where(member == t * per_tile + lane // rank, part, 0.0)
        picked_ref[at, :] = picked + pltpu.roll(picked, rank, 1)
    packed = out_ref.shape[0]
    left = lax.broadcasted_iota(jnp.int32, (packed, LANES), 1) < rank
    out_ref[...] = jnp.where(left, picked_ref[:packed, :], picked_ref[packed:, :])


def down(ids, weight, blocks, after=()):
    count, rows = len(blocks), len(blocks) * blocks[0].shape[0]
    rank = weight.shape[2]
    flat = jnp.transpose(weight, (0, 2, 1)).reshape(-1, weight.shape[1])
    return pl.pallas_call(
        functools.partial(down_body, count, rank),
        in_specs=[vmem_spec] * (2 + count) + [pl.BlockSpec(memory_space=pl.ANY)] * len(after),
        out_specs=vmem_spec,
        out_shape=jax.ShapeDtypeStruct((rows // 2, LANES), jnp.float32),
        scratch_shapes=[pltpu.VMEM((rows, LANES), jnp.float32)],
        compiler_params=pltpu.CompilerParams(vmem_limit_bytes=16 * MIB),
        cost_estimate=light,
        name="down",
    )(ids, flat, *blocks, *after)


def up_body(count, rank, which, with_residual, ids_ref, base_ref, up_ref, *refs):
    mids, out_ref = refs[:count], refs[-1]
    side = lax.axis_index("mp")
    packed = mids[0][...]
    for r in mids[1:]:
        packed += r[...]
    packed = packed.astype(jnp.bfloat16).astype(jnp.float32)
    turned = pltpu.roll(packed, rank, 1)
    rows = out_ref.shape[0]
    left = lax.broadcasted_iota(jnp.int32, packed.shape, 1) < rank
    if which == "all":
        at = pl.ds(0, rows)
        total = jnp.concatenate(
            [jnp.where(left, packed, turned), jnp.where(left, turned, packed)], axis=0
        )
    else:
        part = side if which == "mine" else 1 - side
        at = pl.ds(pl.multiple_of(part * rows, 16), rows)
        total = jnp.where(left == (part == 0), packed, turned)
    lane = lax.broadcasted_iota(jnp.int32, (rows, LANES), 1)
    per_tile = LANES // rank
    local = ids_ref[at, :] - side * (up_ref.shape[0] // rank)
    spread = jnp.concatenate(
        [
            jnp.where(local == t * per_tile + lane // rank, total, 0.0)
            for t in range(up_ref.shape[0] // LANES)
        ],
        axis=1,
    ).astype(jnp.bfloat16)
    delta = jnp.dot(spread, up_ref[...], preferred_element_type=jnp.float32)
    out = base_ref[at, :] + adapter_scale * delta
    if with_residual:
        out += refs[count][...].astype(jnp.float32)
    out_ref[...] = out.astype(out_ref.dtype)


def up(ids, base, weight, mids, which, rows, residual, out_type):
    rank = weight.shape[1]
    flat = weight.reshape(-1, weight.shape[2])
    extra = [] if residual is None else [residual]
    return pl.pallas_call(
        functools.partial(up_body, len(mids), rank, which, residual is not None),
        in_specs=[vmem_spec] * (3 + len(mids) + len(extra)),
        out_specs=vmem_spec,
        out_shape=jax.ShapeDtypeStruct((rows, base.shape[1]), out_type),
        compiler_params=pltpu.CompilerParams(
            vmem_limit_bytes=(24 if which == "all" else 10) * MIB
        ),
        cost_estimate=light,
        name="up",
    )(ids, base, flat, *mids, *extra)


def last_body(kept_ref, back_ref, out_ref):
    out_ref[...] = (kept_ref[...] + back_ref[...].astype(jnp.float32)).astype(out_ref.dtype)


def last(kept, back):
    return pl.pallas_call(
        last_body,
        in_specs=[vmem_spec] * 2,
        out_specs=vmem_spec,
        out_shape=jax.ShapeDtypeStruct(kept.shape, jnp.bfloat16),
        compiler_params=pltpu.CompilerParams(vmem_limit_bytes=4 * MIB),
        name="last",
    )(kept, back)


def base_body(count, unit, tile, w_ref, *refs):
    xs, ys, out_ref = refs[:count], refs[count : 2 * count], refs[-1]
    me, half = lax.axis_index("adapter"), lax.axis_index("kv")
    depth = xs[0].shape[1]
    x = jnp.concatenate([r[...] for r in xs], axis=0) if count > 1 else xs[0][...]
    y = jnp.concatenate([r[...] for r in ys], axis=0) if count > 1 else ys[0][...]
    own = pl.ds(pl.multiple_of(half * depth, depth), depth)
    other = pl.ds(pl.multiple_of((1 - half) * depth, depth), depth)
    for t in range(out_ref.shape[1] // tile):
        at = slice(t * tile, (t + 1) * tile)
        out = jnp.dot(x, w_ref[own, at], preferred_element_type=jnp.float32)
        out += jnp.dot(y, w_ref[other, at], preferred_element_type=jnp.float32)
        for j in range(out.shape[0] // unit):
            source = lax.bitwise_xor(me, j) if count > 1 else 0
            block = pl.ds(pl.multiple_of(source * unit, 16), unit)
            out_ref[block, at] = out[j * unit : (j + 1) * unit]


def base_projection(weight, own, other):
    count = len(own)
    rows = sum(b.shape[0] for b in own)
    columns = weight.shape[1]
    unit = own[0].shape[0]
    return pl.pallas_call(
        functools.partial(base_body, count, unit, min(256, columns)),
        in_specs=[vmem_spec] * (1 + 2 * count),
        out_specs=vmem_spec,
        out_shape=jax.ShapeDtypeStruct((rows, columns), jnp.float32),
        compiler_params=pltpu.CompilerParams(vmem_limit_bytes=24 * MIB),
        cost_estimate=light,
        name="base",
    )(weight, *own, *other)


def swapped(x, axis, other=1):
    return lax.ppermute(x, axis, [(i, i ^ other) for i in range(lax.axis_size(axis))])


def local(
    queries,
    keys,
    values,
    lengths,
    row_adapter_index,
    residual,
    output_weight,
    adapter_down_weight,
    adapter_up_weight,
):
    owners, splits = lax.axis_size("adapter"), lax.axis_size("mp")
    entire_rows = row_adapter_index.shape[0]
    kept_rows = entire_rows // splits
    direct = owners == 4 and splits == 2
    owned_count = adapter_down_weight.shape[0]
    capacity = 2 * queries.shape[0] // owners
    ids = jnp.broadcast_to(row_adapter_index[:, None], (entire_rows, LANES))

    sent, sent_level, *own_operands = attend_away(queries, keys, values, lengths)
    got, got_level = swapped(sent, "kv"), swapped(sent_level, "kv")
    own, own_level = attend_own(*own_operands, lengths)
    partners = range(1, owners) if direct else ()
    attended, *fronts = merge(
        own, own_level, got, got_level, ids, owned_count, len(partners), capacity
    )

    if direct:
        fronts = [swapped(f, "adapter", j) for j, f in zip(partners, fronts)]
        backs = route_rest(ids, attended, fronts[0], capacity, owned_count, len(partners))
        part = down(ids, adapter_down_weight, [attended] + fronts, backs[:1])
        backs = [swapped(b, "adapter", j) for j, b in zip(partners, backs)]
        far = swapped(part, "mp")
        part = part + far
        part = part + swapped(part, "kv")
        blocks = [attended, restore(ids, fronts, backs, far, owned_count)]
    else:
        blocks = [lax.all_gather(attended, "adapter", axis=0, tiled=True)]
        part = down(ids, adapter_down_weight, blocks)
    others = [swapped(b, "kv") for b in blocks]
    base = base_projection(output_weight, blocks, others)

    if direct:
        mids = [part] + [swapped(part, "adapter", j) for j in range(1, owners)]
        away = up(
            ids, base, adapter_up_weight, mids, "theirs", kept_rows, None, jnp.bfloat16
        )
        back = swapped(away, "mp")
        kept = up(
            ids, base, adapter_up_weight, mids, "mine", kept_rows, residual, jnp.float32
        )
        return last(kept, back)
    mids = [lax.psum(part, ("adapter", "mp", "kv"))]
    terms = up(ids, base, adapter_up_weight, mids, "all", entire_rows, None, jnp.float32)
    summed = lax.psum_scatter(terms, "mp", scatter_dimension=0, tiled=True)
    return (residual.astype(jnp.float32) + summed).astype(jnp.bfloat16)


def solution(mesh):
    placed = (
        P(("groups", "adapter"), "mp"),
        P(("groups", "adapter"), "kv", "mp"),
        P(("groups", "adapter"), "kv", "mp"),
        P(("groups", "adapter")),
        P("groups"),
        P(("groups", "mp"), ("adapter", "kv")),
        P("mp", ("adapter", "kv")),
        P("adapter", ("mp", "kv"), None),
        P("mp", None, ("adapter", "kv")),
    )
    return jax.shard_map(
        local,
        mesh=mesh,
        in_specs=placed,
        out_specs=P(("groups", "mp"), ("adapter", "kv")),
        check_vma=False,
    )
```

time: 54.6 us -> 51.2 us (0.938)
  waiting for transfers between devices: 22.9 us -> 15.3 us
  starting transfers between devices: 15.8 us -> 22.2 us
  Pallas kernels: 14.8 us -> 13.2 us
  local copies, waits for them, and re-layouts: 0.76 us -> 0.11 us
    ppermute x15 -> x16, waiting for transfers between devices: 22.9 us -> 15.3 us  [swapped(): lax.ppermute(x, axis, [(i, i ^ other) for i in range(lax.axis_size(axis))])]
    ppermute x15 -> x16, starting transfers between devices: 15.8 us -> 22.2 us  [swapped(): lax.ppermute(x, axis, [(i, i ^ other) for i in range(lax.axis_size(axis))])]
    pallas_call x4 -> x6, Pallas kernels: 12.1 us -> 9.97 us  [the longest x1 3.63 us: attend_away(): pl.pallas_call(functools.partial(attend_away_body, features // kv_feature...]
    unnamed x14, local copies, waits for them, and re-layouts: 0.68 us -> 0.03 us
  transfers between devices with their start and end apart: 15 -> 16, of which waited for: 6 -> 8; matrix products, arithmetic and copies ran while one was open for 0% -> 0% of each run, Pallas kernels for 17% -> 13%
where the time goes in v2:
time: 51.2 us; the launch traced here: 51 us
  starting transfers between devices  22.2 us (43%)
  waiting for transfers between devices  15.3 us (30%)
  Pallas kernels  13.2 us (26%)
    ppermute x16, starting transfers between devices, swapped(): lax.ppermute(x, axis, [(i, i ^ other) for i in range(lax.axis_size(axis))])  22.2 us
    ppermute x16, waiting for transfers between devices, swapped(): lax.ppermute(x, axis, [(i, i ^ other) for i in range(lax.axis_size(axis))])  15.3 us
    pallas_call x1, Pallas kernels, attend_away(): pl.pallas_call(functools.partial(attend_away_body, features // kv_feature...  3.63 us
    pallas_call x1, Pallas kernels, attend_own(): pl.pallas_call(functools.partial(attend_own_body, group), in_specs=[pl.Bl...  1.99 us
    pallas_call x1, Pallas kernels, base_projection(): pl.pallas_call(functools.partial(base_body, count, unit, min(256, columns...  1.82 us
    pallas_call x1, Pallas kernels, down(): pl.pallas_call(functools.partial(down_body, count, rank), in_specs=[vmem_...  1.47 us
    pallas_call x2, Pallas kernels, up(): pl.pallas_call(functools.partial(up_body, len(mids), rank, which, residua...  1.05 us
  transfers between devices with their start and end apart: 16, of which 8 were waited for; matrix products, arithmetic and copies ran while one was open for 0% of the time, Pallas kernels for 13%

profile of v2, /device:TPU:0, one launch (start us, length us, event | category | flops | bytes accessed | tf_op | source)
XLA Modules:
  0.0 51.0 jit_solution(4261442622584516054)
XLA Ops:
  0.0 3.6 %attend_away.1 = (f32[48,2048]{1,0:T(8,128)S(1)}, f32[48,128]{1,0:T(8,128)S(1)}, bf16[3,16,2048]{2,1,0:T(8,128)(2,1)S(1)}, bf16[3,16,64,256]{3,2,1,0:T(8,128)(2,1)S(1)}, bf16[3,16,64,256]{3,2,1,0:T(8,128)(2,1)S(1)}) custom-call(s32[48]{0:T(128)} %lengths.1, bf16[48,4096]{1,0:T(8,128)(2,1)} %q_hbm.1, bf16[48,64,512]{2,1,0:T(8,128)(2,1)} %k_hbm.1, ...), custom_call_target="tpu_custom_call" | custom-call | flops 1000 | bytes 1000 | tf_op jit(solution)/shard_map/attend_away/pallas_call | solution.py:127
  4.3 2.0 %attend_own.1 = (f32[48,2048]{1,0:T(8,128)S(1)}, f32[48,128]{1,0:T(8,128)S(1)}) custom-call(s32[48]{0:T(128)S(1)} %copy-done.3, bf16[3,16,2048]{2,1,0:T(8,128)(2,1)S(1)} %get-tuple-element.19.q_ref, bf16[3,16,64,256]{3,2,1,0:T(8,128)(2,1)S(1)} %get-tuple-element.20.k_ref, bf16[3,16,64,256]{3,2,1,0:T(8,128)(2,1)S(1)} %get-tuple-element.21.v_ref), custom_call_target="tpu_custom_call" | custom-call | flops 1000 | bytes 1000 | tf_op jit(solution)/shard_map/attend_own/pallas_call | solution.py:156
  6.4 0.9 %merge.1 = (bf16[48,2048]{1,0:T(8,128)(2,1)S(1)}, bf16[24,2048]{1,0:T(8,128)(2,1)S(1)}, bf16[24,2048]{1,0:T(8,128)(2,1)S(1)}, bf16[24,2048]{1,0:T(8,128)(2,1)S(1)}) custom-call(f32[48,2048]{1,0:T(8,128)S(1)} %get-tuple-element.22.own_ref, f32[48,128]{1,0:T(8,128)S(1)} %get-tuple-element.23.own_level, f32[48,2048]{1,0:T(8,128)S(1)} %collective-permute-done.other_ref, ...), custom_call_target="tpu_custom_call" | custom-call | flops 1000 | bytes 1000 | tf_op jit(solution)/shard_map/merge/pallas_call | solution.py:214
  7.2 3.1 %collective-permute-start.2 = (bf16[24,2048]{1,0:T(8,128)(2,1)S(1)}, bf16[24,2048]{1,0:T(8,128)(2,1)S(1)}, u32[]{:S(2)}, u32[]{:S(2)}) collective-permute-start(bf16[24,2048]{1,0:T(8,128)(2,1)S(1)} %get-tuple-element.27), channel_id=1, source_target_pairs={{0,4},{4,0},{8,12},{12,8},{1,5},{5,1},{9,13},{13,9},{2,6},{6,2},{1... | collective-permute-start | bytes 294920 | tf_op jit(solution)/shard_map/ppermute | solution.py:426
  10.3 2.6 %collective-permute-start.3 = (bf16[24,2048]{1,0:T(8,128)(2,1)S(1)}, bf16[24,2048]{1,0:T(8,128)(2,1)S(1)}, u32[]{:S(2)}, u32[]{:S(2)}) collective-permute-start(bf16[24,2048]{1,0:T(8,128)(2,1)S(1)} %get-tuple-element.28), channel_id=1, source_target_pairs={{0,8},{4,12},{8,0},{12,4},{1,9},{5,13},{9,1},{13,5},{2,10},{6,14},... | collective-permute-start | bytes 294920 | tf_op jit(solution)/shard_map/ppermute | solution.py:426
  13.4 0.8 %route_rest.1 = (bf16[24,2048]{1,0:T(8,128)(2,1)S(1)}, bf16[24,2048]{1,0:T(8,128)(2,1)S(1)}, bf16[24,2048]{1,0:T(8,128)(2,1)S(1)}) custom-call(s32[192,128]{1,0:T(8,128)S(1)} %broadcast_in_dim.2.ids_ref, bf16[48,2048]{1,0:T(8,128)(2,1)S(1)} %get-tuple-element.26.rows_ref.refs_0_, bf16[24,2048]{1,0:T(8,128)(2,1)S(1)} %collective-permute-done.2._.refs_1_.refs_0_), custom_call_target="tpu_custom_call" | custom-call | flops 1000 | bytes 1000 | tf_op jit(solution)/shard_map/route_rest/pallas_call | solution.py:232
  14.2 1.8 %collective-permute-start.5 = (bf16[24,2048]{1,0:T(8,128)(2,1)S(1)}, bf16[24,2048]{1,0:T(8,128)(2,1)S(1)}, u32[]{:S(2)}, u32[]{:S(2)}) collective-permute-start(bf16[24,2048]{1,0:T(8,128)(2,1)S(1)} %get-tuple-element.30.refs_4_), channel_id=1, source_target_pairs={{0,4},{4,0},{8,12},{12,8},{1,5},{5,1},{9,13},{13,9},{2,6},{6,2},{1... | collective-permute-start | bytes 294920 | tf_op jit(solution)/shard_map/ppermute | solution.py:426
  16.0 3.6 %collective-permute-start.6 = (bf16[24,2048]{1,0:T(8,128)(2,1)S(1)}, bf16[24,2048]{1,0:T(8,128)(2,1)S(1)}, u32[]{:S(2)}, u32[]{:S(2)}) collective-permute-start(bf16[24,2048]{1,0:T(8,128)(2,1)S(1)} %get-tuple-element.31), channel_id=1, source_target_pairs={{0,8},{4,12},{8,0},{12,4},{1,9},{5,13},{9,1},{13,5},{2,10},{6,14},... | collective-permute-start | bytes 294920 | tf_op jit(solution)/shard_map/ppermute | solution.py:426
  19.6 1.5 %collective-permute-done.3.refs_2_.refs_1_ = bf16[24,2048]{1,0:T(8,128)(2,1)S(1)} collective-permute-done((bf16[24,2048]{1,0:T(8,128)(2,1)S(1)}, bf16[24,2048]{1,0:T(8,128)(2,1)S(1)}, u32[]{:S(2)}, u32[]{:S(2)}) %collective-permute-start.3) | collective-permute-done | bytes 98336 | tf_op jit(solution)/shard_map/ppermute | solution.py:426
  21.2 1.5 %down.1 = f32[96,128]{1,0:T(8,128)S(1)} custom-call(s32[192,128]{1,0:T(8,128)S(1)} %broadcast_in_dim.2.ids_ref, bf16[512,2048]{1,0:T(8,128)(2,1)S(1)} %bitcast.8, bf16[48,2048]{1,0:T(8,128)(2,1)S(1)} %get-tuple-element.26.rows_ref.refs_0_, bf16[24,2048]{1,0:T(8,128)(2,1)S(1)} %collective-permute-done.2._.refs_1_.refs_0_, ...), custom_call_target="tpu_custom_call" | custom-call | flops 1000 | bytes 1000 | tf_op jit(solution)/shard_map/down/pallas_call | solution.py:311
  22.7 1.6 %collective-permute-start.8 = (f32[96,128]{1,0:T(8,128)S(1)}, f32[96,128]{1,0:T(8,128)S(1)}, u32[]{:S(2)}, u32[]{:S(2)}) collective-permute-start(f32[96,128]{1,0:T(8,128)S(1)} %down.1), channel_id=1, source_target_pairs={{0,2},{2,0},{1,3},{3,1},{4,6},{6,4},{5,7},{7,5},{8,10},{10,8},{9,1... | collective-permute-start | bytes 147464 | tf_op jit(solution)/shard_map/ppermute | solution.py:426
  24.2 2.6 %collective-permute-done.8.refs_6_ = f32[96,128]{1,0:T(8,128)S(1)} collective-permute-done((f32[96,128]{1,0:T(8,128)S(1)}, f32[96,128]{1,0:T(8,128)S(1)}, u32[]{:S(2)}, u32[]{:S(2)}) %collective-permute-start.8) | collective-permute-done | bytes 49184 | tf_op jit(solution)/shard_map/ppermute | solution.py:426
  26.8 2.6 %collective-permute-done.6.refs_4_ = bf16[24,2048]{1,0:T(8,128)(2,1)S(1)} collective-permute-done((bf16[24,2048]{1,0:T(8,128)(2,1)S(1)}, bf16[24,2048]{1,0:T(8,128)(2,1)S(1)}, u32[]{:S(2)}, u32[]{:S(2)}) %collective-permute-start.6) | collective-permute-done | bytes 98336 | tf_op jit(solution)/shard_map/ppermute | solution.py:426
  29.4 0.8 %restore.1.refs_1_ = bf16[144,2048]{1,0:T(8,128)(2,1)S(1)} custom-call(s32[192,128]{1,0:T(8,128)S(1)} %broadcast_in_dim.2.ids_ref, bf16[24,2048]{1,0:T(8,128)(2,1)S(1)} %collective-permute-done.2._.refs_1_.refs_0_, bf16[24,2048]{1,0:T(8,128)(2,1)S(1)} %collective-permute-done.3.refs_2_.refs_1_, bf16[24,2048]{1,0:T(8,128)(2,1)S(1)} %collective-permute-done.4.refs_3_.refs_2_, ...), custom_call_target="tpu_custom_call" | custom-call | flops 1000 | bytes 1000 | tf_op jit(solution)/shard_map/restore/pallas_call | solution.py:266
  31.0 1.7 %collective-permute-done.11 = f32[96,128]{1,0:T(8,128)S(1)} collective-permute-done((f32[96,128]{1,0:T(8,128)S(1)}, f32[96,128]{1,0:T(8,128)S(1)}, u32[]{:S(2)}, u32[]{:S(2)}) %collective-permute-start.11) | collective-permute-done | bytes 49184 | tf_op jit(solution)/shard_map/ppermute | solution.py:426
  32.7 4.2 %collective-permute-start.12 = (f32[96,128]{1,0:T(8,128)S(1)}, f32[96,128]{1,0:T(8,128)S(1)}, u32[]{:S(2)}, u32[]{:S(2)}) collective-permute-start(f32[96,128]{1,0:T(8,128)S(1)} %add.7.refs_0_), channel_id=1, source_target_pairs={{0,4},{4,0},{8,12},{12,8},{1,5},{5,1},{9,13},{13,9},{2,6},{6,2},{1... | collective-permute-start | bytes 147464 | tf_op jit(solution)/shard_map/ppermute | solution.py:426
  36.9 1.2 %collective-permute-start.13 = (f32[96,128]{1,0:T(8,128)S(1)}, f32[96,128]{1,0:T(8,128)S(1)}, u32[]{:S(2)}, u32[]{:S(2)}) collective-permute-start(f32[96,128]{1,0:T(8,128)S(1)} %add.7.refs_0_), channel_id=1, source_target_pairs={{0,8},{4,12},{8,0},{12,4},{1,9},{5,13},{9,1},{13,5},{2,10},{6,14},... | collective-permute-start | bytes 147464 | tf_op jit(solution)/shard_map/ppermute | solution.py:426
  38.1 1.4 %collective-permute-start.14 = (f32[96,128]{1,0:T(8,128)S(1)}, f32[96,128]{1,0:T(8,128)S(1)}, u32[]{:S(2)}, u32[]{:S(2)}) collective-permute-start(f32[96,128]{1,0:T(8,128)S(1)} %add.7.refs_0_), channel_id=1, source_target_pairs={{0,12},{4,8},{8,4},{12,0},{1,13},{5,9},{9,5},{13,1},{2,14},{6,10},... | collective-permute-start | bytes 147464 | tf_op jit(solution)/shard_map/ppermute | solution.py:426
  39.5 1.8 %base.1.base_ref = f32[192,1024]{1,0:T(8,128)S(1)} custom-call(bf16[4096,1024]{1,0:T(8,128)(2,1)S(1)} %bitcast.7, bf16[48,2048]{1,0:T(8,128)(2,1)S(1)} %get-tuple-element.26.rows_ref.refs_0_, bf16[144,2048]{1,0:T(8,128)(2,1)S(1)} %restore.1.refs_1_, bf16[48,2048]{1,0:T(8,128)(2,1)S(1)} %collective-permute-done.9.refs_2_, ...), custom_call_target="tpu_custom_call" | custom-call | flops 1000 | bytes 1000 | tf_op jit(solution)/shard_map/base/pallas_call | solution.py:414
  41.3 1.9 %collective-permute-done.13.refs_2_ = f32[96,128]{1,0:T(8,128)S(1)} collective-permute-done((f32[96,128]{1,0:T(8,128)S(1)}, f32[96,128]{1,0:T(8,128)S(1)}, u32[]{:S(2)}, u32[]{:S(2)}) %collective-permute-start.13) | collective-permute-done | bytes 49184 | tf_op jit(solution)/shard_map/ppermute | solution.py:426
  43.3 0.8 %collective-permute-done.14.refs_3_ = f32[96,128]{1,0:T(8,128)S(1)} collective-permute-done((f32[96,128]{1,0:T(8,128)S(1)}, f32[96,128]{1,0:T(8,128)S(1)}, u32[]{:S(2)}, u32[]{:S(2)}) %collective-permute-start.14) | collective-permute-done | bytes 49184 | tf_op jit(solution)/shard_map/ppermute | solution.py:426
  44.6 1.6 %collective-permute-start.15 = (bf16[96,1024]{1,0:T(8,128)(2,1)S(1)}, bf16[96,1024]{1,0:T(8,128)(2,1)S(1)}, u32[]{:S(2)}, u32[]{:S(2)}) collective-permute-start(bf16[96,1024]{1,0:T(8,128)(2,1)S(1)} %up.3), channel_id=1, source_target_pairs={{0,2},{2,0},{1,3},{3,1},{4,6},{6,4},{5,7},{7,5},{8,10},{10,8},{9,1... | collective-permute-start | bytes 589832 | tf_op jit(solution)/shard_map/ppermute | solution.py:426
  46.7 3.6 %collective-permute-done.15.back_ref = bf16[96,1024]{1,0:T(8,128)(2,1)S(1)} collective-permute-done((bf16[96,1024]{1,0:T(8,128)(2,1)S(1)}, bf16[96,1024]{1,0:T(8,128)(2,1)S(1)}, u32[]{:S(2)}, u32[]{:S(2)}) %collective-permute-start.15) | collective-permute-done | bytes 196640 | tf_op jit(solution)/shard_map/ppermute | solution.py:426
  50.3 0.7 %last.1 = bf16[96,1024]{1,0:T(8,128)(2,1)} custom-call(f32[96,1024]{1,0:T(8,128)S(1)} %up.2.kept_ref, bf16[96,1024]{1,0:T(8,128)(2,1)S(1)} %collective-permute-done.15.back_ref), custom_call_target="tpu_custom_call" | custom-call | tf_op jit(solution)/shard_map/last/pallas_call | solution.py:381
  (36 shorter events, 2.9 us)
Async XLA Ops:
  0.0 4.3 %copy-start.3 = (s32[48]{0:T(128)S(1)}, s32[48]{0:T(128)}, u32[]{:S(2)}) copy-start(s32[48]{0:T(128)} %lengths.1) | copy-start | bytes 580
  0.0 39.4 %slice-start = ((s8[8388608]{0:T(1024)(128)(4,1)}), s8[4194304]{0:T(1024)(128)(4,1)S(1)}, s32[]{:S(2)}) async-start(s8[8388608]{0:T(1024)(128)(4,1)} %bitcast.6), calls=%async_computation | async-start | bytes 8388608
  3.6 2.6 %copy-start.4 = (s32[192]{0:T(256)S(1)}, s32[192]{0:T(256)}, u32[]{:S(2)}) copy-start(s32[192]{0:T(256)} %param.13) | copy-start | bytes 2308
  3.7 2.6 %collective-permute-start = (f32[48,2048]{1,0:T(8,128)S(1)}, f32[48,2048]{1,0:T(8,128)S(1)}, u32[]{:S(2)}, u32[]{:S(2)}) collective-permute-start(f32[48,2048]{1,0:T(8,128)S(1)} %get-tuple-element.24), channel_id=1, source_target_pairs={{0,1},{1,0},{2,3},{3,2},{4,5},{5,4},{6,7},{7,6},{8,9},{9,8},{10,11... | collective-permute-start | bytes 1179656 | tf_op jit(solution)/shard_map/ppermute | solution.py:426
  4.2 2.1 %collective-permute-start.1 = (f32[48,128]{1,0:T(8,128)S(1)}, f32[48,128]{1,0:T(8,128)S(1)}, u32[]{:S(2)}, u32[]{:S(2)}) collective-permute-start(f32[48,128]{1,0:T(8,128)S(1)} %get-tuple-element.25), channel_id=1, source_target_pairs={{0,1},{1,0},{2,3},{3,2},{4,5},{5,4},{6,7},{7,6},{8,9},{9,8},{10,11... | collective-permute-start | bytes 73736 | tf_op jit(solution)/shard_map/ppermute | solution.py:426
  4.3 16.9 %copy-start.1 = (bf16[8,2048,64]{1,2,0:T(8,128)(2,1)S(1)}, bf16[8,2048,64]{1,2,0:T(8,128)(2,1)}, u32[]{:S(2)}) copy-start(bf16[8,2048,64]{1,2,0:T(8,128)(2,1)} %param.16) | copy-start | bytes 6291460
  4.3 35.2 %slice-start.1 = ((s8[8388608]{0:T(1024)(128)(4,1)}), s8[4194304]{0:T(1024)(128)(4,1)S(1)}, s32[]{:S(2)}) async-start(s8[8388608]{0:T(1024)(128)(4,1)} %bitcast.6), calls=%async_computation.1 | async-start | bytes 8388608
  7.2 6.1 %collective-permute-start.2 = (bf16[24,2048]{1,0:T(8,128)(2,1)S(1)}, bf16[24,2048]{1,0:T(8,128)(2,1)S(1)}, u32[]{:S(2)}, u32[]{:S(2)}) collective-permute-start(bf16[24,2048]{1,0:T(8,128)(2,1)S(1)} %get-tuple-element.27), channel_id=1, source_target_pairs={{0,4},{4,0},{8,12},{12,8},{1,5},{5,1},{9,13},{13,9},{2,6},{6,2},{1... | collective-permute-start | bytes 294920 | tf_op jit(solution)/shard_map/ppermute | solution.py:426
  10.3 10.9 %collective-permute-start.3 = (bf16[24,2048]{1,0:T(8,128)(2,1)S(1)}, bf16[24,2048]{1,0:T(8,128)(2,1)S(1)}, u32[]{:S(2)}, u32[]{:S(2)}) collective-permute-start(bf16[24,2048]{1,0:T(8,128)(2,1)S(1)} %get-tuple-element.28), channel_id=1, source_target_pairs={{0,8},{4,12},{8,0},{12,4},{1,9},{5,13},{9,1},{13,5},{2,10},{6,14},... | collective-permute-start | bytes 294920 | tf_op jit(solution)/shard_map/ppermute | solution.py:426
  12.9 8.3 %collective-permute-start.4 = (bf16[24,2048]{1,0:T(8,128)(2,1)S(1)}, bf16[24,2048]{1,0:T(8,128)(2,1)S(1)}, u32[]{:S(2)}, u32[]{:S(2)}) collective-permute-start(bf16[24,2048]{1,0:T(8,128)(2,1)S(1)} %get-tuple-element.29), channel_id=1, source_target_pairs={{0,12},{4,8},{8,4},{12,0},{1,13},{5,9},{9,5},{13,1},{2,14},{6,10},... | collective-permute-start | bytes 294920 | tf_op jit(solution)/shard_map/ppermute | solution.py:426
  14.2 12.6 %collective-permute-start.5 = (bf16[24,2048]{1,0:T(8,128)(2,1)S(1)}, bf16[24,2048]{1,0:T(8,128)(2,1)S(1)}, u32[]{:S(2)}, u32[]{:S(2)}) collective-permute-start(bf16[24,2048]{1,0:T(8,128)(2,1)S(1)} %get-tuple-element.30.refs_4_), channel_id=1, source_target_pairs={{0,4},{4,0},{8,12},{12,8},{1,5},{5,1},{9,13},{13,9},{2,6},{6,2},{1... | collective-permute-start | bytes 294920 | tf_op jit(solution)/shard_map/ppermute | solution.py:426
  16.0 13.4 %collective-permute-start.6 = (bf16[24,2048]{1,0:T(8,128)(2,1)S(1)}, bf16[24,2048]{1,0:T(8,128)(2,1)S(1)}, u32[]{:S(2)}, u32[]{:S(2)}) collective-permute-start(bf16[24,2048]{1,0:T(8,128)(2,1)S(1)} %get-tuple-element.31), channel_id=1, source_target_pairs={{0,8},{4,12},{8,0},{12,4},{1,9},{5,13},{9,1},{13,5},{2,10},{6,14},... | collective-permute-start | bytes 294920 | tf_op jit(solution)/shard_map/ppermute | solution.py:426
  19.6 9.8 %collective-permute-start.7 = (bf16[24,2048]{1,0:T(8,128)(2,1)S(1)}, bf16[24,2048]{1,0:T(8,128)(2,1)S(1)}, u32[]{:S(2)}, u32[]{:S(2)}) collective-permute-start(bf16[24,2048]{1,0:T(8,128)(2,1)S(1)} %get-tuple-element.32), channel_id=1, source_target_pairs={{0,12},{4,8},{8,4},{12,0},{1,13},{5,9},{9,5},{13,1},{2,14},{6,10},... | collective-permute-start | bytes 294920 | tf_op jit(solution)/shard_map/ppermute | solution.py:426
  22.7 4.2 %collective-permute-start.8 = (f32[96,128]{1,0:T(8,128)S(1)}, f32[96,128]{1,0:T(8,128)S(1)}, u32[]{:S(2)}, u32[]{:S(2)}) collective-permute-start(f32[96,128]{1,0:T(8,128)S(1)} %down.1), channel_id=1, source_target_pairs={{0,2},{2,0},{1,3},{3,1},{4,6},{6,4},{5,7},{7,5},{8,10},{10,8},{9,1... | collective-permute-start | bytes 147464 | tf_op jit(solution)/shard_map/ppermute | solution.py:426
  30.3 9.2 %collective-permute-start.10 = (bf16[144,2048]{1,0:T(8,128)(2,1)S(1)}, bf16[144,2048]{1,0:T(8,128)(2,1)S(1)}, u32[]{:S(2)}, u32[]{:S(2)}) collective-permute-start(bf16[144,2048]{1,0:T(8,128)(2,1)S(1)} %restore.1.refs_1_), channel_id=1, source_target_pairs={{0,1},{1,0},{2,3},{3,2},{4,5},{5,4},{6,7},{7,6},{8,9},{9,8},{10,11... | collective-permute-start | bytes 1769480 | tf_op jit(solution)/shard_map/ppermute | solution.py:426
  30.3 9.1 %collective-permute-start.9 = (bf16[48,2048]{1,0:T(8,128)(2,1)S(1)}, bf16[48,2048]{1,0:T(8,128)(2,1)S(1)}, u32[]{:S(2)}, u32[]{:S(2)}) collective-permute-start(bf16[48,2048]{1,0:T(8,128)(2,1)S(1)} %get-tuple-element.26.rows_ref.refs_0_), channel_id=1, source_target_pairs={{0,1},{1,0},{2,3},{3,2},{4,5},{5,4},{6,7},{7,6},{8,9},{9,8},{10,11... | collective-permute-start | bytes 589832 | tf_op jit(solution)/shard_map/ppermute | solution.py:426
  30.8 1.8 %collective-permute-start.11 = (f32[96,128]{1,0:T(8,128)S(1)}, f32[96,128]{1,0:T(8,128)S(1)}, u32[]{:S(2)}, u32[]{:S(2)}) collective-permute-start(f32[96,128]{1,0:T(8,128)S(1)} %add.6), channel_id=1, source_target_pairs={{0,1},{1,0},{2,3},{3,2},{4,5},{5,4},{6,7},{7,6},{8,9},{9,8},{10,11... | collective-permute-start | bytes 147464 | tf_op jit(solution)/shard_map/ppermute | solution.py:426
  32.7 11.4 %copy-start = (bf16[16,64,1024]{2,1,0:T(8,128)(2,1)S(1)}, bf16[16,64,1024]{2,1,0:T(8,128)(2,1)}, u32[]{:S(2)}) copy-start(bf16[16,64,1024]{2,1,0:T(8,128)(2,1)} %param.17) | copy-start | bytes 6291460
  32.7 8.6 %collective-permute-start.12 = (f32[96,128]{1,0:T(8,128)S(1)}, f32[96,128]{1,0:T(8,128)S(1)}, u32[]{:S(2)}, u32[]{:S(2)}) collective-permute-start(f32[96,128]{1,0:T(8,128)S(1)} %add.7.refs_0_), channel_id=1, source_target_pairs={{0,4},{4,0},{8,12},{12,8},{1,5},{5,1},{9,13},{13,9},{2,6},{6,2},{1... | collective-permute-start | bytes 147464 | tf_op jit(solution)/shard_map/ppermute | solution.py:426
  36.9 6.4 %collective-permute-start.13 = (f32[96,128]{1,0:T(8,128)S(1)}, f32[96,128]{1,0:T(8,128)S(1)}, u32[]{:S(2)}, u32[]{:S(2)}) collective-permute-start(f32[96,128]{1,0:T(8,128)S(1)} %add.7.refs_0_), channel_id=1, source_target_pairs={{0,8},{4,12},{8,0},{12,4},{1,9},{5,13},{9,1},{13,5},{2,10},{6,14},... | collective-permute-start | bytes 147464 | tf_op jit(solution)/shard_map/ppermute | solution.py:426
  38.1 6.0 %collective-permute-start.14 = (f32[96,128]{1,0:T(8,128)S(1)}, f32[96,128]{1,0:T(8,128)S(1)}, u32[]{:S(2)}, u32[]{:S(2)}) collective-permute-start(f32[96,128]{1,0:T(8,128)S(1)} %add.7.refs_0_), channel_id=1, source_target_pairs={{0,12},{4,8},{8,4},{12,0},{1,13},{5,9},{9,5},{13,1},{2,14},{6,10},... | collective-permute-start | bytes 147464 | tf_op jit(solution)/shard_map/ppermute | solution.py:426
  41.3 4.8 %copy-start.2 = (bf16[96,1024]{1,0:T(8,128)(2,1)S(1)}, bf16[96,1024]{1,0:T(8,128)(2,1)}, u32[]{:S(2)}) copy-start(bf16[96,1024]{1,0:T(8,128)(2,1)} %refs_4_.1) | copy-start | bytes 589828
  44.6 5.7 %collective-permute-start.15 = (bf16[96,1024]{1,0:T(8,128)(2,1)S(1)}, bf16[96,1024]{1,0:T(8,128)(2,1)S(1)}, u32[]{:S(2)}, u32[]{:S(2)}) collective-permute-start(bf16[96,1024]{1,0:T(8,128)(2,1)S(1)} %up.3), channel_id=1, source_target_pairs={{0,2},{2,0},{1,3},{3,1},{4,6},{6,4},{5,7},{7,5},{8,10},{10,8},{9,1... | collective-permute-start | bytes 589832 | tf_op jit(solution)/shard_map/ppermute | solution.py:426

commit v3 on v2

--- a/solution.py
+++ b/solution.py
@@ -185,7 +185,7 @@
     return jnp.where(owned, before, count + row - before)
 
 
-def merge_body(owned_count, own_ref, own_level, other_ref, other_level, ids_ref, out_ref, *fronts):
+def merge_body(shifts, owned_count, own_ref, own_level, other_ref, other_level, ids_ref, out_ref, *fronts):
     rows = own_ref.shape[0]
     share = 1.0 / (1.0 + jnp.exp2(own_level[...] - other_level[...]))
     for j in range(own_ref.shape[1] // HD):
@@ -193,8 +193,8 @@
         own = own_ref[:, at]
         other = other_ref[:, at].astype(jnp.float32)
         out_ref[:, at] = (own + (other - own) * share[:, j : j + 1]).astype(out_ref.dtype)
-    for j, ref in enumerate(fronts):
-        route_to(j + 1, owned_count, ids_ref, out_ref, ref, 0)
+    for shift, ref in zip(shifts, fronts):
+        route_to(shift, owned_count, ids_ref, out_ref, ref, 0)
 
 
 def route_to(shift, owned_count, ids_ref, rows_ref, out_ref, first):
@@ -209,10 +209,10 @@
     ).astype(out_ref.dtype)
 
 
-def merge(own, own_level, other, other_level, ids, owned_count, partners, capacity):
-    shapes = [own.shape] + [(capacity, own.shape[1])] * partners
-    return pl.pallas_call(
-        functools.partial(merge_body, owned_count),
+def merge(own, own_level, other, other_level, ids, owned_count, shifts, capacity):
+    shapes = [own.shape] + [(capacity, own.shape[1])] * len(shifts)
+    return pl.pallas_call(
+        functools.partial(merge_body, shifts, owned_count),
         in_specs=[vmem_spec] * 5,
         out_specs=[vmem_spec] * len(shapes),
         out_shape=[jax.ShapeDtypeStruct(s, jnp.bfloat16) for s in shapes],
@@ -222,18 +222,18 @@
     )(own, own_level, other, other_level, ids)
 
 
-def route_rest_body(first, owned_count, ids_ref, rows_ref, _, *outs):
-    for j, ref in enumerate(outs):
-        route_to(j + 1, owned_count, ids_ref, rows_ref, ref, first)
-
-
-def route_rest(ids, rows, after, first, owned_count, partners):
+def route_rest_body(first, shifts, owned_count, ids_ref, rows_ref, _, *outs):
+    for shift, ref in zip(shifts, outs):
+        route_to(shift, owned_count, ids_ref, rows_ref, ref, first)
+
+
+def route_rest(ids, rows, after, first, owned_count, shifts):
     shape = (rows.shape[0] - first, rows.shape[1])
     return pl.pallas_call(
-        functools.partial(route_rest_body, first, owned_count),
+        functools.partial(route_rest_body, first, shifts, owned_count),
         in_specs=[vmem_spec] * 2 + [pl.BlockSpec(memory_space=pl.ANY)],
-        out_specs=[vmem_spec] * partners,
-        out_shape=[jax.ShapeDtypeStruct(shape, jnp.bfloat16)] * partners,
+        out_specs=[vmem_spec] * len(shifts),
+        out_shape=[jax.ShapeDtypeStruct(shape, jnp.bfloat16)] * len(shifts),
         compiler_params=pltpu.CompilerParams(vmem_limit_bytes=6 * MIB),
         cost_estimate=light,
         name="route_rest",
@@ -249,67 +249,98 @@
     return jnp.dot(put.astype(jnp.bfloat16), part, preferred_element_type=jnp.float32)
 
 
-def restore_body(count, owned_count, ids_ref, *refs):
-    fronts, backs, out_ref = refs[:count], refs[count : 2 * count], refs[-1]
-    rows = out_ref.shape[0] // count
-    for j in range(count):
-        source = lax.bitwise_xor(lax.axis_index("adapter"), j + 1)
+def join_body(count, *refs):
+    for j, ref in enumerate(refs[:count]):
+        refs[-1][j] = ref[...]
+
+
+def join(parts, after=()):
+    shape = (len(parts), *parts[0].shape)
+    return pl.pallas_call(
+        functools.partial(join_body, len(parts)),
+        in_specs=[vmem_spec] * len(parts) + [pl.BlockSpec(memory_space=pl.ANY)] * len(after),
+        out_specs=vmem_spec,
+        out_shape=jax.ShapeDtypeStruct(shape, parts[0].dtype),
+        compiler_params=pltpu.CompilerParams(vmem_limit_bytes=4 * MIB),
+        cost_estimate=pl.CostEstimate(flops=1000, bytes_accessed=1000, transcendentals=0),
+        name="join",
+    )(*parts, *after)
+
+
+def restore_body(shifts, owned_count, ids_ref, *refs):
+    count, outs = len(shifts), refs[-2:]
+    rows = outs[0].shape[0] // count
+    slots = refs[0].shape[1]
+    for j, shift in enumerate(shifts):
+        source = lax.bitwise_xor(lax.axis_index("adapter"), shift)
         ids = ids_ref[pl.ds(pl.multiple_of(source * rows, 16), rows), :]
-        front = put_back(ids, source, fronts[j][...], 0, owned_count)
-        back = put_back(ids, source, backs[j][...], fronts[j].shape[0], owned_count)
-        out_ref[j * rows : (j + 1) * rows, :] = (front + back).astype(out_ref.dtype)
-
-
-def restore(ids, fronts, backs, after, owned_count):
-    count = len(fronts)
-    rows, features = fronts[0].shape[0] + backs[0].shape[0], fronts[0].shape[1]
-    return pl.pallas_call(
-        functools.partial(restore_body, count, owned_count),
-        in_specs=[vmem_spec] * (1 + 2 * count) + [pl.BlockSpec(memory_space=pl.ANY)],
-        out_specs=vmem_spec,
-        out_shape=jax.ShapeDtypeStruct((count * rows, features), jnp.bfloat16),
+        for n, out_ref in enumerate(outs):
+            front = put_back(ids, source, refs[2 * n][j], 0, owned_count)
+            back = put_back(ids, source, refs[2 * n + 1][j], slots, owned_count)
+            out_ref[j * rows : (j + 1) * rows, :] = (front + back).astype(out_ref.dtype)
+
+
+def restore(ids, own, other, after, owned_count, shifts):
+    count = len(shifts)
+    rows, features = own[0].shape[1] + own[1].shape[1], own[0].shape[2]
+    return pl.pallas_call(
+        functools.partial(restore_body, shifts, owned_count),
+        in_specs=[vmem_spec] * 5 + [pl.BlockSpec(memory_space=pl.ANY)],
+        out_specs=[vmem_spec] * 2,
+        out_shape=[jax.ShapeDtypeStruct((count * rows, features), jnp.bfloat16)] * 2,
         compiler_params=pltpu.CompilerParams(vmem_limit_bytes=8 * MIB),
         cost_estimate=light,
         name="restore",
-    )(ids, *fronts, *backs, after)
-
-
-def down_body(count, rank, ids_ref, d_ref, *refs):
+    )(ids, *own, *other, after)
+
+
+def down_body(count, plain, rank, owned_count, ids_ref, own_ref, *refs):
     xs, (out_ref, picked_ref) = refs[:count], refs[-2:]
     me = lax.axis_index("adapter")
-    rows = xs[0].shape[0]
-    width = d_ref.shape[0]
-    parts = [xs[0][...]]
-    for j in range(1, count):
-        source = lax.bitwise_xor(me, j)
-        ids = ids_ref[pl.ds(pl.multiple_of(source * rows, 16), rows), :]
-        parts.append(put_back(ids, source, xs[j][...], 0, width // rank).astype(jnp.bfloat16))
-    x = jnp.concatenate(parts, axis=0) if count > 1 else parts[0]
-    product = lax.dot_general(
-        x, d_ref[...], (((1,), (1,)), ((), ())), preferred_element_type=jnp.float32
-    )
-    lane = lax.broadcasted_iota(jnp.int32, (rows, LANES), 1)
+    rows = out_ref.shape[0] * 2 // count
+    width = own_ref.shape[0]
+    transposed = (((1,), (1,)), ((), ()))
+    x = jnp.concatenate([r[...] for r in xs], axis=0) if count > 1 else xs[0][...]
+    product = lax.dot_general(x, own_ref[...], transposed, preferred_element_type=jnp.float32)
     per_tile = LANES // rank
+    first = 0
     for j in range(count):
         source = lax.bitwise_xor(me, j) if count > 1 else 0
         at = pl.ds(pl.multiple_of(source * rows, 16), rows)
-        member = ids_ref[at, :] - me * (width // rank)
-        picked = jnp.zeros((rows, LANES), jnp.float32)
+        ids = ids_ref[at, :]
+        member = ids - me * owned_count
+        slots = xs[j].shape[0]
+        if j >= plain:
+            place = places(ids, me, owned_count)
+            slot = lax.broadcasted_iota(jnp.int32, (slots, rows), 0).astype(jnp.float32)
+            take = jnp.where(place.T[:slots, :] == slot, 1.0, 0.0).astype(jnp.bfloat16)
+            member = jnp.dot(
+                take,
+                member.astype(jnp.float32).astype(jnp.bfloat16),
+                preferred_element_type=jnp.float32,
+            ).astype(jnp.int32)
+        lane = lax.broadcasted_iota(jnp.int32, (slots, LANES), 1)
+        picked = jnp.zeros((slots, LANES), jnp.float32)
         for t in range(width // LANES):
-            part = product[j * rows : (j + 1) * rows, t * LANES : (t + 1) * LANES]
+            part = product[first : first + slots, t * LANES : (t + 1) * LANES]
             picked += jnp.where(member == t * per_tile + lane // rank, part, 0.0)
+        first += slots
+        if j >= plain:
+            slot = lax.broadcasted_iota(jnp.int32, (rows, slots), 1).astype(jnp.float32)
+            put = jnp.where(place[:, :slots] == slot, 1.0, 0.0)
+            picked = jnp.dot(
+                put, picked, precision=lax.Precision.HIGHEST, preferred_element_type=jnp.float32
+            )
         picked_ref[at, :] = picked + pltpu.roll(picked, rank, 1)
     packed = out_ref.shape[0]
     left = lax.broadcasted_iota(jnp.int32, (packed, LANES), 1) < rank
     out_ref[...] = jnp.where(left, picked_ref[:packed, :], picked_ref[packed:, :])
 
 
-def down(ids, weight, blocks, after=()):
-    count, rows = len(blocks), len(blocks) * blocks[0].shape[0]
-    rank = weight.shape[2]
-    flat = jnp.transpose(weight, (0, 2, 1)).reshape(-1, weight.shape[1])
-    return pl.pallas_call(
-        functools.partial(down_body, count, rank),
+def down(ids, weight, owned_count, rank, own, plain, after=()):
+    count, rows = len(own), ids.shape[0]
+    return pl.pallas_call(
+        functools.partial(down_body, count, plain, rank, owned_count),
         in_specs=[vmem_spec] * (2 + count) + [pl.BlockSpec(memory_space=pl.ANY)] * len(after),
         out_specs=vmem_spec,
         out_shape=jax.ShapeDtypeStruct((rows // 2, LANES), jnp.float32),
@@ -317,15 +348,15 @@
         compiler_params=pltpu.CompilerParams(vmem_limit_bytes=16 * MIB),
         cost_estimate=light,
         name="down",
-    )(ids, flat, *blocks, *after)
+    )(ids, weight, *own, *after)
 
 
 def up_body(count, rank, which, with_residual, ids_ref, base_ref, up_ref, *refs):
     mids, out_ref = refs[:count], refs[-1]
     side = lax.axis_index("mp")
-    packed = mids[0][...]
+    packed = mids[0][...].astype(jnp.float32)
     for r in mids[1:]:
-        packed += r[...]
+        packed += r[...].astype(jnp.float32)
     packed = packed.astype(jnp.bfloat16).astype(jnp.float32)
     turned = pltpu.roll(packed, rank, 1)
     rows = out_ref.shape[0]
@@ -448,28 +479,29 @@
     sent, sent_level, *own_operands = attend_away(queries, keys, values, lengths)
     got, got_level = swapped(sent, "kv"), swapped(sent_level, "kv")
     own, own_level = attend_own(*own_operands, lengths)
-    partners = range(1, owners) if direct else ()
+    shifts = tuple(range(2, owners)) if direct else ()
     attended, *fronts = merge(
-        own, own_level, got, got_level, ids, owned_count, len(partners), capacity
+        own, own_level, got, got_level, ids, owned_count, shifts, capacity
     )
 
+    rank = adapter_down_weight.shape[2]
+    down_own = jnp.transpose(adapter_down_weight, (0, 2, 1)).reshape(-1, attended.shape[1])
     if direct:
-        fronts = [swapped(f, "adapter", j) for j, f in zip(partners, fronts)]
-        backs = route_rest(ids, attended, fronts[0], capacity, owned_count, len(partners))
-        part = down(ids, adapter_down_weight, [attended] + fronts, backs[:1])
-        backs = [swapped(b, "adapter", j) for j, b in zip(partners, backs)]
-        far = swapped(part, "mp")
-        part = part + far
-        part = part + swapped(part, "kv")
-        blocks = [attended, restore(ids, fronts, backs, far, owned_count)]
-    else:
-        blocks = [lax.all_gather(attended, "adapter", axis=0, tiled=True)]
-        part = down(ids, adapter_down_weight, blocks)
-    others = [swapped(b, "kv") for b in blocks]
-    base = base_projection(output_weight, blocks, others)
-
-    if direct:
+        fronts = [swapped(f, "adapter", j) for j, f in zip(shifts, fronts)]
+        beside = swapped(attended, "adapter", 1)
+        own = [attended, beside]
+        other = [swapped(b, "kv") for b in own]
+        backs = route_rest(ids, attended, fronts[0], capacity, owned_count, shifts)
+        part = down(ids, down_own, owned_count, rank, own + fronts, 2, backs[:1])
+        backs = [swapped(b, "adapter", j) for j, b in zip(shifts, backs)]
+        routed = [join(fronts), join(backs, ())]
+        part = part + swapped(part, "mp")
+        part = (part + swapped(part, "kv")).astype(jnp.bfloat16)
         mids = [part] + [swapped(part, "adapter", j) for j in range(1, owners)]
+        own_rest, other_rest = restore(
+            ids, routed, [swapped(r, "kv") for r in routed], part, owned_count, shifts
+        )
+        base = base_projection(output_weight, own + [own_rest], other + [other_rest])
         away = up(
             ids, base, adapter_up_weight, mids, "theirs", kept_rows, None, jnp.bfloat16
         )
@@ -478,7 +510,11 @@
             ids, base, adapter_up_weight, mids, "mine", kept_rows, residual, jnp.float32
         )
         return last(kept, back)
+    blocks = lax.all_gather(attended, "adapter", axis=0, tiled=True)
+    others = swapped(blocks, "kv")
+    part = down(ids, down_own, owned_count, rank, [blocks], 1)
     mids = [lax.psum(part, ("adapter", "mp", "kv"))]
+    base = base_projection(output_weight, [blocks], [others])
     terms = up(ids, base, adapter_up_weight, mids, "all", entire_rows, None, jnp.float32)
     summed = lax.psum_scatter(terms, "mp", scatter_dimension=0, tiled=True)
     return (residual.astype(jnp.float32) + summed).astype(jnp.bfloat16)

time: 51.2 us -> 46.3 us (0.904)
  waiting for transfers between devices: 15.3 us -> 12.2 us
  starting transfers between devices: 22.2 us -> 21 us
  Pallas kernels: 13.2 us -> 12.6 us
    ppermute x16 -> x17, waiting for transfers between devices: 15.3 us -> 12.2 us  [swapped(): lax.ppermute(x, axis, [(i, i ^ other) for i in range(lax.axis_size(axis))])]
    ppermute x16 -> x17, starting transfers between devices: 22.2 us -> 21 us  [swapped(): lax.ppermute(x, axis, [(i, i ^ other) for i in range(lax.axis_size(axis))])]
    pallas_call x4 -> x6, Pallas kernels: 3.99 us -> 3.38 us  [the longest x1 1.29 us: down(): pl.pallas_call(functools.partial(down_body, count, plain, rank, owned_cou...]
  transfers between devices with their start and end apart: 16 -> 17, of which waited for: 8 -> 5; matrix products, arithmetic and copies ran while one was open for 0% -> 0% of each run, Pallas kernels for 13% -> 15%
where the time goes in v3:
time: 46.3 us; the launch traced here: 46.1 us
  starting transfers between devices  21 us (45%)
  Pallas kernels  12.6 us (27%)
  waiting for transfers between devices  12.2 us (26%)
    ppermute x17, starting transfers between devices, swapped(): lax.ppermute(x, axis, [(i, i ^ other) for i in range(lax.axis_size(axis))])  21 us
    ppermute x17, waiting for transfers between devices, swapped(): lax.ppermute(x, axis, [(i, i ^ other) for i in range(lax.axis_size(axis))])  12.2 us
    pallas_call x1, Pallas kernels, attend_away(): pl.pallas_call(functools.partial(attend_away_body, features // kv_feature...  3.63 us
    pallas_call x1, Pallas kernels, attend_own(): pl.pallas_call(functools.partial(attend_own_body, group), in_specs=[pl.Bl...  1.99 us
    pallas_call x1, Pallas kernels, base_projection(): pl.pallas_call(functools.partial(base_body, count, unit, min(256, columns...  1.83 us
    pallas_call x1, Pallas kernels, down(): pl.pallas_call(functools.partial(down_body, count, plain, rank, owned_cou...  1.29 us
    pallas_call x2, Pallas kernels, up(): pl.pallas_call(functools.partial(up_body, len(mids), rank, which, residua...  1.06 us
  transfers between devices with their start and end apart: 17, of which 5 were waited for; matrix products, arithmetic and copies ran while one was open for 0% of the time, Pallas kernels for 15%

profile of v3, /device:TPU:0, one launch (start us, length us, event | category | flops | bytes accessed | tf_op | source)
XLA Modules:
  0.0 46.1 jit_solution(11023800791672418541)
XLA Ops:
  0.0 3.6 %attend_away.1 = (f32[48,2048]{1,0:T(8,128)S(1)}, f32[48,128]{1,0:T(8,128)S(1)}, bf16[3,16,2048]{2,1,0:T(8,128)(2,1)S(1)}, bf16[3,16,64,256]{3,2,1,0:T(8,128)(2,1)S(1)}, bf16[3,16,64,256]{3,2,1,0:T(8,128)(2,1)S(1)}) custom-call(s32[48]{0:T(128)} %lengths.1, bf16[48,4096]{1,0:T(8,128)(2,1)} %q_hbm.1, bf16[48,64,512]{2,1,0:T(8,128)(2,1)} %k_hbm.1, ...), custom_call_target="tpu_custom_call" | custom-call | flops 1000 | bytes 1000 | tf_op jit(solution)/shard_map/attend_away/pallas_call | solution.py:127
  3.7 0.5 %collective-permute-start = (f32[48,2048]{1,0:T(8,128)S(1)}, f32[48,2048]{1,0:T(8,128)S(1)}, u32[]{:S(2)}, u32[]{:S(2)}) collective-permute-start(f32[48,2048]{1,0:T(8,128)S(1)} %get-tuple-element.24), channel_id=1, source_target_pairs={{0,1},{1,0},{2,3},{3,2},{4,5},{5,4},{6,7},{7,6},{8,9},{9,8},{10,11... | collective-permute-start | bytes 1179656 | tf_op jit(solution)/shard_map/ppermute | solution.py:457
  4.3 2.0 %attend_own.1 = (f32[48,2048]{1,0:T(8,128)S(1)}, f32[48,128]{1,0:T(8,128)S(1)}) custom-call(s32[48]{0:T(128)S(1)} %copy-done.3, bf16[3,16,2048]{2,1,0:T(8,128)(2,1)S(1)} %get-tuple-element.19.q_ref, bf16[3,16,64,256]{3,2,1,0:T(8,128)(2,1)S(1)} %get-tuple-element.20.k_ref, bf16[3,16,64,256]{3,2,1,0:T(8,128)(2,1)S(1)} %get-tuple-element.21.v_ref), custom_call_target="tpu_custom_call" | custom-call | flops 1000 | bytes 1000 | tf_op jit(solution)/shard_map/attend_own/pallas_call | solution.py:156
  6.4 0.6 %merge.1 = (bf16[48,2048]{1,0:T(8,128)(2,1)S(1)}, bf16[24,2048]{1,0:T(8,128)(2,1)S(1)}, bf16[24,2048]{1,0:T(8,128)(2,1)S(1)}) custom-call(f32[48,2048]{1,0:T(8,128)S(1)} %get-tuple-element.22.own_ref, f32[48,128]{1,0:T(8,128)S(1)} %get-tuple-element.23.own_level, f32[48,2048]{1,0:T(8,128)S(1)} %collective-permute-done.other_ref, ...), custom_call_target="tpu_custom_call" | custom-call | flops 1000 | bytes 1000 | tf_op jit(solution)/shard_map/merge/pallas_call | solution.py:214
  7.0 3.1 %collective-permute-start.2 = (bf16[48,2048]{1,0:T(8,128)(2,1)S(1)}, bf16[48,2048]{1,0:T(8,128)(2,1)S(1)}, u32[]{:S(2)}, u32[]{:S(2)}) collective-permute-start(bf16[48,2048]{1,0:T(8,128)(2,1)S(1)} %get-tuple-element.26.rows_ref.refs_0_), channel_id=1, source_target_pairs={{0,4},{4,0},{8,12},{12,8},{1,5},{5,1},{9,13},{13,9},{2,6},{6,2},{1... | collective-permute-start | bytes 589832 | tf_op jit(solution)/shard_map/ppermute | solution.py:457
  10.1 2.6 %collective-permute-start.3 = (bf16[24,2048]{1,0:T(8,128)(2,1)S(1)}, bf16[24,2048]{1,0:T(8,128)(2,1)S(1)}, u32[]{:S(2)}, u32[]{:S(2)}) collective-permute-start(bf16[24,2048]{1,0:T(8,128)(2,1)S(1)} %get-tuple-element.27), channel_id=1, source_target_pairs={{0,8},{4,12},{8,0},{12,4},{1,9},{5,13},{9,1},{13,5},{2,10},{6,14},... | collective-permute-start | bytes 294920 | tf_op jit(solution)/shard_map/ppermute | solution.py:457
  12.7 4.8 %collective-permute-done.3.refs_0_._.refs_2_ = bf16[24,2048]{1,0:T(8,128)(2,1)S(1)} collective-permute-done((bf16[24,2048]{1,0:T(8,128)(2,1)S(1)}, bf16[24,2048]{1,0:T(8,128)(2,1)S(1)}, u32[]{:S(2)}, u32[]{:S(2)}) %collective-permute-start.3) | collective-permute-done | bytes 98336 | tf_op jit(solution)/shard_map/ppermute | solution.py:457
  17.5 0.6 %route_rest.1 = (bf16[24,2048]{1,0:T(8,128)(2,1)S(1)}, bf16[24,2048]{1,0:T(8,128)(2,1)S(1)}) custom-call(s32[192,128]{1,0:T(8,128)S(1)} %broadcast_in_dim.2.ids_ref, bf16[48,2048]{1,0:T(8,128)(2,1)S(1)} %get-tuple-element.26.rows_ref.refs_0_, bf16[24,2048]{1,0:T(8,128)(2,1)S(1)} %collective-permute-done.3.refs_0_._.refs_2_), custom_call_target="tpu_custom_call" | custom-call | flops 1000 | bytes 1000 | tf_op jit(solution)/shard_map/route_rest/pallas_call | solution.py:232
  18.1 3.5 %collective-permute-start.5 = (bf16[24,2048]{1,0:T(8,128)(2,1)S(1)}, bf16[24,2048]{1,0:T(8,128)(2,1)S(1)}, u32[]{:S(2)}, u32[]{:S(2)}) collective-permute-start(bf16[24,2048]{1,0:T(8,128)(2,1)S(1)} %get-tuple-element.29.refs_4_), channel_id=1, source_target_pairs={{0,8},{4,12},{8,0},{12,4},{1,9},{5,13},{9,1},{13,5},{2,10},{6,14},... | collective-permute-start | bytes 294920 | tf_op jit(solution)/shard_map/ppermute | solution.py:457
  21.6 2.5 %collective-permute-start.6 = (bf16[24,2048]{1,0:T(8,128)(2,1)S(1)}, bf16[24,2048]{1,0:T(8,128)(2,1)S(1)}, u32[]{:S(2)}, u32[]{:S(2)}) collective-permute-start(bf16[24,2048]{1,0:T(8,128)(2,1)S(1)} %get-tuple-element.30), channel_id=1, source_target_pairs={{0,12},{4,8},{8,4},{12,0},{1,13},{5,9},{9,5},{13,1},{2,14},{6,10},... | collective-permute-start | bytes 294920 | tf_op jit(solution)/shard_map/ppermute | solution.py:457
  24.1 1.3 %down.1 = f32[96,128]{1,0:T(8,128)S(1)} custom-call(s32[192,128]{1,0:T(8,128)S(1)} %broadcast_in_dim.2.ids_ref, bf16[512,2048]{1,0:T(8,128)(2,1)S(1)} %bitcast.8, bf16[48,2048]{1,0:T(8,128)(2,1)S(1)} %get-tuple-element.26.rows_ref.refs_0_, bf16[48,2048]{1,0:T(8,128)(2,1)S(1)} %collective-permute-done.2.refs_1_, ...), custom_call_target="tpu_custom_call" | custom-call | flops 1000 | bytes 1000 | tf_op jit(solution)/shard_map/down/pallas_call | solution.py:342
  25.4 1.6 %collective-permute-start.9 = (f32[96,128]{1,0:T(8,128)S(1)}, f32[96,128]{1,0:T(8,128)S(1)}, u32[]{:S(2)}, u32[]{:S(2)}) collective-permute-start(f32[96,128]{1,0:T(8,128)S(1)} %down.1), channel_id=1, source_target_pairs={{0,2},{2,0},{1,3},{3,1},{4,6},{6,4},{5,7},{7,5},{8,10},{10,8},{9,1... | collective-permute-start | bytes 147464 | tf_op jit(solution)/shard_map/ppermute | solution.py:457
  26.9 2.6 %collective-permute-done.9 = f32[96,128]{1,0:T(8,128)S(1)} collective-permute-done((f32[96,128]{1,0:T(8,128)S(1)}, f32[96,128]{1,0:T(8,128)S(1)}, u32[]{:S(2)}, u32[]{:S(2)}) %collective-permute-start.9) | collective-permute-done | bytes 49184 | tf_op jit(solution)/shard_map/ppermute | solution.py:457
  30.9 0.7 %collective-permute-start.13 = (bf16[96,128]{1,0:T(8,128)(2,1)S(1)}, bf16[96,128]{1,0:T(8,128)(2,1)S(1)}, u32[]{:S(2)}, u32[]{:S(2)}) collective-permute-start(bf16[96,128]{1,0:T(8,128)(2,1)S(1)} %add_convert_fusion.refs_4_.refs_0_), channel_id=1, source_target_pairs={{0,4},{4,0},{8,12},{12,8},{1,5},{5,1},{9,13},{13,9},{2,6},{6,2},{1... | collective-permute-start | bytes 73736 | tf_op jit(solution)/shard_map/ppermute | solution.py:457
  31.6 1.9 %collective-permute-start.14 = (bf16[96,128]{1,0:T(8,128)(2,1)S(1)}, bf16[96,128]{1,0:T(8,128)(2,1)S(1)}, u32[]{:S(2)}, u32[]{:S(2)}) collective-permute-start(bf16[96,128]{1,0:T(8,128)(2,1)S(1)} %add_convert_fusion.refs_4_.refs_0_), channel_id=1, source_target_pairs={{0,8},{4,12},{8,0},{12,4},{1,9},{5,13},{9,1},{13,5},{2,10},{6,14},... | collective-permute-start | bytes 73736 | tf_op jit(solution)/shard_map/ppermute | solution.py:457
  33.5 1.8 %collective-permute-start.15 = (bf16[96,128]{1,0:T(8,128)(2,1)S(1)}, bf16[96,128]{1,0:T(8,128)(2,1)S(1)}, u32[]{:S(2)}, u32[]{:S(2)}) collective-permute-start(bf16[96,128]{1,0:T(8,128)(2,1)S(1)} %add_convert_fusion.refs_4_.refs_0_), channel_id=1, source_target_pairs={{0,12},{4,8},{8,4},{12,0},{1,13},{5,9},{9,5},{13,1},{2,14},{6,10},... | collective-permute-start | bytes 73736 | tf_op jit(solution)/shard_map/ppermute | solution.py:457
  35.4 0.9 %restore.1 = (bf16[96,2048]{1,0:T(8,128)(2,1)S(1)}, bf16[96,2048]{1,0:T(8,128)(2,1)S(1)}) custom-call(s32[192,128]{1,0:T(8,128)S(1)} %broadcast_in_dim.2.ids_ref, bf16[2,24,2048]{2,1,0:T(8,128)(2,1)S(1)} %join.2.refs_0_, bf16[2,24,2048]{2,1,0:T(8,128)(2,1)S(1)} %join.3.refs_1_, bf16[2,24,2048]{2,1,0:T(8,128)(2,1)S(1)} %collective-permute-done.7.refs_2_, ...), custom_call_target="tpu_custom_call" | custom-call | flops 1000 | bytes 1000 | tf_op jit(solution)/shard_map/restore/pallas_call | solution.py:286
  36.3 1.8 %base.1.base_ref = f32[192,1024]{1,0:T(8,128)S(1)} custom-call(bf16[4096,1024]{1,0:T(8,128)(2,1)S(1)} %bitcast.7, bf16[48,2048]{1,0:T(8,128)(2,1)S(1)} %get-tuple-element.26.rows_ref.refs_0_, bf16[48,2048]{1,0:T(8,128)(2,1)S(1)} %collective-permute-done.2.refs_1_, bf16[96,2048]{1,0:T(8,128)(2,1)S(1)} %get-tuple-element.31.refs_2_, ...), custom_call_target="tpu_custom_call" | custom-call | flops 1000 | bytes 1000 | tf_op jit(solution)/shard_map/base/pallas_call | solution.py:445
  38.2 1.0 %collective-permute-done.15.refs_3_ = bf16[96,128]{1,0:T(8,128)(2,1)S(1)} collective-permute-done((bf16[96,128]{1,0:T(8,128)(2,1)S(1)}, bf16[96,128]{1,0:T(8,128)(2,1)S(1)}, u32[]{:S(2)}, u32[]{:S(2)}) %collective-permute-start.15) | collective-permute-done | bytes 24608 | tf_op jit(solution)/shard_map/ppermute | solution.py:457
  39.1 0.5 %up.3 = bf16[96,1024]{1,0:T(8,128)(2,1)S(1)} custom-call(s32[192,128]{1,0:T(8,128)S(1)} %broadcast_in_dim.2.ids_ref, f32[192,1024]{1,0:T(8,128)S(1)} %base.1.base_ref, bf16[1024,1024]{1,0:T(8,128)(2,1)S(1)} %bitcast.4, bf16[96,128]{1,0:T(8,128)(2,1)S(1)} %add_convert_fusion.refs_4_.refs_0_, bf16[96,128]{1,0:T(8,128)(2,1)S(1)} %collective-permute-done.13.refs_1_, ...), custom_call_target="tpu_custom_call" | custom-call | flops 1000 | bytes 1000 | tf_op jit(solution)/shard_map/up/pallas_call | solution.py:394
  39.7 1.6 %collective-permute-start.16 = (bf16[96,1024]{1,0:T(8,128)(2,1)S(1)}, bf16[96,1024]{1,0:T(8,128)(2,1)S(1)}, u32[]{:S(2)}, u32[]{:S(2)}) collective-permute-start(bf16[96,1024]{1,0:T(8,128)(2,1)S(1)} %up.3), channel_id=1, source_target_pairs={{0,2},{2,0},{1,3},{3,1},{4,6},{6,4},{5,7},{7,5},{8,10},{10,8},{9,1... | collective-permute-start | bytes 589832 | tf_op jit(solution)/shard_map/ppermute | solution.py:457
  41.2 0.5 %up.2.kept_ref = f32[96,1024]{1,0:T(8,128)S(1)} custom-call(s32[192,128]{1,0:T(8,128)S(1)} %broadcast_in_dim.2.ids_ref, f32[192,1024]{1,0:T(8,128)S(1)} %base.1.base_ref, bf16[1024,1024]{1,0:T(8,128)(2,1)S(1)} %bitcast.5, bf16[96,128]{1,0:T(8,128)(2,1)S(1)} %add_convert_fusion.refs_4_.refs_0_, bf16[96,128]{1,0:T(8,128)(2,1)S(1)} %collective-permute-done.13.refs_1_, ...), custom_call_target="tpu_custom_call" | custom-call | flops 1000 | bytes 1000 | tf_op jit(solution)/shard_map/up/pallas_call | solution.py:394
  41.8 3.6 %collective-permute-done.16.back_ref = bf16[96,1024]{1,0:T(8,128)(2,1)S(1)} collective-permute-done((bf16[96,1024]{1,0:T(8,128)(2,1)S(1)}, bf16[96,1024]{1,0:T(8,128)(2,1)S(1)}, u32[]{:S(2)}, u32[]{:S(2)}) %collective-permute-start.16) | collective-permute-done | bytes 196640 | tf_op jit(solution)/shard_map/ppermute | solution.py:457
  45.4 0.7 %last.1 = bf16[96,1024]{1,0:T(8,128)(2,1)} custom-call(f32[96,1024]{1,0:T(8,128)S(1)} %up.2.kept_ref, bf16[96,1024]{1,0:T(8,128)(2,1)S(1)} %collective-permute-done.16.back_ref), custom_call_target="tpu_custom_call" | custom-call | tf_op jit(solution)/shard_map/last/pallas_call | solution.py:412
  (40 shorter events, 1.6 us)
Async XLA Ops:
  0.0 4.3 %copy-start.3 = (s32[48]{0:T(128)S(1)}, s32[48]{0:T(128)}, u32[]{:S(2)}) copy-start(s32[48]{0:T(128)} %lengths.1) | copy-start | bytes 580
  0.0 36.2 %slice-start = ((s8[8388608]{0:T(1024)(128)(4,1)}), s8[4194304]{0:T(1024)(128)(4,1)S(1)}, s32[]{:S(2)}) async-start(s8[8388608]{0:T(1024)(128)(4,1)} %bitcast.6), calls=%async_computation | async-start | bytes 8388608
  3.6 2.6 %copy-start.4 = (s32[192]{0:T(256)S(1)}, s32[192]{0:T(256)}, u32[]{:S(2)}) copy-start(s32[192]{0:T(256)} %param.13) | copy-start | bytes 2308
  3.7 2.6 %collective-permute-start = (f32[48,2048]{1,0:T(8,128)S(1)}, f32[48,2048]{1,0:T(8,128)S(1)}, u32[]{:S(2)}, u32[]{:S(2)}) collective-permute-start(f32[48,2048]{1,0:T(8,128)S(1)} %get-tuple-element.24), channel_id=1, source_target_pairs={{0,1},{1,0},{2,3},{3,2},{4,5},{5,4},{6,7},{7,6},{8,9},{9,8},{10,11... | collective-permute-start | bytes 1179656 | tf_op jit(solution)/shard_map/ppermute | solution.py:457
  4.2 2.1 %collective-permute-start.1 = (f32[48,128]{1,0:T(8,128)S(1)}, f32[48,128]{1,0:T(8,128)S(1)}, u32[]{:S(2)}, u32[]{:S(2)}) collective-permute-start(f32[48,128]{1,0:T(8,128)S(1)} %get-tuple-element.25), channel_id=1, source_target_pairs={{0,1},{1,0},{2,3},{3,2},{4,5},{5,4},{6,7},{7,6},{8,9},{9,8},{10,11... | collective-permute-start | bytes 73736 | tf_op jit(solution)/shard_map/ppermute | solution.py:457
  4.3 19.8 %copy-start.1 = (bf16[8,2048,64]{1,2,0:T(8,128)(2,1)S(1)}, bf16[8,2048,64]{1,2,0:T(8,128)(2,1)}, u32[]{:S(2)}) copy-start(bf16[8,2048,64]{1,2,0:T(8,128)(2,1)} %param.16) | copy-start | bytes 6291460
  4.3 32.0 %slice-start.1 = ((s8[8388608]{0:T(1024)(128)(4,1)}), s8[4194304]{0:T(1024)(128)(4,1)S(1)}, s32[]{:S(2)}) async-start(s8[8388608]{0:T(1024)(128)(4,1)} %bitcast.6), calls=%async_computation.1 | async-start | bytes 8388608
  7.0 17.1 %collective-permute-start.2 = (bf16[48,2048]{1,0:T(8,128)(2,1)S(1)}, bf16[48,2048]{1,0:T(8,128)(2,1)S(1)}, u32[]{:S(2)}, u32[]{:S(2)}) collective-permute-start(bf16[48,2048]{1,0:T(8,128)(2,1)S(1)} %get-tuple-element.26.rows_ref.refs_0_), channel_id=1, source_target_pairs={{0,4},{4,0},{8,12},{12,8},{1,5},{5,1},{9,13},{13,9},{2,6},{6,2},{1... | collective-permute-start | bytes 589832 | tf_op jit(solution)/shard_map/ppermute | solution.py:457
  10.1 7.4 %collective-permute-start.3 = (bf16[24,2048]{1,0:T(8,128)(2,1)S(1)}, bf16[24,2048]{1,0:T(8,128)(2,1)S(1)}, u32[]{:S(2)}, u32[]{:S(2)}) collective-permute-start(bf16[24,2048]{1,0:T(8,128)(2,1)S(1)} %get-tuple-element.27), channel_id=1, source_target_pairs={{0,8},{4,12},{8,0},{12,4},{1,9},{5,13},{9,1},{13,5},{2,10},{6,14},... | collective-permute-start | bytes 294920 | tf_op jit(solution)/shard_map/ppermute | solution.py:457
  12.7 11.4 %collective-permute-start.4 = (bf16[24,2048]{1,0:T(8,128)(2,1)S(1)}, bf16[24,2048]{1,0:T(8,128)(2,1)S(1)}, u32[]{:S(2)}, u32[]{:S(2)}) collective-permute-start(bf16[24,2048]{1,0:T(8,128)(2,1)S(1)} %get-tuple-element.28), channel_id=1, source_target_pairs={{0,12},{4,8},{8,4},{12,0},{1,13},{5,9},{9,5},{13,1},{2,14},{6,10},... | collective-permute-start | bytes 294920 | tf_op jit(solution)/shard_map/ppermute | solution.py:457
  18.1 12.2 %collective-permute-start.5 = (bf16[24,2048]{1,0:T(8,128)(2,1)S(1)}, bf16[24,2048]{1,0:T(8,128)(2,1)S(1)}, u32[]{:S(2)}, u32[]{:S(2)}) collective-permute-start(bf16[24,2048]{1,0:T(8,128)(2,1)S(1)} %get-tuple-element.29.refs_4_), channel_id=1, source_target_pairs={{0,8},{4,12},{8,0},{12,4},{1,9},{5,13},{9,1},{13,5},{2,10},{6,14},... | collective-permute-start | bytes 294920 | tf_op jit(solution)/shard_map/ppermute | solution.py:457
  21.6 8.7 %collective-permute-start.6 = (bf16[24,2048]{1,0:T(8,128)(2,1)S(1)}, bf16[24,2048]{1,0:T(8,128)(2,1)S(1)}, u32[]{:S(2)}, u32[]{:S(2)}) collective-permute-start(bf16[24,2048]{1,0:T(8,128)(2,1)S(1)} %get-tuple-element.30), channel_id=1, source_target_pairs={{0,12},{4,8},{8,4},{12,0},{1,13},{5,9},{9,5},{13,1},{2,14},{6,10},... | collective-permute-start | bytes 294920 | tf_op jit(solution)/shard_map/ppermute | solution.py:457
  25.4 4.2 %collective-permute-start.9 = (f32[96,128]{1,0:T(8,128)S(1)}, f32[96,128]{1,0:T(8,128)S(1)}, u32[]{:S(2)}, u32[]{:S(2)}) collective-permute-start(f32[96,128]{1,0:T(8,128)S(1)} %down.1), channel_id=1, source_target_pairs={{0,2},{2,0},{1,3},{3,1},{4,6},{6,4},{5,7},{7,5},{8,10},{10,8},{9,1... | collective-permute-start | bytes 147464 | tf_op jit(solution)/shard_map/ppermute | solution.py:457
  29.5 1.3 %collective-permute-start.10 = (f32[96,128]{1,0:T(8,128)S(1)}, f32[96,128]{1,0:T(8,128)S(1)}, u32[]{:S(2)}, u32[]{:S(2)}) collective-permute-start(f32[96,128]{1,0:T(8,128)S(1)} %add.6), channel_id=1, source_target_pairs={{0,1},{1,0},{2,3},{3,2},{4,5},{5,4},{6,7},{7,6},{8,9},{9,8},{10,11... | collective-permute-start | bytes 147464 | tf_op jit(solution)/shard_map/ppermute | solution.py:457
  29.6 6.6 %collective-permute-start.11 = (bf16[48,2048]{1,0:T(8,128)(2,1)S(1)}, bf16[48,2048]{1,0:T(8,128)(2,1)S(1)}, u32[]{:S(2)}, u32[]{:S(2)}) collective-permute-start(bf16[48,2048]{1,0:T(8,128)(2,1)S(1)} %get-tuple-element.26.rows_ref.refs_0_), channel_id=1, source_target_pairs={{0,1},{1,0},{2,3},{3,2},{4,5},{5,4},{6,7},{7,6},{8,9},{9,8},{10,11... | collective-permute-start | bytes 589832 | tf_op jit(solution)/shard_map/ppermute | solution.py:457
  30.1 1.5 %collective-permute-start.7 = (bf16[2,24,2048]{2,1,0:T(8,128)(2,1)S(1)}, bf16[2,24,2048]{2,1,0:T(8,128)(2,1)S(1)}, u32[]{:S(2)}, u32[]{:S(2)}) collective-permute-start(bf16[2,24,2048]{2,1,0:T(8,128)(2,1)S(1)} %join.2.refs_0_), channel_id=1, source_target_pairs={{0,1},{1,0},{2,3},{3,2},{4,5},{5,4},{6,7},{7,6},{8,9},{9,8},{10,11... | collective-permute-start | bytes 589832 | tf_op jit(solution)/shard_map/ppermute | solution.py:457
  30.3 3.2 %collective-permute-start.8 = (bf16[2,24,2048]{2,1,0:T(8,128)(2,1)S(1)}, bf16[2,24,2048]{2,1,0:T(8,128)(2,1)S(1)}, u32[]{:S(2)}, u32[]{:S(2)}) collective-permute-start(bf16[2,24,2048]{2,1,0:T(8,128)(2,1)S(1)} %join.3.refs_1_), channel_id=1, source_target_pairs={{0,1},{1,0},{2,3},{3,2},{4,5},{5,4},{6,7},{7,6},{8,9},{9,8},{10,11... | collective-permute-start | bytes 589832 | tf_op jit(solution)/shard_map/ppermute | solution.py:457
  30.8 5.4 %collective-permute-start.12 = (bf16[48,2048]{1,0:T(8,128)(2,1)S(1)}, bf16[48,2048]{1,0:T(8,128)(2,1)S(1)}, u32[]{:S(2)}, u32[]{:S(2)}) collective-permute-start(bf16[48,2048]{1,0:T(8,128)(2,1)S(1)} %collective-permute-done.2.refs_1_), channel_id=1, source_target_pairs={{0,1},{1,0},{2,3},{3,2},{4,5},{5,4},{6,7},{7,6},{8,9},{9,8},{10,11... | collective-permute-start | bytes 589832 | tf_op jit(solution)/shard_map/ppermute | solution.py:457
  30.9 7.2 %collective-permute-start.13 = (bf16[96,128]{1,0:T(8,128)(2,1)S(1)}, bf16[96,128]{1,0:T(8,128)(2,1)S(1)}, u32[]{:S(2)}, u32[]{:S(2)}) collective-permute-start(bf16[96,128]{1,0:T(8,128)(2,1)S(1)} %add_convert_fusion.refs_4_.refs_0_), channel_id=1, source_target_pairs={{0,4},{4,0},{8,12},{12,8},{1,5},{5,1},{9,13},{13,9},{2,6},{6,2},{1... | collective-permute-start | bytes 73736 | tf_op jit(solution)/shard_map/ppermute | solution.py:457
  31.6 6.5 %collective-permute-start.14 = (bf16[96,128]{1,0:T(8,128)(2,1)S(1)}, bf16[96,128]{1,0:T(8,128)(2,1)S(1)}, u32[]{:S(2)}, u32[]{:S(2)}) collective-permute-start(bf16[96,128]{1,0:T(8,128)(2,1)S(1)} %add_convert_fusion.refs_4_.refs_0_), channel_id=1, source_target_pairs={{0,8},{4,12},{8,0},{12,4},{1,9},{5,13},{9,1},{13,5},{2,10},{6,14},... | collective-permute-start | bytes 73736 | tf_op jit(solution)/shard_map/ppermute | solution.py:457
  33.5 5.6 %collective-permute-start.15 = (bf16[96,128]{1,0:T(8,128)(2,1)S(1)}, bf16[96,128]{1,0:T(8,128)(2,1)S(1)}, u32[]{:S(2)}, u32[]{:S(2)}) collective-permute-start(bf16[96,128]{1,0:T(8,128)(2,1)S(1)} %add_convert_fusion.refs_4_.refs_0_), channel_id=1, source_target_pairs={{0,12},{4,8},{8,4},{12,0},{1,13},{5,9},{9,5},{13,1},{2,14},{6,10},... | collective-permute-start | bytes 73736 | tf_op jit(solution)/shard_map/ppermute | solution.py:457
  36.3 2.9 %copy-start = (bf16[16,64,1024]{2,1,0:T(8,128)(2,1)S(1)}, bf16[16,64,1024]{2,1,0:T(8,128)(2,1)}, u32[]{:S(2)}) copy-start(bf16[16,64,1024]{2,1,0:T(8,128)(2,1)} %param.17) | copy-start | bytes 6291460
  38.1 3.1 %copy-start.2 = (bf16[96,1024]{1,0:T(8,128)(2,1)S(1)}, bf16[96,1024]{1,0:T(8,128)(2,1)}, u32[]{:S(2)}) copy-start(bf16[96,1024]{1,0:T(8,128)(2,1)} %refs_4_.1) | copy-start | bytes 589828
  39.7 5.7 %collective-permute-start.16 = (bf16[96,1024]{1,0:T(8,128)(2,1)S(1)}, bf16[96,1024]{1,0:T(8,128)(2,1)S(1)}, u32[]{:S(2)}, u32[]{:S(2)}) collective-permute-start(bf16[96,1024]{1,0:T(8,128)(2,1)S(1)} %up.3), channel_id=1, source_target_pairs={{0,2},{2,0},{1,3},{3,1},{4,6},{6,4},{5,7},{7,5},{8,10},{10,8},{9,1... | collective-permute-start | bytes 589832 | tf_op jit(solution)/shard_map/ppermute | solution.py:457

commit v4 on v3

--- a/solution.py
+++ b/solution.py
@@ -492,7 +492,7 @@
         own = [attended, beside]
         other = [swapped(b, "kv") for b in own]
         backs = route_rest(ids, attended, fronts[0], capacity, owned_count, shifts)
-        part = down(ids, down_own, owned_count, rank, own + fronts, 2, backs[:1])
+        part = down(ids, down_own, owned_count, rank, own + fronts, 2, [backs[0], other[0]])
         backs = [swapped(b, "adapter", j) for j, b in zip(shifts, backs)]
         routed = [join(fronts), join(backs, ())]
         part = part + swapped(part, "mp")

time: 46.3 us -> 46.1 us (level)
  transfers between devices with their start and end apart: 17 -> 17, of which waited for: 5 -> 4; matrix products, arithmetic and copies ran while one was open for 0% -> 0% of each run, Pallas kernels for 15% -> 15%
where the time goes in v4:
time: 46.1 us; the launch traced here: 45.9 us
  starting transfers between devices  21 us (46%)
  Pallas kernels  12.6 us (27%)
  waiting for transfers between devices  12 us (26%)
    ppermute x17, starting transfers between devices, swapped(): lax.ppermute(x, axis, [(i, i ^ other) for i in range(lax.axis_size(axis))])  21 us
    ppermute x17, waiting for transfers between devices, swapped(): lax.ppermute(x, axis, [(i, i ^ other) for i in range(lax.axis_size(axis))])  12 us
    pallas_call x1, Pallas kernels, attend_away(): pl.pallas_call(functools.partial(attend_away_body, features // kv_feature...  3.63 us
    pallas_call x1, Pallas kernels, attend_own(): pl.pallas_call(functools.partial(attend_own_body, group), in_specs=[pl.Bl...  1.99 us
    pallas_call x1, Pallas kernels, base_projection(): pl.pallas_call(functools.partial(base_body, count, unit, min(256, columns...  1.83 us
    pallas_call x1, Pallas kernels, down(): pl.pallas_call(functools.partial(down_body, count, plain, rank, owned_cou...  1.29 us
    pallas_call x2, Pallas kernels, up(): pl.pallas_call(functools.partial(up_body, len(mids), rank, which, residua...  1.06 us
  transfers between devices with their start and end apart: 17, of which 4 were waited for; matrix products, arithmetic and copies ran while one was open for 0% of the time, Pallas kernels for 15%

profile of v4, /device:TPU:0, one launch (start us, length us, event | category | flops | bytes accessed | tf_op | source)
XLA Modules:
  0.0 45.9 jit_solution(4873121977012070071)
XLA Ops:
  0.0 3.6 %attend_away.1 = (f32[48,2048]{1,0:T(8,128)S(1)}, f32[48,128]{1,0:T(8,128)S(1)}, bf16[3,16,2048]{2,1,0:T(8,128)(2,1)S(1)}, bf16[3,16,64,256]{3,2,1,0:T(8,128)(2,1)S(1)}, bf16[3,16,64,256]{3,2,1,0:T(8,128)(2,1)S(1)}) custom-call(s32[48]{0:T(128)} %lengths.1, bf16[48,4096]{1,0:T(8,128)(2,1)} %q_hbm.1, bf16[48,64,512]{2,1,0:T(8,128)(2,1)} %k_hbm.1, ...), custom_call_target="tpu_custom_call" | custom-call | flops 1000 | bytes 1000 | tf_op jit(solution)/shard_map/attend_away/pallas_call | solution.py:127
  4.3 2.0 %attend_own.1 = (f32[48,2048]{1,0:T(8,128)S(1)}, f32[48,128]{1,0:T(8,128)S(1)}) custom-call(s32[48]{0:T(128)S(1)} %copy-done.3, bf16[3,16,2048]{2,1,0:T(8,128)(2,1)S(1)} %get-tuple-element.19.q_ref, bf16[3,16,64,256]{3,2,1,0:T(8,128)(2,1)S(1)} %get-tuple-element.20.k_ref, bf16[3,16,64,256]{3,2,1,0:T(8,128)(2,1)S(1)} %get-tuple-element.21.v_ref), custom_call_target="tpu_custom_call" | custom-call | flops 1000 | bytes 1000 | tf_op jit(solution)/shard_map/attend_own/pallas_call | solution.py:156
  6.4 0.6 %merge.1 = (bf16[48,2048]{1,0:T(8,128)(2,1)S(1)}, bf16[24,2048]{1,0:T(8,128)(2,1)S(1)}, bf16[24,2048]{1,0:T(8,128)(2,1)S(1)}) custom-call(f32[48,2048]{1,0:T(8,128)S(1)} %get-tuple-element.22.own_ref, f32[48,128]{1,0:T(8,128)S(1)} %get-tuple-element.23.own_level, f32[48,2048]{1,0:T(8,128)S(1)} %collective-permute-done.other_ref, ...), custom_call_target="tpu_custom_call" | custom-call | flops 1000 | bytes 1000 | tf_op jit(solution)/shard_map/merge/pallas_call | solution.py:214
  7.0 3.1 %collective-permute-start.2 = (bf16[48,2048]{1,0:T(8,128)(2,1)S(1)}, bf16[48,2048]{1,0:T(8,128)(2,1)S(1)}, u32[]{:S(2)}, u32[]{:S(2)}) collective-permute-start(bf16[48,2048]{1,0:T(8,128)(2,1)S(1)} %get-tuple-element.26.rows_ref.refs_0_), channel_id=1, source_target_pairs={{0,4},{4,0},{8,12},{12,8},{1,5},{5,1},{9,13},{13,9},{2,6},{6,2},{1... | collective-permute-start | bytes 589832 | tf_op jit(solution)/shard_map/ppermute | solution.py:457
  10.1 2.6 %collective-permute-start.3 = (bf16[24,2048]{1,0:T(8,128)(2,1)S(1)}, bf16[24,2048]{1,0:T(8,128)(2,1)S(1)}, u32[]{:S(2)}, u32[]{:S(2)}) collective-permute-start(bf16[24,2048]{1,0:T(8,128)(2,1)S(1)} %get-tuple-element.27), channel_id=1, source_target_pairs={{0,8},{4,12},{8,0},{12,4},{1,9},{5,13},{9,1},{13,5},{2,10},{6,14},... | collective-permute-start | bytes 294920 | tf_op jit(solution)/shard_map/ppermute | solution.py:457
  12.7 4.8 %collective-permute-done.3.refs_0_._.refs_2_ = bf16[24,2048]{1,0:T(8,128)(2,1)S(1)} collective-permute-done((bf16[24,2048]{1,0:T(8,128)(2,1)S(1)}, bf16[24,2048]{1,0:T(8,128)(2,1)S(1)}, u32[]{:S(2)}, u32[]{:S(2)}) %collective-permute-start.3) | collective-permute-done | bytes 98336 | tf_op jit(solution)/shard_map/ppermute | solution.py:457
  17.5 0.6 %route_rest.1 = (bf16[24,2048]{1,0:T(8,128)(2,1)S(1)}, bf16[24,2048]{1,0:T(8,128)(2,1)S(1)}) custom-call(s32[192,128]{1,0:T(8,128)S(1)} %broadcast_in_dim.2.ids_ref, bf16[48,2048]{1,0:T(8,128)(2,1)S(1)} %get-tuple-element.26.rows_ref.refs_0_, bf16[24,2048]{1,0:T(8,128)(2,1)S(1)} %collective-permute-done.3.refs_0_._.refs_2_), custom_call_target="tpu_custom_call" | custom-call | flops 1000 | bytes 1000 | tf_op jit(solution)/shard_map/route_rest/pallas_call | solution.py:232
  18.1 3.5 %collective-permute-start.5 = (bf16[24,2048]{1,0:T(8,128)(2,1)S(1)}, bf16[24,2048]{1,0:T(8,128)(2,1)S(1)}, u32[]{:S(2)}, u32[]{:S(2)}) collective-permute-start(bf16[24,2048]{1,0:T(8,128)(2,1)S(1)} %get-tuple-element.29.refs_4_), channel_id=1, source_target_pairs={{0,8},{4,12},{8,0},{12,4},{1,9},{5,13},{9,1},{13,5},{2,10},{6,14},... | collective-permute-start | bytes 294920 | tf_op jit(solution)/shard_map/ppermute | solution.py:457
  21.6 2.5 %collective-permute-start.6 = (bf16[24,2048]{1,0:T(8,128)(2,1)S(1)}, bf16[24,2048]{1,0:T(8,128)(2,1)S(1)}, u32[]{:S(2)}, u32[]{:S(2)}) collective-permute-start(bf16[24,2048]{1,0:T(8,128)(2,1)S(1)} %get-tuple-element.30), channel_id=1, source_target_pairs={{0,12},{4,8},{8,4},{12,0},{1,13},{5,9},{9,5},{13,1},{2,14},{6,10},... | collective-permute-start | bytes 294920 | tf_op jit(solution)/shard_map/ppermute | solution.py:457
  24.1 1.3 %down.1 = f32[96,128]{1,0:T(8,128)S(1)} custom-call(s32[192,128]{1,0:T(8,128)S(1)} %broadcast_in_dim.2.ids_ref, bf16[512,2048]{1,0:T(8,128)(2,1)S(1)} %bitcast.8, bf16[48,2048]{1,0:T(8,128)(2,1)S(1)} %get-tuple-element.26.rows_ref.refs_0_, bf16[48,2048]{1,0:T(8,128)(2,1)S(1)} %collective-permute-done.2.refs_1_, ...), custom_call_target="tpu_custom_call" | custom-call | flops 1000 | bytes 1000 | tf_op jit(solution)/shard_map/down/pallas_call | solution.py:342
  25.4 1.5 %collective-permute-start.10 = (f32[96,128]{1,0:T(8,128)S(1)}, f32[96,128]{1,0:T(8,128)S(1)}, u32[]{:S(2)}, u32[]{:S(2)}) collective-permute-start(f32[96,128]{1,0:T(8,128)S(1)} %down.1), channel_id=1, source_target_pairs={{0,2},{2,0},{1,3},{3,1},{4,6},{6,4},{5,7},{7,5},{8,10},{10,8},{9,1... | collective-permute-start | bytes 147464 | tf_op jit(solution)/shard_map/ppermute | solution.py:457
  26.9 2.6 %collective-permute-done.10 = f32[96,128]{1,0:T(8,128)S(1)} collective-permute-done((f32[96,128]{1,0:T(8,128)S(1)}, f32[96,128]{1,0:T(8,128)S(1)}, u32[]{:S(2)}, u32[]{:S(2)}) %collective-permute-start.10) | collective-permute-done | bytes 49184 | tf_op jit(solution)/shard_map/ppermute | solution.py:457
  29.7 0.6 %collective-permute-start.7 = (bf16[2,24,2048]{2,1,0:T(8,128)(2,1)S(1)}, bf16[2,24,2048]{2,1,0:T(8,128)(2,1)S(1)}, u32[]{:S(2)}, u32[]{:S(2)}) collective-permute-start(bf16[2,24,2048]{2,1,0:T(8,128)(2,1)S(1)} %join.2.refs_0_), channel_id=1, source_target_pairs={{0,1},{1,0},{2,3},{3,2},{4,5},{5,4},{6,7},{7,6},{8,9},{9,8},{10,11... | collective-permute-start | bytes 589832 | tf_op jit(solution)/shard_map/ppermute | solution.py:457
  30.9 1.3 %collective-permute-start.13 = (bf16[96,128]{1,0:T(8,128)(2,1)S(1)}, bf16[96,128]{1,0:T(8,128)(2,1)S(1)}, u32[]{:S(2)}, u32[]{:S(2)}) collective-permute-start(bf16[96,128]{1,0:T(8,128)(2,1)S(1)} %add_convert_fusion.refs_4_.refs_0_), channel_id=1, source_target_pairs={{0,4},{4,0},{8,12},{12,8},{1,5},{5,1},{9,13},{13,9},{2,6},{6,2},{1... | collective-permute-start | bytes 73736 | tf_op jit(solution)/shard_map/ppermute | solution.py:457
  32.2 1.1 %collective-permute-start.14 = (bf16[96,128]{1,0:T(8,128)(2,1)S(1)}, bf16[96,128]{1,0:T(8,128)(2,1)S(1)}, u32[]{:S(2)}, u32[]{:S(2)}) collective-permute-start(bf16[96,128]{1,0:T(8,128)(2,1)S(1)} %add_convert_fusion.refs_4_.refs_0_), channel_id=1, source_target_pairs={{0,8},{4,12},{8,0},{12,4},{1,9},{5,13},{9,1},{13,5},{2,10},{6,14},... | collective-permute-start | bytes 73736 | tf_op jit(solution)/shard_map/ppermute | solution.py:457
  33.3 2.0 %collective-permute-start.15 = (bf16[96,128]{1,0:T(8,128)(2,1)S(1)}, bf16[96,128]{1,0:T(8,128)(2,1)S(1)}, u32[]{:S(2)}, u32[]{:S(2)}) collective-permute-start(bf16[96,128]{1,0:T(8,128)(2,1)S(1)} %add_convert_fusion.refs_4_.refs_0_), channel_id=1, source_target_pairs={{0,12},{4,8},{8,4},{12,0},{1,13},{5,9},{9,5},{13,1},{2,14},{6,10},... | collective-permute-start | bytes 73736 | tf_op jit(solution)/shard_map/ppermute | solution.py:457
  35.3 0.8 %restore.1 = (bf16[96,2048]{1,0:T(8,128)(2,1)S(1)}, bf16[96,2048]{1,0:T(8,128)(2,1)S(1)}) custom-call(s32[192,128]{1,0:T(8,128)S(1)} %broadcast_in_dim.2.ids_ref, bf16[2,24,2048]{2,1,0:T(8,128)(2,1)S(1)} %join.2.refs_0_, bf16[2,24,2048]{2,1,0:T(8,128)(2,1)S(1)} %join.3.refs_1_, bf16[2,24,2048]{2,1,0:T(8,128)(2,1)S(1)} %collective-permute-done.7.refs_2_, ...), custom_call_target="tpu_custom_call" | custom-call | flops 1000 | bytes 1000 | tf_op jit(solution)/shard_map/restore/pallas_call | solution.py:286
  36.2 1.8 %base.1.base_ref = f32[192,1024]{1,0:T(8,128)S(1)} custom-call(bf16[4096,1024]{1,0:T(8,128)(2,1)S(1)} %bitcast.7, bf16[48,2048]{1,0:T(8,128)(2,1)S(1)} %get-tuple-element.26.rows_ref.refs_0_, bf16[48,2048]{1,0:T(8,128)(2,1)S(1)} %collective-permute-done.2.refs_1_, bf16[96,2048]{1,0:T(8,128)(2,1)S(1)} %get-tuple-element.31.refs_2_, ...), custom_call_target="tpu_custom_call" | custom-call | flops 1000 | bytes 1000 | tf_op jit(solution)/shard_map/base/pallas_call | solution.py:445
  38.1 0.9 %collective-permute-done.15.refs_3_ = bf16[96,128]{1,0:T(8,128)(2,1)S(1)} collective-permute-done((bf16[96,128]{1,0:T(8,128)(2,1)S(1)}, bf16[96,128]{1,0:T(8,128)(2,1)S(1)}, u32[]{:S(2)}, u32[]{:S(2)}) %collective-permute-start.15) | collective-permute-done | bytes 24608 | tf_op jit(solution)/shard_map/ppermute | solution.py:457
  38.9 0.5 %up.3 = bf16[96,1024]{1,0:T(8,128)(2,1)S(1)} custom-call(s32[192,128]{1,0:T(8,128)S(1)} %broadcast_in_dim.2.ids_ref, f32[192,1024]{1,0:T(8,128)S(1)} %base.1.base_ref, bf16[1024,1024]{1,0:T(8,128)(2,1)S(1)} %bitcast.4, bf16[96,128]{1,0:T(8,128)(2,1)S(1)} %add_convert_fusion.refs_4_.refs_0_, bf16[96,128]{1,0:T(8,128)(2,1)S(1)} %collective-permute-done.13.refs_1_, ...), custom_call_target="tpu_custom_call" | custom-call | flops 1000 | bytes 1000 | tf_op jit(solution)/shard_map/up/pallas_call | solution.py:394
  39.5 1.6 %collective-permute-start.16 = (bf16[96,1024]{1,0:T(8,128)(2,1)S(1)}, bf16[96,1024]{1,0:T(8,128)(2,1)S(1)}, u32[]{:S(2)}, u32[]{:S(2)}) collective-permute-start(bf16[96,1024]{1,0:T(8,128)(2,1)S(1)} %up.3), channel_id=1, source_target_pairs={{0,2},{2,0},{1,3},{3,1},{4,6},{6,4},{5,7},{7,5},{8,10},{10,8},{9,1... | collective-permute-start | bytes 589832 | tf_op jit(solution)/shard_map/ppermute | solution.py:457
  41.0 0.5 %up.2.kept_ref = f32[96,1024]{1,0:T(8,128)S(1)} custom-call(s32[192,128]{1,0:T(8,128)S(1)} %broadcast_in_dim.2.ids_ref, f32[192,1024]{1,0:T(8,128)S(1)} %base.1.base_ref, bf16[1024,1024]{1,0:T(8,128)(2,1)S(1)} %bitcast.5, bf16[96,128]{1,0:T(8,128)(2,1)S(1)} %add_convert_fusion.refs_4_.refs_0_, bf16[96,128]{1,0:T(8,128)(2,1)S(1)} %collective-permute-done.13.refs_1_, ...), custom_call_target="tpu_custom_call" | custom-call | flops 1000 | bytes 1000 | tf_op jit(solution)/shard_map/up/pallas_call | solution.py:394
  41.6 3.6 %collective-permute-done.16.back_ref = bf16[96,1024]{1,0:T(8,128)(2,1)S(1)} collective-permute-done((bf16[96,1024]{1,0:T(8,128)(2,1)S(1)}, bf16[96,1024]{1,0:T(8,128)(2,1)S(1)}, u32[]{:S(2)}, u32[]{:S(2)}) %collective-permute-start.16) | collective-permute-done | bytes 196640 | tf_op jit(solution)/shard_map/ppermute | solution.py:457
  45.2 0.7 %last.1 = bf16[96,1024]{1,0:T(8,128)(2,1)} custom-call(f32[96,1024]{1,0:T(8,128)S(1)} %up.2.kept_ref, bf16[96,1024]{1,0:T(8,128)(2,1)S(1)} %collective-permute-done.16.back_ref), custom_call_target="tpu_custom_call" | custom-call | tf_op jit(solution)/shard_map/last/pallas_call | solution.py:412
  (40 shorter events, 1.5 us)
Async XLA Ops:
  0.0 4.3 %copy-start.3 = (s32[48]{0:T(128)S(1)}, s32[48]{0:T(128)}, u32[]{:S(2)}) copy-start(s32[48]{0:T(128)} %lengths.1) | copy-start | bytes 580
  0.0 36.2 %slice-start = ((s8[8388608]{0:T(1024)(128)(4,1)}), s8[4194304]{0:T(1024)(128)(4,1)S(1)}, s32[]{:S(2)}) async-start(s8[8388608]{0:T(1024)(128)(4,1)} %bitcast.6), calls=%async_computation | async-start | bytes 8388608
  3.6 2.6 %copy-start.4 = (s32[192]{0:T(256)S(1)}, s32[192]{0:T(256)}, u32[]{:S(2)}) copy-start(s32[192]{0:T(256)} %param.13) | copy-start | bytes 2308
  3.7 2.6 %collective-permute-start = (f32[48,2048]{1,0:T(8,128)S(1)}, f32[48,2048]{1,0:T(8,128)S(1)}, u32[]{:S(2)}, u32[]{:S(2)}) collective-permute-start(f32[48,2048]{1,0:T(8,128)S(1)} %get-tuple-element.24), channel_id=1, source_target_pairs={{0,1},{1,0},{2,3},{3,2},{4,5},{5,4},{6,7},{7,6},{8,9},{9,8},{10,11... | collective-permute-start | bytes 1179656 | tf_op jit(solution)/shard_map/ppermute | solution.py:457
  4.2 2.1 %collective-permute-start.1 = (f32[48,128]{1,0:T(8,128)S(1)}, f32[48,128]{1,0:T(8,128)S(1)}, u32[]{:S(2)}, u32[]{:S(2)}) collective-permute-start(f32[48,128]{1,0:T(8,128)S(1)} %get-tuple-element.25), channel_id=1, source_target_pairs={{0,1},{1,0},{2,3},{3,2},{4,5},{5,4},{6,7},{7,6},{8,9},{9,8},{10,11... | collective-permute-start | bytes 73736 | tf_op jit(solution)/shard_map/ppermute | solution.py:457
  4.3 19.8 %copy-start.1 = (bf16[8,2048,64]{1,2,0:T(8,128)(2,1)S(1)}, bf16[8,2048,64]{1,2,0:T(8,128)(2,1)}, u32[]{:S(2)}) copy-start(bf16[8,2048,64]{1,2,0:T(8,128)(2,1)} %param.16) | copy-start | bytes 6291460
  4.3 31.9 %slice-start.1 = ((s8[8388608]{0:T(1024)(128)(4,1)}), s8[4194304]{0:T(1024)(128)(4,1)S(1)}, s32[]{:S(2)}) async-start(s8[8388608]{0:T(1024)(128)(4,1)} %bitcast.6), calls=%async_computation.1 | async-start | bytes 8388608
  7.0 17.1 %collective-permute-start.2 = (bf16[48,2048]{1,0:T(8,128)(2,1)S(1)}, bf16[48,2048]{1,0:T(8,128)(2,1)S(1)}, u32[]{:S(2)}, u32[]{:S(2)}) collective-permute-start(bf16[48,2048]{1,0:T(8,128)(2,1)S(1)} %get-tuple-element.26.rows_ref.refs_0_), channel_id=1, source_target_pairs={{0,4},{4,0},{8,12},{12,8},{1,5},{5,1},{9,13},{13,9},{2,6},{6,2},{1... | collective-permute-start | bytes 589832 | tf_op jit(solution)/shard_map/ppermute | solution.py:457
  10.1 14.0 %collective-permute-start.9 = (bf16[48,2048]{1,0:T(8,128)(2,1)S(1)}, bf16[48,2048]{1,0:T(8,128)(2,1)S(1)}, u32[]{:S(2)}, u32[]{:S(2)}) collective-permute-start(bf16[48,2048]{1,0:T(8,128)(2,1)S(1)} %get-tuple-element.26.rows_ref.refs_0_), channel_id=1, source_target_pairs={{0,1},{1,0},{2,3},{3,2},{4,5},{5,4},{6,7},{7,6},{8,9},{9,8},{10,11... | collective-permute-start | bytes 589832 | tf_op jit(solution)/shard_map/ppermute | solution.py:457
  10.1 7.4 %collective-permute-start.3 = (bf16[24,2048]{1,0:T(8,128)(2,1)S(1)}, bf16[24,2048]{1,0:T(8,128)(2,1)S(1)}, u32[]{:S(2)}, u32[]{:S(2)}) collective-permute-start(bf16[24,2048]{1,0:T(8,128)(2,1)S(1)} %get-tuple-element.27), channel_id=1, source_target_pairs={{0,8},{4,12},{8,0},{12,4},{1,9},{5,13},{9,1},{13,5},{2,10},{6,14},... | collective-permute-start | bytes 294920 | tf_op jit(solution)/shard_map/ppermute | solution.py:457
  12.7 11.4 %collective-permute-start.4 = (bf16[24,2048]{1,0:T(8,128)(2,1)S(1)}, bf16[24,2048]{1,0:T(8,128)(2,1)S(1)}, u32[]{:S(2)}, u32[]{:S(2)}) collective-permute-start(bf16[24,2048]{1,0:T(8,128)(2,1)S(1)} %get-tuple-element.28), channel_id=1, source_target_pairs={{0,12},{4,8},{8,4},{12,0},{1,13},{5,9},{9,5},{13,1},{2,14},{6,10},... | collective-permute-start | bytes 294920 | tf_op jit(solution)/shard_map/ppermute | solution.py:457
  18.1 12.1 %collective-permute-start.5 = (bf16[24,2048]{1,0:T(8,128)(2,1)S(1)}, bf16[24,2048]{1,0:T(8,128)(2,1)S(1)}, u32[]{:S(2)}, u32[]{:S(2)}) collective-permute-start(bf16[24,2048]{1,0:T(8,128)(2,1)S(1)} %get-tuple-element.29.refs_4_), channel_id=1, source_target_pairs={{0,8},{4,12},{8,0},{12,4},{1,9},{5,13},{9,1},{13,5},{2,10},{6,14},... | collective-permute-start | bytes 294920 | tf_op jit(solution)/shard_map/ppermute | solution.py:457
  21.6 8.6 %collective-permute-start.6 = (bf16[24,2048]{1,0:T(8,128)(2,1)S(1)}, bf16[24,2048]{1,0:T(8,128)(2,1)S(1)}, u32[]{:S(2)}, u32[]{:S(2)}) collective-permute-start(bf16[24,2048]{1,0:T(8,128)(2,1)S(1)} %get-tuple-element.30), channel_id=1, source_target_pairs={{0,12},{4,8},{8,4},{12,0},{1,13},{5,9},{9,5},{13,1},{2,14},{6,10},... | collective-permute-start | bytes 294920 | tf_op jit(solution)/shard_map/ppermute | solution.py:457
  25.4 4.2 %collective-permute-start.10 = (f32[96,128]{1,0:T(8,128)S(1)}, f32[96,128]{1,0:T(8,128)S(1)}, u32[]{:S(2)}, u32[]{:S(2)}) collective-permute-start(f32[96,128]{1,0:T(8,128)S(1)} %down.1), channel_id=1, source_target_pairs={{0,2},{2,0},{1,3},{3,1},{4,6},{6,4},{5,7},{7,5},{8,10},{10,8},{9,1... | collective-permute-start | bytes 147464 | tf_op jit(solution)/shard_map/ppermute | solution.py:457
  29.6 1.3 %collective-permute-start.11 = (f32[96,128]{1,0:T(8,128)S(1)}, f32[96,128]{1,0:T(8,128)S(1)}, u32[]{:S(2)}, u32[]{:S(2)}) collective-permute-start(f32[96,128]{1,0:T(8,128)S(1)} %add.6), channel_id=1, source_target_pairs={{0,1},{1,0},{2,3},{3,2},{4,5},{5,4},{6,7},{7,6},{8,9},{9,8},{10,11... | collective-permute-start | bytes 147464 | tf_op jit(solution)/shard_map/ppermute | solution.py:457
  29.7 3.7 %collective-permute-start.7 = (bf16[2,24,2048]{2,1,0:T(8,128)(2,1)S(1)}, bf16[2,24,2048]{2,1,0:T(8,128)(2,1)S(1)}, u32[]{:S(2)}, u32[]{:S(2)}) collective-permute-start(bf16[2,24,2048]{2,1,0:T(8,128)(2,1)S(1)} %join.2.refs_0_), channel_id=1, source_target_pairs={{0,1},{1,0},{2,3},{3,2},{4,5},{5,4},{6,7},{7,6},{8,9},{9,8},{10,11... | collective-permute-start | bytes 589832 | tf_op jit(solution)/shard_map/ppermute | solution.py:457
  30.2 5.1 %collective-permute-start.8 = (bf16[2,24,2048]{2,1,0:T(8,128)(2,1)S(1)}, bf16[2,24,2048]{2,1,0:T(8,128)(2,1)S(1)}, u32[]{:S(2)}, u32[]{:S(2)}) collective-permute-start(bf16[2,24,2048]{2,1,0:T(8,128)(2,1)S(1)} %join.3.refs_1_), channel_id=1, source_target_pairs={{0,1},{1,0},{2,3},{3,2},{4,5},{5,4},{6,7},{7,6},{8,9},{9,8},{10,11... | collective-permute-start | bytes 589832 | tf_op jit(solution)/shard_map/ppermute | solution.py:457
  30.3 5.8 %collective-permute-start.12 = (bf16[48,2048]{1,0:T(8,128)(2,1)S(1)}, bf16[48,2048]{1,0:T(8,128)(2,1)S(1)}, u32[]{:S(2)}, u32[]{:S(2)}) collective-permute-start(bf16[48,2048]{1,0:T(8,128)(2,1)S(1)} %collective-permute-done.2.refs_1_), channel_id=1, source_target_pairs={{0,1},{1,0},{2,3},{3,2},{4,5},{5,4},{6,7},{7,6},{8,9},{9,8},{10,11... | collective-permute-start | bytes 589832 | tf_op jit(solution)/shard_map/ppermute | solution.py:457
  30.9 7.2 %collective-permute-start.13 = (bf16[96,128]{1,0:T(8,128)(2,1)S(1)}, bf16[96,128]{1,0:T(8,128)(2,1)S(1)}, u32[]{:S(2)}, u32[]{:S(2)}) collective-permute-start(bf16[96,128]{1,0:T(8,128)(2,1)S(1)} %add_convert_fusion.refs_4_.refs_0_), channel_id=1, source_target_pairs={{0,4},{4,0},{8,12},{12,8},{1,5},{5,1},{9,13},{13,9},{2,6},{6,2},{1... | collective-permute-start | bytes 73736 | tf_op jit(solution)/shard_map/ppermute | solution.py:457
  32.2 5.8 %collective-permute-start.14 = (bf16[96,128]{1,0:T(8,128)(2,1)S(1)}, bf16[96,128]{1,0:T(8,128)(2,1)S(1)}, u32[]{:S(2)}, u32[]{:S(2)}) collective-permute-start(bf16[96,128]{1,0:T(8,128)(2,1)S(1)} %add_convert_fusion.refs_4_.refs_0_), channel_id=1, source_target_pairs={{0,8},{4,12},{8,0},{12,4},{1,9},{5,13},{9,1},{13,5},{2,10},{6,14},... | collective-permute-start | bytes 73736 | tf_op jit(solution)/shard_map/ppermute | solution.py:457
  33.3 5.6 %collective-permute-start.15 = (bf16[96,128]{1,0:T(8,128)(2,1)S(1)}, bf16[96,128]{1,0:T(8,128)(2,1)S(1)}, u32[]{:S(2)}, u32[]{:S(2)}) collective-permute-start(bf16[96,128]{1,0:T(8,128)(2,1)S(1)} %add_convert_fusion.refs_4_.refs_0_), channel_id=1, source_target_pairs={{0,12},{4,8},{8,4},{12,0},{1,13},{5,9},{9,5},{13,1},{2,14},{6,10},... | collective-permute-start | bytes 73736 | tf_op jit(solution)/shard_map/ppermute | solution.py:457
  36.2 2.8 %copy-start = (bf16[16,64,1024]{2,1,0:T(8,128)(2,1)S(1)}, bf16[16,64,1024]{2,1,0:T(8,128)(2,1)}, u32[]{:S(2)}) copy-start(bf16[16,64,1024]{2,1,0:T(8,128)(2,1)} %param.17) | copy-start | bytes 6291460
  38.0 3.0 %copy-start.2 = (bf16[96,1024]{1,0:T(8,128)(2,1)S(1)}, bf16[96,1024]{1,0:T(8,128)(2,1)}, u32[]{:S(2)}) copy-start(bf16[96,1024]{1,0:T(8,128)(2,1)} %refs_4_.1) | copy-start | bytes 589828
  39.5 5.7 %collective-permute-start.16 = (bf16[96,1024]{1,0:T(8,128)(2,1)S(1)}, bf16[96,1024]{1,0:T(8,128)(2,1)S(1)}, u32[]{:S(2)}, u32[]{:S(2)}) collective-permute-start(bf16[96,1024]{1,0:T(8,128)(2,1)S(1)} %up.3), channel_id=1, source_target_pairs={{0,2},{2,0},{1,3},{3,1},{4,6},{6,4},{5,7},{7,5},{8,10},{10,8},{9,1... | collective-permute-start | bytes 589832 | tf_op jit(solution)/shard_map/ppermute | solution.py:457

commit v5 on v4

--- a/solution.py
+++ b/solution.py
@@ -497,7 +497,7 @@
         routed = [join(fronts), join(backs, ())]
         part = part + swapped(part, "mp")
         part = (part + swapped(part, "kv")).astype(jnp.bfloat16)
-        mids = [part] + [swapped(part, "adapter", j) for j in range(1, owners)]
+        mids = [part] + [swapped(part, "adapter", j) for j in range(owners - 1, 0, -1)]
         own_rest, other_rest = restore(
             ids, routed, [swapped(r, "kv") for r in routed], part, owned_count, shifts
         )

time: 46.1 us -> 45.7 us (level)
  transfers between devices with their start and end apart: 17 -> 17, of which waited for: 4 -> 3; matrix products, arithmetic and copies ran while one was open for 0% -> 0% of each run, Pallas kernels for 15% -> 16%
where the time goes in v5:
time: 45.7 us; the launch traced here: 45.5 us
  starting transfers between devices  21 us (46%)
  Pallas kernels  12.6 us (28%)
  waiting for transfers between devices  11.6 us (25%)
    ppermute x17, starting transfers between devices, swapped(): lax.ppermute(x, axis, [(i, i ^ other) for i in range(lax.axis_size(axis))])  21 us
    ppermute x17, waiting for transfers between devices, swapped(): lax.ppermute(x, axis, [(i, i ^ other) for i in range(lax.axis_size(axis))])  11.6 us
    pallas_call x1, Pallas kernels, attend_away(): pl.pallas_call(functools.partial(attend_away_body, features // kv_feature...  3.63 us
    pallas_call x1, Pallas kernels, attend_own(): pl.pallas_call(functools.partial(attend_own_body, group), in_specs=[pl.Bl...  1.99 us
    pallas_call x1, Pallas kernels, base_projection(): pl.pallas_call(functools.partial(base_body, count, unit, min(256, columns...  1.83 us
    pallas_call x1, Pallas kernels, down(): pl.pallas_call(functools.partial(down_body, count, plain, rank, owned_cou...  1.29 us
    pallas_call x2, Pallas kernels, up(): pl.pallas_call(functools.partial(up_body, len(mids), rank, which, residua...  1.06 us
  transfers between devices with their start and end apart: 17, of which 3 were waited for; matrix products, arithmetic and copies ran while one was open for 0% of the time, Pallas kernels for 16%

profile of v5, /device:TPU:0, one launch (start us, length us, event | category | flops | bytes accessed | tf_op | source)
XLA Modules:
  0.0 45.5 jit_solution(16210931995777722073)
XLA Ops:
  0.0 3.6 %attend_away.1 = (f32[48,2048]{1,0:T(8,128)S(1)}, f32[48,128]{1,0:T(8,128)S(1)}, bf16[3,16,2048]{2,1,0:T(8,128)(2,1)S(1)}, bf16[3,16,64,256]{3,2,1,0:T(8,128)(2,1)S(1)}, bf16[3,16,64,256]{3,2,1,0:T(8,128)(2,1)S(1)}) custom-call(s32[48]{0:T(128)} %lengths.1, bf16[48,4096]{1,0:T(8,128)(2,1)} %q_hbm.1, bf16[48,64,512]{2,1,0:T(8,128)(2,1)} %k_hbm.1, ...), custom_call_target="tpu_custom_call" | custom-call | flops 1000 | bytes 1000 | tf_op jit(solution)/shard_map/attend_away/pallas_call | solution.py:127
  3.7 0.5 %collective-permute-start = (f32[48,2048]{1,0:T(8,128)S(1)}, f32[48,2048]{1,0:T(8,128)S(1)}, u32[]{:S(2)}, u32[]{:S(2)}) collective-permute-start(f32[48,2048]{1,0:T(8,128)S(1)} %get-tuple-element.24), channel_id=1, source_target_pairs={{0,1},{1,0},{2,3},{3,2},{4,5},{5,4},{6,7},{7,6},{8,9},{9,8},{10,11... | collective-permute-start | bytes 1179656 | tf_op jit(solution)/shard_map/ppermute | solution.py:457
  4.3 2.0 %attend_own.1 = (f32[48,2048]{1,0:T(8,128)S(1)}, f32[48,128]{1,0:T(8,128)S(1)}) custom-call(s32[48]{0:T(128)S(1)} %copy-done.3, bf16[3,16,2048]{2,1,0:T(8,128)(2,1)S(1)} %get-tuple-element.19.q_ref, bf16[3,16,64,256]{3,2,1,0:T(8,128)(2,1)S(1)} %get-tuple-element.20.k_ref, bf16[3,16,64,256]{3,2,1,0:T(8,128)(2,1)S(1)} %get-tuple-element.21.v_ref), custom_call_target="tpu_custom_call" | custom-call | flops 1000 | bytes 1000 | tf_op jit(solution)/shard_map/attend_own/pallas_call | solution.py:156
  6.4 0.6 %merge.1 = (bf16[48,2048]{1,0:T(8,128)(2,1)S(1)}, bf16[24,2048]{1,0:T(8,128)(2,1)S(1)}, bf16[24,2048]{1,0:T(8,128)(2,1)S(1)}) custom-call(f32[48,2048]{1,0:T(8,128)S(1)} %get-tuple-element.22.own_ref, f32[48,128]{1,0:T(8,128)S(1)} %get-tuple-element.23.own_level, f32[48,2048]{1,0:T(8,128)S(1)} %collective-permute-done.other_ref, ...), custom_call_target="tpu_custom_call" | custom-call | flops 1000 | bytes 1000 | tf_op jit(solution)/shard_map/merge/pallas_call | solution.py:214
  7.0 3.1 %collective-permute-start.2 = (bf16[48,2048]{1,0:T(8,128)(2,1)S(1)}, bf16[48,2048]{1,0:T(8,128)(2,1)S(1)}, u32[]{:S(2)}, u32[]{:S(2)}) collective-permute-start(bf16[48,2048]{1,0:T(8,128)(2,1)S(1)} %get-tuple-element.26.rows_ref.refs_0_), channel_id=1, source_target_pairs={{0,4},{4,0},{8,12},{12,8},{1,5},{5,1},{9,13},{13,9},{2,6},{6,2},{1... | collective-permute-start | bytes 589832 | tf_op jit(solution)/shard_map/ppermute | solution.py:457
  10.1 2.6 %collective-permute-start.3 = (bf16[24,2048]{1,0:T(8,128)(2,1)S(1)}, bf16[24,2048]{1,0:T(8,128)(2,1)S(1)}, u32[]{:S(2)}, u32[]{:S(2)}) collective-permute-start(bf16[24,2048]{1,0:T(8,128)(2,1)S(1)} %get-tuple-element.27), channel_id=1, source_target_pairs={{0,8},{4,12},{8,0},{12,4},{1,9},{5,13},{9,1},{13,5},{2,10},{6,14},... | collective-permute-start | bytes 294920 | tf_op jit(solution)/shard_map/ppermute | solution.py:457
  12.7 4.8 %collective-permute-done.3.refs_0_._.refs_2_ = bf16[24,2048]{1,0:T(8,128)(2,1)S(1)} collective-permute-done((bf16[24,2048]{1,0:T(8,128)(2,1)S(1)}, bf16[24,2048]{1,0:T(8,128)(2,1)S(1)}, u32[]{:S(2)}, u32[]{:S(2)}) %collective-permute-start.3) | collective-permute-done | bytes 98336 | tf_op jit(solution)/shard_map/ppermute | solution.py:457
  17.5 0.6 %route_rest.1 = (bf16[24,2048]{1,0:T(8,128)(2,1)S(1)}, bf16[24,2048]{1,0:T(8,128)(2,1)S(1)}) custom-call(s32[192,128]{1,0:T(8,128)S(1)} %broadcast_in_dim.2.ids_ref, bf16[48,2048]{1,0:T(8,128)(2,1)S(1)} %get-tuple-element.26.rows_ref.refs_0_, bf16[24,2048]{1,0:T(8,128)(2,1)S(1)} %collective-permute-done.3.refs_0_._.refs_2_), custom_call_target="tpu_custom_call" | custom-call | flops 1000 | bytes 1000 | tf_op jit(solution)/shard_map/route_rest/pallas_call | solution.py:232
  18.1 3.5 %collective-permute-start.5 = (bf16[24,2048]{1,0:T(8,128)(2,1)S(1)}, bf16[24,2048]{1,0:T(8,128)(2,1)S(1)}, u32[]{:S(2)}, u32[]{:S(2)}) collective-permute-start(bf16[24,2048]{1,0:T(8,128)(2,1)S(1)} %get-tuple-element.29.refs_4_), channel_id=1, source_target_pairs={{0,8},{4,12},{8,0},{12,4},{1,9},{5,13},{9,1},{13,5},{2,10},{6,14},... | collective-permute-start | bytes 294920 | tf_op jit(solution)/shard_map/ppermute | solution.py:457
  21.6 2.5 %collective-permute-start.6 = (bf16[24,2048]{1,0:T(8,128)(2,1)S(1)}, bf16[24,2048]{1,0:T(8,128)(2,1)S(1)}, u32[]{:S(2)}, u32[]{:S(2)}) collective-permute-start(bf16[24,2048]{1,0:T(8,128)(2,1)S(1)} %get-tuple-element.30), channel_id=1, source_target_pairs={{0,12},{4,8},{8,4},{12,0},{1,13},{5,9},{9,5},{13,1},{2,14},{6,10},... | collective-permute-start | bytes 294920 | tf_op jit(solution)/shard_map/ppermute | solution.py:457
  24.1 1.3 %down.1 = f32[96,128]{1,0:T(8,128)S(1)} custom-call(s32[192,128]{1,0:T(8,128)S(1)} %broadcast_in_dim.2.ids_ref, bf16[512,2048]{1,0:T(8,128)(2,1)S(1)} %bitcast.8, bf16[48,2048]{1,0:T(8,128)(2,1)S(1)} %get-tuple-element.26.rows_ref.refs_0_, bf16[48,2048]{1,0:T(8,128)(2,1)S(1)} %collective-permute-done.2.refs_1_, ...), custom_call_target="tpu_custom_call" | custom-call | flops 1000 | bytes 1000 | tf_op jit(solution)/shard_map/down/pallas_call | solution.py:342
  25.4 1.5 %collective-permute-start.10 = (f32[96,128]{1,0:T(8,128)S(1)}, f32[96,128]{1,0:T(8,128)S(1)}, u32[]{:S(2)}, u32[]{:S(2)}) collective-permute-start(f32[96,128]{1,0:T(8,128)S(1)} %down.1), channel_id=1, source_target_pairs={{0,2},{2,0},{1,3},{3,1},{4,6},{6,4},{5,7},{7,5},{8,10},{10,8},{9,1... | collective-permute-start | bytes 147464 | tf_op jit(solution)/shard_map/ppermute | solution.py:457
  26.9 2.6 %collective-permute-done.10 = f32[96,128]{1,0:T(8,128)S(1)} collective-permute-done((f32[96,128]{1,0:T(8,128)S(1)}, f32[96,128]{1,0:T(8,128)S(1)}, u32[]{:S(2)}, u32[]{:S(2)}) %collective-permute-start.10) | collective-permute-done | bytes 49184 | tf_op jit(solution)/shard_map/ppermute | solution.py:457
  29.7 0.6 %collective-permute-start.7 = (bf16[2,24,2048]{2,1,0:T(8,128)(2,1)S(1)}, bf16[2,24,2048]{2,1,0:T(8,128)(2,1)S(1)}, u32[]{:S(2)}, u32[]{:S(2)}) collective-permute-start(bf16[2,24,2048]{2,1,0:T(8,128)(2,1)S(1)} %join.2.refs_0_), channel_id=1, source_target_pairs={{0,1},{1,0},{2,3},{3,2},{4,5},{5,4},{6,7},{7,6},{8,9},{9,8},{10,11... | collective-permute-start | bytes 589832 | tf_op jit(solution)/shard_map/ppermute | solution.py:457
  30.9 1.7 %collective-permute-start.13 = (bf16[96,128]{1,0:T(8,128)(2,1)S(1)}, bf16[96,128]{1,0:T(8,128)(2,1)S(1)}, u32[]{:S(2)}, u32[]{:S(2)}) collective-permute-start(bf16[96,128]{1,0:T(8,128)(2,1)S(1)} %add_convert_fusion.refs_4_.refs_0_), channel_id=1, source_target_pairs={{0,12},{4,8},{8,4},{12,0},{1,13},{5,9},{9,5},{13,1},{2,14},{6,10},... | collective-permute-start | bytes 73736 | tf_op jit(solution)/shard_map/ppermute | solution.py:457
  32.6 1.1 %collective-permute-start.14 = (bf16[96,128]{1,0:T(8,128)(2,1)S(1)}, bf16[96,128]{1,0:T(8,128)(2,1)S(1)}, u32[]{:S(2)}, u32[]{:S(2)}) collective-permute-start(bf16[96,128]{1,0:T(8,128)(2,1)S(1)} %add_convert_fusion.refs_4_.refs_0_), channel_id=1, source_target_pairs={{0,8},{4,12},{8,0},{12,4},{1,9},{5,13},{9,1},{13,5},{2,10},{6,14},... | collective-permute-start | bytes 73736 | tf_op jit(solution)/shard_map/ppermute | solution.py:457
  33.7 1.6 %collective-permute-start.15 = (bf16[96,128]{1,0:T(8,128)(2,1)S(1)}, bf16[96,128]{1,0:T(8,128)(2,1)S(1)}, u32[]{:S(2)}, u32[]{:S(2)}) collective-permute-start(bf16[96,128]{1,0:T(8,128)(2,1)S(1)} %add_convert_fusion.refs_4_.refs_0_), channel_id=1, source_target_pairs={{0,4},{4,0},{8,12},{12,8},{1,5},{5,1},{9,13},{13,9},{2,6},{6,2},{1... | collective-permute-start | bytes 73736 | tf_op jit(solution)/shard_map/ppermute | solution.py:457
  35.3 0.8 %restore.1 = (bf16[96,2048]{1,0:T(8,128)(2,1)S(1)}, bf16[96,2048]{1,0:T(8,128)(2,1)S(1)}) custom-call(s32[192,128]{1,0:T(8,128)S(1)} %broadcast_in_dim.2.ids_ref, bf16[2,24,2048]{2,1,0:T(8,128)(2,1)S(1)} %join.2.refs_0_, bf16[2,24,2048]{2,1,0:T(8,128)(2,1)S(1)} %join.3.refs_1_, bf16[2,24,2048]{2,1,0:T(8,128)(2,1)S(1)} %collective-permute-done.7.refs_2_, ...), custom_call_target="tpu_custom_call" | custom-call | flops 1000 | bytes 1000 | tf_op jit(solution)/shard_map/restore/pallas_call | solution.py:286
  36.2 1.8 %base.1.base_ref = f32[192,1024]{1,0:T(8,128)S(1)} custom-call(bf16[4096,1024]{1,0:T(8,128)(2,1)S(1)} %bitcast.7, bf16[48,2048]{1,0:T(8,128)(2,1)S(1)} %get-tuple-element.26.rows_ref.refs_0_, bf16[48,2048]{1,0:T(8,128)(2,1)S(1)} %collective-permute-done.2.refs_1_, bf16[96,2048]{1,0:T(8,128)(2,1)S(1)} %get-tuple-element.31.refs_2_, ...), custom_call_target="tpu_custom_call" | custom-call | flops 1000 | bytes 1000 | tf_op jit(solution)/shard_map/base/pallas_call | solution.py:445
  38.1 0.5 %up.3 = bf16[96,1024]{1,0:T(8,128)(2,1)S(1)} custom-call(s32[192,128]{1,0:T(8,128)S(1)} %broadcast_in_dim.2.ids_ref, f32[192,1024]{1,0:T(8,128)S(1)} %base.1.base_ref, bf16[1024,1024]{1,0:T(8,128)(2,1)S(1)} %bitcast.4, bf16[96,128]{1,0:T(8,128)(2,1)S(1)} %add_convert_fusion.refs_4_.refs_0_, bf16[96,128]{1,0:T(8,128)(2,1)S(1)} %collective-permute-done.13.refs_1_, ...), custom_call_target="tpu_custom_call" | custom-call | flops 1000 | bytes 1000 | tf_op jit(solution)/shard_map/up/pallas_call | solution.py:394
  38.6 1.6 %collective-permute-start.16 = (bf16[96,1024]{1,0:T(8,128)(2,1)S(1)}, bf16[96,1024]{1,0:T(8,128)(2,1)S(1)}, u32[]{:S(2)}, u32[]{:S(2)}) collective-permute-start(bf16[96,1024]{1,0:T(8,128)(2,1)S(1)} %up.3), channel_id=1, source_target_pairs={{0,2},{2,0},{1,3},{3,1},{4,6},{6,4},{5,7},{7,5},{8,10},{10,8},{9,1... | collective-permute-start | bytes 589832 | tf_op jit(solution)/shard_map/ppermute | solution.py:457
  40.2 0.5 %up.2.kept_ref = f32[96,1024]{1,0:T(8,128)S(1)} custom-call(s32[192,128]{1,0:T(8,128)S(1)} %broadcast_in_dim.2.ids_ref, f32[192,1024]{1,0:T(8,128)S(1)} %base.1.base_ref, bf16[1024,1024]{1,0:T(8,128)(2,1)S(1)} %bitcast.5, bf16[96,128]{1,0:T(8,128)(2,1)S(1)} %add_convert_fusion.refs_4_.refs_0_, bf16[96,128]{1,0:T(8,128)(2,1)S(1)} %collective-permute-done.13.refs_1_, ...), custom_call_target="tpu_custom_call" | custom-call | flops 1000 | bytes 1000 | tf_op jit(solution)/shard_map/up/pallas_call | solution.py:394
  40.8 4.1 %collective-permute-done.16.back_ref = bf16[96,1024]{1,0:T(8,128)(2,1)S(1)} collective-permute-done((bf16[96,1024]{1,0:T(8,128)(2,1)S(1)}, bf16[96,1024]{1,0:T(8,128)(2,1)S(1)}, u32[]{:S(2)}, u32[]{:S(2)}) %collective-permute-start.16) | collective-permute-done | bytes 196640 | tf_op jit(solution)/shard_map/ppermute | solution.py:457
  44.8 0.7 %last.1 = bf16[96,1024]{1,0:T(8,128)(2,1)} custom-call(f32[96,1024]{1,0:T(8,128)S(1)} %up.2.kept_ref, bf16[96,1024]{1,0:T(8,128)(2,1)S(1)} %collective-permute-done.16.back_ref), custom_call_target="tpu_custom_call" | custom-call | tf_op jit(solution)/shard_map/last/pallas_call | solution.py:412
  (40 shorter events, 1.0 us)
Async XLA Ops:
  0.0 4.3 %copy-start.3 = (s32[48]{0:T(128)S(1)}, s32[48]{0:T(128)}, u32[]{:S(2)}) copy-start(s32[48]{0:T(128)} %lengths.1) | copy-start | bytes 580
  0.0 36.2 %slice-start = ((s8[8388608]{0:T(1024)(128)(4,1)}), s8[4194304]{0:T(1024)(128)(4,1)S(1)}, s32[]{:S(2)}) async-start(s8[8388608]{0:T(1024)(128)(4,1)} %bitcast.6), calls=%async_computation | async-start | bytes 8388608
  3.6 2.6 %copy-start.4 = (s32[192]{0:T(256)S(1)}, s32[192]{0:T(256)}, u32[]{:S(2)}) copy-start(s32[192]{0:T(256)} %param.13) | copy-start | bytes 2308
  3.7 2.6 %collective-permute-start = (f32[48,2048]{1,0:T(8,128)S(1)}, f32[48,2048]{1,0:T(8,128)S(1)}, u32[]{:S(2)}, u32[]{:S(2)}) collective-permute-start(f32[48,2048]{1,0:T(8,128)S(1)} %get-tuple-element.24), channel_id=1, source_target_pairs={{0,1},{1,0},{2,3},{3,2},{4,5},{5,4},{6,7},{7,6},{8,9},{9,8},{10,11... | collective-permute-start | bytes 1179656 | tf_op jit(solution)/shard_map/ppermute | solution.py:457
  4.2 2.1 %collective-permute-start.1 = (f32[48,128]{1,0:T(8,128)S(1)}, f32[48,128]{1,0:T(8,128)S(1)}, u32[]{:S(2)}, u32[]{:S(2)}) collective-permute-start(f32[48,128]{1,0:T(8,128)S(1)} %get-tuple-element.25), channel_id=1, source_target_pairs={{0,1},{1,0},{2,3},{3,2},{4,5},{5,4},{6,7},{7,6},{8,9},{9,8},{10,11... | collective-permute-start | bytes 73736 | tf_op jit(solution)/shard_map/ppermute | solution.py:457
  4.3 19.8 %copy-start.1 = (bf16[8,2048,64]{1,2,0:T(8,128)(2,1)S(1)}, bf16[8,2048,64]{1,2,0:T(8,128)(2,1)}, u32[]{:S(2)}) copy-start(bf16[8,2048,64]{1,2,0:T(8,128)(2,1)} %param.16) | copy-start | bytes 6291460
  4.3 31.9 %slice-start.1 = ((s8[8388608]{0:T(1024)(128)(4,1)}), s8[4194304]{0:T(1024)(128)(4,1)S(1)}, s32[]{:S(2)}) async-start(s8[8388608]{0:T(1024)(128)(4,1)} %bitcast.6), calls=%async_computation.1 | async-start | bytes 8388608
  7.0 17.1 %collective-permute-start.2 = (bf16[48,2048]{1,0:T(8,128)(2,1)S(1)}, bf16[48,2048]{1,0:T(8,128)(2,1)S(1)}, u32[]{:S(2)}, u32[]{:S(2)}) collective-permute-start(bf16[48,2048]{1,0:T(8,128)(2,1)S(1)} %get-tuple-element.26.rows_ref.refs_0_), channel_id=1, source_target_pairs={{0,4},{4,0},{8,12},{12,8},{1,5},{5,1},{9,13},{13,9},{2,6},{6,2},{1... | collective-permute-start | bytes 589832 | tf_op jit(solution)/shard_map/ppermute | solution.py:457
  10.1 14.0 %collective-permute-start.9 = (bf16[48,2048]{1,0:T(8,128)(2,1)S(1)}, bf16[48,2048]{1,0:T(8,128)(2,1)S(1)}, u32[]{:S(2)}, u32[]{:S(2)}) collective-permute-start(bf16[48,2048]{1,0:T(8,128)(2,1)S(1)} %get-tuple-element.26.rows_ref.refs_0_), channel_id=1, source_target_pairs={{0,1},{1,0},{2,3},{3,2},{4,5},{5,4},{6,7},{7,6},{8,9},{9,8},{10,11... | collective-permute-start | bytes 589832 | tf_op jit(solution)/shard_map/ppermute | solution.py:457
  10.1 7.4 %collective-permute-start.3 = (bf16[24,2048]{1,0:T(8,128)(2,1)S(1)}, bf16[24,2048]{1,0:T(8,128)(2,1)S(1)}, u32[]{:S(2)}, u32[]{:S(2)}) collective-permute-start(bf16[24,2048]{1,0:T(8,128)(2,1)S(1)} %get-tuple-element.27), channel_id=1, source_target_pairs={{0,8},{4,12},{8,0},{12,4},{1,9},{5,13},{9,1},{13,5},{2,10},{6,14},... | collective-permute-start | bytes 294920 | tf_op jit(solution)/shard_map/ppermute | solution.py:457
  12.7 11.4 %collective-permute-start.4 = (bf16[24,2048]{1,0:T(8,128)(2,1)S(1)}, bf16[24,2048]{1,0:T(8,128)(2,1)S(1)}, u32[]{:S(2)}, u32[]{:S(2)}) collective-permute-start(bf16[24,2048]{1,0:T(8,128)(2,1)S(1)} %get-tuple-element.28), channel_id=1, source_target_pairs={{0,12},{4,8},{8,4},{12,0},{1,13},{5,9},{9,5},{13,1},{2,14},{6,10},... | collective-permute-start | bytes 294920 | tf_op jit(solution)/shard_map/ppermute | solution.py:457
  18.1 12.1 %collective-permute-start.5 = (bf16[24,2048]{1,0:T(8,128)(2,1)S(1)}, bf16[24,2048]{1,0:T(8,128)(2,1)S(1)}, u32[]{:S(2)}, u32[]{:S(2)}) collective-permute-start(bf16[24,2048]{1,0:T(8,128)(2,1)S(1)} %get-tuple-element.29.refs_4_), channel_id=1, source_target_pairs={{0,8},{4,12},{8,0},{12,4},{1,9},{5,13},{9,1},{13,5},{2,10},{6,14},... | collective-permute-start | bytes 294920 | tf_op jit(solution)/shard_map/ppermute | solution.py:457
  21.6 8.6 %collective-permute-start.6 = (bf16[24,2048]{1,0:T(8,128)(2,1)S(1)}, bf16[24,2048]{1,0:T(8,128)(2,1)S(1)}, u32[]{:S(2)}, u32[]{:S(2)}) collective-permute-start(bf16[24,2048]{1,0:T(8,128)(2,1)S(1)} %get-tuple-element.30), channel_id=1, source_target_pairs={{0,12},{4,8},{8,4},{12,0},{1,13},{5,9},{9,5},{13,1},{2,14},{6,10},... | collective-permute-start | bytes 294920 | tf_op jit(solution)/shard_map/ppermute | solution.py:457
  25.4 4.2 %collective-permute-start.10 = (f32[96,128]{1,0:T(8,128)S(1)}, f32[96,128]{1,0:T(8,128)S(1)}, u32[]{:S(2)}, u32[]{:S(2)}) collective-permute-start(f32[96,128]{1,0:T(8,128)S(1)} %down.1), channel_id=1, source_target_pairs={{0,2},{2,0},{1,3},{3,1},{4,6},{6,4},{5,7},{7,5},{8,10},{10,8},{9,1... | collective-permute-start | bytes 147464 | tf_op jit(solution)/shard_map/ppermute | solution.py:457
  29.6 1.3 %collective-permute-start.11 = (f32[96,128]{1,0:T(8,128)S(1)}, f32[96,128]{1,0:T(8,128)S(1)}, u32[]{:S(2)}, u32[]{:S(2)}) collective-permute-start(f32[96,128]{1,0:T(8,128)S(1)} %add.6), channel_id=1, source_target_pairs={{0,1},{1,0},{2,3},{3,2},{4,5},{5,4},{6,7},{7,6},{8,9},{9,8},{10,11... | collective-permute-start | bytes 147464 | tf_op jit(solution)/shard_map/ppermute | solution.py:457
  29.7 4.0 %collective-permute-start.7 = (bf16[2,24,2048]{2,1,0:T(8,128)(2,1)S(1)}, bf16[2,24,2048]{2,1,0:T(8,128)(2,1)S(1)}, u32[]{:S(2)}, u32[]{:S(2)}) collective-permute-start(bf16[2,24,2048]{2,1,0:T(8,128)(2,1)S(1)} %join.2.refs_0_), channel_id=1, source_target_pairs={{0,1},{1,0},{2,3},{3,2},{4,5},{5,4},{6,7},{7,6},{8,9},{9,8},{10,11... | collective-permute-start | bytes 589832 | tf_op jit(solution)/shard_map/ppermute | solution.py:457
  30.2 5.1 %collective-permute-start.8 = (bf16[2,24,2048]{2,1,0:T(8,128)(2,1)S(1)}, bf16[2,24,2048]{2,1,0:T(8,128)(2,1)S(1)}, u32[]{:S(2)}, u32[]{:S(2)}) collective-permute-start(bf16[2,24,2048]{2,1,0:T(8,128)(2,1)S(1)} %join.3.refs_1_), channel_id=1, source_target_pairs={{0,1},{1,0},{2,3},{3,2},{4,5},{5,4},{6,7},{7,6},{8,9},{9,8},{10,11... | collective-permute-start | bytes 589832 | tf_op jit(solution)/shard_map/ppermute | solution.py:457
  30.3 5.8 %collective-permute-start.12 = (bf16[48,2048]{1,0:T(8,128)(2,1)S(1)}, bf16[48,2048]{1,0:T(8,128)(2,1)S(1)}, u32[]{:S(2)}, u32[]{:S(2)}) collective-permute-start(bf16[48,2048]{1,0:T(8,128)(2,1)S(1)} %collective-permute-done.2.refs_1_), channel_id=1, source_target_pairs={{0,1},{1,0},{2,3},{3,2},{4,5},{5,4},{6,7},{7,6},{8,9},{9,8},{10,11... | collective-permute-start | bytes 589832 | tf_op jit(solution)/shard_map/ppermute | solution.py:457
  30.9 7.2 %collective-permute-start.13 = (bf16[96,128]{1,0:T(8,128)(2,1)S(1)}, bf16[96,128]{1,0:T(8,128)(2,1)S(1)}, u32[]{:S(2)}, u32[]{:S(2)}) collective-permute-start(bf16[96,128]{1,0:T(8,128)(2,1)S(1)} %add_convert_fusion.refs_4_.refs_0_), channel_id=1, source_target_pairs={{0,12},{4,8},{8,4},{12,0},{1,13},{5,9},{9,5},{13,1},{2,14},{6,10},... | collective-permute-start | bytes 73736 | tf_op jit(solution)/shard_map/ppermute | solution.py:457
  32.6 5.5 %collective-permute-start.14 = (bf16[96,128]{1,0:T(8,128)(2,1)S(1)}, bf16[96,128]{1,0:T(8,128)(2,1)S(1)}, u32[]{:S(2)}, u32[]{:S(2)}) collective-permute-start(bf16[96,128]{1,0:T(8,128)(2,1)S(1)} %add_convert_fusion.refs_4_.refs_0_), channel_id=1, source_target_pairs={{0,8},{4,12},{8,0},{12,4},{1,9},{5,13},{9,1},{13,5},{2,10},{6,14},... | collective-permute-start | bytes 73736 | tf_op jit(solution)/shard_map/ppermute | solution.py:457
  33.7 4.4 %collective-permute-start.15 = (bf16[96,128]{1,0:T(8,128)(2,1)S(1)}, bf16[96,128]{1,0:T(8,128)(2,1)S(1)}, u32[]{:S(2)}, u32[]{:S(2)}) collective-permute-start(bf16[96,128]{1,0:T(8,128)(2,1)S(1)} %add_convert_fusion.refs_4_.refs_0_), channel_id=1, source_target_pairs={{0,4},{4,0},{8,12},{12,8},{1,5},{5,1},{9,13},{13,9},{2,6},{6,2},{1... | collective-permute-start | bytes 73736 | tf_op jit(solution)/shard_map/ppermute | solution.py:457
  36.2 1.9 %copy-start = (bf16[16,64,1024]{2,1,0:T(8,128)(2,1)S(1)}, bf16[16,64,1024]{2,1,0:T(8,128)(2,1)}, u32[]{:S(2)}) copy-start(bf16[16,64,1024]{2,1,0:T(8,128)(2,1)} %param.17) | copy-start | bytes 6291460
  38.0 2.2 %copy-start.2 = (bf16[96,1024]{1,0:T(8,128)(2,1)S(1)}, bf16[96,1024]{1,0:T(8,128)(2,1)}, u32[]{:S(2)}) copy-start(bf16[96,1024]{1,0:T(8,128)(2,1)} %refs_4_.1) | copy-start | bytes 589828
  38.6 6.2 %collective-permute-start.16 = (bf16[96,1024]{1,0:T(8,128)(2,1)S(1)}, bf16[96,1024]{1,0:T(8,128)(2,1)S(1)}, u32[]{:S(2)}, u32[]{:S(2)}) collective-permute-start(bf16[96,1024]{1,0:T(8,128)(2,1)S(1)} %up.3), channel_id=1, source_target_pairs={{0,2},{2,0},{1,3},{3,1},{4,6},{6,4},{5,7},{7,5},{8,10},{10,8},{9,1... | collective-permute-start | bytes 589832 | tf_op jit(solution)/shard_map/ppermute | solution.py:457

commit v6 on v5

--- a/solution.py
+++ b/solution.py
@@ -495,8 +495,9 @@
         part = down(ids, down_own, owned_count, rank, own + fronts, 2, [backs[0], other[0]])
         backs = [swapped(b, "adapter", j) for j, b in zip(shifts, backs)]
         routed = [join(fronts), join(backs, ())]
-        part = part + swapped(part, "mp")
-        part = (part + swapped(part, "kv")).astype(jnp.bfloat16)
+        chip = splits * lax.axis_size("kv")
+        across = lax.ppermute(part, ("mp", "kv"), [(i, chip - 1 - i) for i in range(chip)])
+        part = (part + swapped(part, "mp") + swapped(part, "kv") + across).astype(jnp.bfloat16)
         mids = [part] + [swapped(part, "adapter", j) for j in range(owners - 1, 0, -1)]
         own_rest, other_rest = restore(
             ids, routed, [swapped(r, "kv") for r in routed], part, owned_count, shifts

time: 45.7 us -> 45.6 us (level)
    ppermute x0 -> x1, starting transfers between devices: none -> 0.65 us  [local(): lax.ppermute(part, ('mp', 'kv'), [(i, chip - 1 - i) for i in range(chip)])]
    ppermute x17, starting transfers between devices: 21 us -> 20.4 us  [swapped(): lax.ppermute(x, axis, [(i, i ^ other) for i in range(lax.axis_size(axis))])]
  transfers between devices with their start and end apart: 17 -> 18, of which waited for: 3 -> 4; matrix products, arithmetic and copies ran while one was open for 0% -> 0% of each run, Pallas kernels for 16% -> 16%
where the time goes in v6:
time: 45.6 us; the launch traced here: 45.5 us
  starting transfers between devices  21.1 us (46%)
  Pallas kernels  12.6 us (28%)
  waiting for transfers between devices  11.5 us (25%)
    ppermute x17, starting transfers between devices, swapped(): lax.ppermute(x, axis, [(i, i ^ other) for i in range(lax.axis_size(axis))])  20.4 us
    ppermute x17, waiting for transfers between devices, swapped(): lax.ppermute(x, axis, [(i, i ^ other) for i in range(lax.axis_size(axis))])  11.1 us
    pallas_call x1, Pallas kernels, attend_away(): pl.pallas_call(functools.partial(attend_away_body, features // kv_feature...  3.63 us
    pallas_call x1, Pallas kernels, attend_own(): pl.pallas_call(functools.partial(attend_own_body, group), in_specs=[pl.Bl...  1.99 us
    pallas_call x1, Pallas kernels, base_projection(): pl.pallas_call(functools.partial(base_body, count, unit, min(256, columns...  1.83 us
    pallas_call x1, Pallas kernels, down(): pl.pallas_call(functools.partial(down_body, count, plain, rank, owned_cou...  1.29 us
    pallas_call x2, Pallas kernels, up(): pl.pallas_call(functools.partial(up_body, len(mids), rank, which, residua...  1.06 us
  transfers between devices with their start and end apart: 18, of which 4 were waited for; matrix products, arithmetic and copies ran while one was open for 0% of the time, Pallas kernels for 16%

profile of v6, /device:TPU:0, one launch (start us, length us, event | category | flops | bytes accessed | tf_op | source)
XLA Modules:
  0.0 45.5 jit_solution(14122722565753031694)
XLA Ops:
  0.0 3.6 %attend_away.1 = (f32[48,2048]{1,0:T(8,128)S(1)}, f32[48,128]{1,0:T(8,128)S(1)}, bf16[3,16,2048]{2,1,0:T(8,128)(2,1)S(1)}, bf16[3,16,64,256]{3,2,1,0:T(8,128)(2,1)S(1)}, bf16[3,16,64,256]{3,2,1,0:T(8,128)(2,1)S(1)}) custom-call(s32[48]{0:T(128)} %lengths.1, bf16[48,4096]{1,0:T(8,128)(2,1)} %q_hbm.1, bf16[48,64,512]{2,1,0:T(8,128)(2,1)} %k_hbm.1, ...), custom_call_target="tpu_custom_call" | custom-call | flops 1000 | bytes 1000 | tf_op jit(solution)/shard_map/attend_away/pallas_call | solution.py:127
  4.3 2.0 %attend_own.1 = (f32[48,2048]{1,0:T(8,128)S(1)}, f32[48,128]{1,0:T(8,128)S(1)}) custom-call(s32[48]{0:T(128)S(1)} %copy-done.3, bf16[3,16,2048]{2,1,0:T(8,128)(2,1)S(1)} %get-tuple-element.19.q_ref, bf16[3,16,64,256]{3,2,1,0:T(8,128)(2,1)S(1)} %get-tuple-element.20.k_ref, bf16[3,16,64,256]{3,2,1,0:T(8,128)(2,1)S(1)} %get-tuple-element.21.v_ref), custom_call_target="tpu_custom_call" | custom-call | flops 1000 | bytes 1000 | tf_op jit(solution)/shard_map/attend_own/pallas_call | solution.py:156
  6.4 0.6 %merge.1 = (bf16[48,2048]{1,0:T(8,128)(2,1)S(1)}, bf16[24,2048]{1,0:T(8,128)(2,1)S(1)}, bf16[24,2048]{1,0:T(8,128)(2,1)S(1)}) custom-call(f32[48,2048]{1,0:T(8,128)S(1)} %get-tuple-element.22.own_ref, f32[48,128]{1,0:T(8,128)S(1)} %get-tuple-element.23.own_level, f32[48,2048]{1,0:T(8,128)S(1)} %collective-permute-done.other_ref, ...), custom_call_target="tpu_custom_call" | custom-call | flops 1000 | bytes 1000 | tf_op jit(solution)/shard_map/merge/pallas_call | solution.py:214
  7.0 3.1 %collective-permute-start.2 = (bf16[48,2048]{1,0:T(8,128)(2,1)S(1)}, bf16[48,2048]{1,0:T(8,128)(2,1)S(1)}, u32[]{:S(2)}, u32[]{:S(2)}) collective-permute-start(bf16[48,2048]{1,0:T(8,128)(2,1)S(1)} %get-tuple-element.26.rows_ref.refs_0_), channel_id=1, source_target_pairs={{0,4},{4,0},{8,12},{12,8},{1,5},{5,1},{9,13},{13,9},{2,6},{6,2},{1... | collective-permute-start | bytes 589832 | tf_op jit(solution)/shard_map/ppermute | solution.py:457
  10.1 2.6 %collective-permute-start.3 = (bf16[24,2048]{1,0:T(8,128)(2,1)S(1)}, bf16[24,2048]{1,0:T(8,128)(2,1)S(1)}, u32[]{:S(2)}, u32[]{:S(2)}) collective-permute-start(bf16[24,2048]{1,0:T(8,128)(2,1)S(1)} %get-tuple-element.27), channel_id=1, source_target_pairs={{0,8},{4,12},{8,0},{12,4},{1,9},{5,13},{9,1},{13,5},{2,10},{6,14},... | collective-permute-start | bytes 294920 | tf_op jit(solution)/shard_map/ppermute | solution.py:457
  12.7 4.8 %collective-permute-done.3.refs_0_._.refs_2_ = bf16[24,2048]{1,0:T(8,128)(2,1)S(1)} collective-permute-done((bf16[24,2048]{1,0:T(8,128)(2,1)S(1)}, bf16[24,2048]{1,0:T(8,128)(2,1)S(1)}, u32[]{:S(2)}, u32[]{:S(2)}) %collective-permute-start.3) | collective-permute-done | bytes 98336 | tf_op jit(solution)/shard_map/ppermute | solution.py:457
  17.5 0.6 %route_rest.1 = (bf16[24,2048]{1,0:T(8,128)(2,1)S(1)}, bf16[24,2048]{1,0:T(8,128)(2,1)S(1)}) custom-call(s32[192,128]{1,0:T(8,128)S(1)} %broadcast_in_dim.2.ids_ref, bf16[48,2048]{1,0:T(8,128)(2,1)S(1)} %get-tuple-element.26.rows_ref.refs_0_, bf16[24,2048]{1,0:T(8,128)(2,1)S(1)} %collective-permute-done.3.refs_0_._.refs_2_), custom_call_target="tpu_custom_call" | custom-call | flops 1000 | bytes 1000 | tf_op jit(solution)/shard_map/route_rest/pallas_call | solution.py:232
  18.1 3.5 %collective-permute-start.5 = (bf16[24,2048]{1,0:T(8,128)(2,1)S(1)}, bf16[24,2048]{1,0:T(8,128)(2,1)S(1)}, u32[]{:S(2)}, u32[]{:S(2)}) collective-permute-start(bf16[24,2048]{1,0:T(8,128)(2,1)S(1)} %get-tuple-element.29.refs_4_), channel_id=1, source_target_pairs={{0,8},{4,12},{8,0},{12,4},{1,9},{5,13},{9,1},{13,5},{2,10},{6,14},... | collective-permute-start | bytes 294920 | tf_op jit(solution)/shard_map/ppermute | solution.py:457
  21.6 2.5 %collective-permute-start.6 = (bf16[24,2048]{1,0:T(8,128)(2,1)S(1)}, bf16[24,2048]{1,0:T(8,128)(2,1)S(1)}, u32[]{:S(2)}, u32[]{:S(2)}) collective-permute-start(bf16[24,2048]{1,0:T(8,128)(2,1)S(1)} %get-tuple-element.30), channel_id=1, source_target_pairs={{0,12},{4,8},{8,4},{12,0},{1,13},{5,9},{9,5},{13,1},{2,14},{6,10},... | collective-permute-start | bytes 294920 | tf_op jit(solution)/shard_map/ppermute | solution.py:457
  24.1 1.3 %down.1 = f32[96,128]{1,0:T(8,128)S(1)} custom-call(s32[192,128]{1,0:T(8,128)S(1)} %broadcast_in_dim.2.ids_ref, bf16[512,2048]{1,0:T(8,128)(2,1)S(1)} %bitcast.8, bf16[48,2048]{1,0:T(8,128)(2,1)S(1)} %get-tuple-element.26.rows_ref.refs_0_, bf16[48,2048]{1,0:T(8,128)(2,1)S(1)} %collective-permute-done.2.refs_1_, ...), custom_call_target="tpu_custom_call" | custom-call | flops 1000 | bytes 1000 | tf_op jit(solution)/shard_map/down/pallas_call | solution.py:342
  25.4 1.5 %collective-permute-start.10 = (f32[96,128]{1,0:T(8,128)S(1)}, f32[96,128]{1,0:T(8,128)S(1)}, u32[]{:S(2)}, u32[]{:S(2)}) collective-permute-start(f32[96,128]{1,0:T(8,128)S(1)} %down.1), channel_id=1, source_target_pairs={{0,2},{2,0},{1,3},{3,1},{4,6},{6,4},{5,7},{7,5},{8,10},{10,8},{9,1... | collective-permute-start | bytes 147464 | tf_op jit(solution)/shard_map/ppermute | solution.py:457
  26.9 0.7 %collective-permute-start.12 = (f32[96,128]{1,0:T(8,128)S(1)}, f32[96,128]{1,0:T(8,128)S(1)}, u32[]{:S(2)}, u32[]{:S(2)}) collective-permute-start(f32[96,128]{1,0:T(8,128)S(1)} %down.1), channel_id=1, source_target_pairs={{0,3},{1,2},{2,1},{3,0},{4,7},{5,6},{6,5},{7,4},{8,11},{9,10},{10,... | collective-permute-start | bytes 147464 | tf_op jit(solution)/shard_map/ppermute | solution.py:499
  27.6 1.8 %collective-permute-done.5.refs_0_ = bf16[24,2048]{1,0:T(8,128)(2,1)S(1)} collective-permute-done((bf16[24,2048]{1,0:T(8,128)(2,1)S(1)}, bf16[24,2048]{1,0:T(8,128)(2,1)S(1)}, u32[]{:S(2)}, u32[]{:S(2)}) %collective-permute-start.5) | collective-permute-done | bytes 98336 | tf_op jit(solution)/shard_map/ppermute | solution.py:457
  29.4 0.6 %collective-permute-start.8 = (bf16[2,24,2048]{2,1,0:T(8,128)(2,1)S(1)}, bf16[2,24,2048]{2,1,0:T(8,128)(2,1)S(1)}, u32[]{:S(2)}, u32[]{:S(2)}) collective-permute-start(bf16[2,24,2048]{2,1,0:T(8,128)(2,1)S(1)} %join.3.refs_1_), channel_id=1, source_target_pairs={{0,1},{1,0},{2,3},{3,2},{4,5},{5,4},{6,7},{7,6},{8,9},{9,8},{10,11... | collective-permute-start | bytes 589832 | tf_op jit(solution)/shard_map/ppermute | solution.py:457
  30.5 2.2 %collective-permute-start.14 = (bf16[96,128]{1,0:T(8,128)(2,1)S(1)}, bf16[96,128]{1,0:T(8,128)(2,1)S(1)}, u32[]{:S(2)}, u32[]{:S(2)}) collective-permute-start(bf16[96,128]{1,0:T(8,128)(2,1)S(1)} %add_convert_fusion.refs_4_.refs_0_), channel_id=1, source_target_pairs={{0,12},{4,8},{8,4},{12,0},{1,13},{5,9},{9,5},{13,1},{2,14},{6,10},... | collective-permute-start | bytes 73736 | tf_op jit(solution)/shard_map/ppermute | solution.py:457
  32.7 1.0 %collective-permute-start.15 = (bf16[96,128]{1,0:T(8,128)(2,1)S(1)}, bf16[96,128]{1,0:T(8,128)(2,1)S(1)}, u32[]{:S(2)}, u32[]{:S(2)}) collective-permute-start(bf16[96,128]{1,0:T(8,128)(2,1)S(1)} %add_convert_fusion.refs_4_.refs_0_), channel_id=1, source_target_pairs={{0,8},{4,12},{8,0},{12,4},{1,9},{5,13},{9,1},{13,5},{2,10},{6,14},... | collective-permute-start | bytes 73736 | tf_op jit(solution)/shard_map/ppermute | solution.py:457
  33.7 1.2 %collective-permute-start.16 = (bf16[96,128]{1,0:T(8,128)(2,1)S(1)}, bf16[96,128]{1,0:T(8,128)(2,1)S(1)}, u32[]{:S(2)}, u32[]{:S(2)}) collective-permute-start(bf16[96,128]{1,0:T(8,128)(2,1)S(1)} %add_convert_fusion.refs_4_.refs_0_), channel_id=1, source_target_pairs={{0,4},{4,0},{8,12},{12,8},{1,5},{5,1},{9,13},{13,9},{2,6},{6,2},{1... | collective-permute-start | bytes 73736 | tf_op jit(solution)/shard_map/ppermute | solution.py:457
  34.9 0.8 %restore.1 = (bf16[96,2048]{1,0:T(8,128)(2,1)S(1)}, bf16[96,2048]{1,0:T(8,128)(2,1)S(1)}) custom-call(s32[192,128]{1,0:T(8,128)S(1)} %broadcast_in_dim.2.ids_ref, bf16[2,24,2048]{2,1,0:T(8,128)(2,1)S(1)} %join.2.refs_0_, bf16[2,24,2048]{2,1,0:T(8,128)(2,1)S(1)} %join.3.refs_1_, bf16[2,24,2048]{2,1,0:T(8,128)(2,1)S(1)} %collective-permute-done.7.refs_2_, ...), custom_call_target="tpu_custom_call" | custom-call | flops 1000 | bytes 1000 | tf_op jit(solution)/shard_map/restore/pallas_call | solution.py:286
  35.8 1.8 %base.1.base_ref = f32[192,1024]{1,0:T(8,128)S(1)} custom-call(bf16[4096,1024]{1,0:T(8,128)(2,1)S(1)} %bitcast.7, bf16[48,2048]{1,0:T(8,128)(2,1)S(1)} %get-tuple-element.26.rows_ref.refs_0_, bf16[48,2048]{1,0:T(8,128)(2,1)S(1)} %collective-permute-done.2.refs_1_, bf16[96,2048]{1,0:T(8,128)(2,1)S(1)} %get-tuple-element.31.refs_2_, ...), custom_call_target="tpu_custom_call" | custom-call | flops 1000 | bytes 1000 | tf_op jit(solution)/shard_map/base/pallas_call | solution.py:445
  37.7 0.5 %up.3 = bf16[96,1024]{1,0:T(8,128)(2,1)S(1)} custom-call(s32[192,128]{1,0:T(8,128)S(1)} %broadcast_in_dim.2.ids_ref, f32[192,1024]{1,0:T(8,128)S(1)} %base.1.base_ref, bf16[1024,1024]{1,0:T(8,128)(2,1)S(1)} %bitcast.4, bf16[96,128]{1,0:T(8,128)(2,1)S(1)} %add_convert_fusion.refs_4_.refs_0_, bf16[96,128]{1,0:T(8,128)(2,1)S(1)} %collective-permute-done.14.refs_1_, ...), custom_call_target="tpu_custom_call" | custom-call | flops 1000 | bytes 1000 | tf_op jit(solution)/shard_map/up/pallas_call | solution.py:394
  38.2 1.5 %collective-permute-start.17 = (bf16[96,1024]{1,0:T(8,128)(2,1)S(1)}, bf16[96,1024]{1,0:T(8,128)(2,1)S(1)}, u32[]{:S(2)}, u32[]{:S(2)}) collective-permute-start(bf16[96,1024]{1,0:T(8,128)(2,1)S(1)} %up.3), channel_id=1, source_target_pairs={{0,2},{2,0},{1,3},{3,1},{4,6},{6,4},{5,7},{7,5},{8,10},{10,8},{9,1... | collective-permute-start | bytes 589832 | tf_op jit(solution)/shard_map/ppermute | solution.py:457
  39.7 0.5 %up.2.kept_ref = f32[96,1024]{1,0:T(8,128)S(1)} custom-call(s32[192,128]{1,0:T(8,128)S(1)} %broadcast_in_dim.2.ids_ref, f32[192,1024]{1,0:T(8,128)S(1)} %base.1.base_ref, bf16[1024,1024]{1,0:T(8,128)(2,1)S(1)} %bitcast.5, bf16[96,128]{1,0:T(8,128)(2,1)S(1)} %add_convert_fusion.refs_4_.refs_0_, bf16[96,128]{1,0:T(8,128)(2,1)S(1)} %collective-permute-done.14.refs_1_, ...), custom_call_target="tpu_custom_call" | custom-call | flops 1000 | bytes 1000 | tf_op jit(solution)/shard_map/up/pallas_call | solution.py:394
  40.3 4.5 %collective-permute-done.17.back_ref = bf16[96,1024]{1,0:T(8,128)(2,1)S(1)} collective-permute-done((bf16[96,1024]{1,0:T(8,128)(2,1)S(1)}, bf16[96,1024]{1,0:T(8,128)(2,1)S(1)}, u32[]{:S(2)}, u32[]{:S(2)}) %collective-permute-start.17) | collective-permute-done | bytes 196640 | tf_op jit(solution)/shard_map/ppermute | solution.py:457
  44.8 0.7 %last.1 = bf16[96,1024]{1,0:T(8,128)(2,1)} custom-call(f32[96,1024]{1,0:T(8,128)S(1)} %up.2.kept_ref, bf16[96,1024]{1,0:T(8,128)(2,1)S(1)} %collective-permute-done.17.back_ref), custom_call_target="tpu_custom_call" | custom-call | tf_op jit(solution)/shard_map/last/pallas_call | solution.py:412
  (41 shorter events, 1.3 us)
Async XLA Ops:
  0.0 4.3 %copy-start.3 = (s32[48]{0:T(128)S(1)}, s32[48]{0:T(128)}, u32[]{:S(2)}) copy-start(s32[48]{0:T(128)} %lengths.1) | copy-start | bytes 580
  0.0 35.8 %slice-start = ((s8[8388608]{0:T(1024)(128)(4,1)}), s8[4194304]{0:T(1024)(128)(4,1)S(1)}, s32[]{:S(2)}) async-start(s8[8388608]{0:T(1024)(128)(4,1)} %bitcast.6), calls=%async_computation | async-start | bytes 8388608
  3.6 2.6 %copy-start.4 = (s32[192]{0:T(256)S(1)}, s32[192]{0:T(256)}, u32[]{:S(2)}) copy-start(s32[192]{0:T(256)} %param.13) | copy-start | bytes 2308
  3.7 2.6 %collective-permute-start = (f32[48,2048]{1,0:T(8,128)S(1)}, f32[48,2048]{1,0:T(8,128)S(1)}, u32[]{:S(2)}, u32[]{:S(2)}) collective-permute-start(f32[48,2048]{1,0:T(8,128)S(1)} %get-tuple-element.24), channel_id=1, source_target_pairs={{0,1},{1,0},{2,3},{3,2},{4,5},{5,4},{6,7},{7,6},{8,9},{9,8},{10,11... | collective-permute-start | bytes 1179656 | tf_op jit(solution)/shard_map/ppermute | solution.py:457
  4.2 2.1 %collective-permute-start.1 = (f32[48,128]{1,0:T(8,128)S(1)}, f32[48,128]{1,0:T(8,128)S(1)}, u32[]{:S(2)}, u32[]{:S(2)}) collective-permute-start(f32[48,128]{1,0:T(8,128)S(1)} %get-tuple-element.25), channel_id=1, source_target_pairs={{0,1},{1,0},{2,3},{3,2},{4,5},{5,4},{6,7},{7,6},{8,9},{9,8},{10,11... | collective-permute-start | bytes 73736 | tf_op jit(solution)/shard_map/ppermute | solution.py:457
  4.3 19.8 %copy-start.1 = (bf16[8,2048,64]{1,2,0:T(8,128)(2,1)S(1)}, bf16[8,2048,64]{1,2,0:T(8,128)(2,1)}, u32[]{:S(2)}) copy-start(bf16[8,2048,64]{1,2,0:T(8,128)(2,1)} %param.16) | copy-start | bytes 6291460
  4.3 31.5 %slice-start.1 = ((s8[8388608]{0:T(1024)(128)(4,1)}), s8[4194304]{0:T(1024)(128)(4,1)S(1)}, s32[]{:S(2)}) async-start(s8[8388608]{0:T(1024)(128)(4,1)} %bitcast.6), calls=%async_computation.1 | async-start | bytes 8388608
  7.0 17.1 %collective-permute-start.2 = (bf16[48,2048]{1,0:T(8,128)(2,1)S(1)}, bf16[48,2048]{1,0:T(8,128)(2,1)S(1)}, u32[]{:S(2)}, u32[]{:S(2)}) collective-permute-start(bf16[48,2048]{1,0:T(8,128)(2,1)S(1)} %get-tuple-element.26.rows_ref.refs_0_), channel_id=1, source_target_pairs={{0,4},{4,0},{8,12},{12,8},{1,5},{5,1},{9,13},{13,9},{2,6},{6,2},{1... | collective-permute-start | bytes 589832 | tf_op jit(solution)/shard_map/ppermute | solution.py:457
  10.1 14.0 %collective-permute-start.9 = (bf16[48,2048]{1,0:T(8,128)(2,1)S(1)}, bf16[48,2048]{1,0:T(8,128)(2,1)S(1)}, u32[]{:S(2)}, u32[]{:S(2)}) collective-permute-start(bf16[48,2048]{1,0:T(8,128)(2,1)S(1)} %get-tuple-element.26.rows_ref.refs_0_), channel_id=1, source_target_pairs={{0,1},{1,0},{2,3},{3,2},{4,5},{5,4},{6,7},{7,6},{8,9},{9,8},{10,11... | collective-permute-start | bytes 589832 | tf_op jit(solution)/shard_map/ppermute | solution.py:457
  10.1 7.4 %collective-permute-start.3 = (bf16[24,2048]{1,0:T(8,128)(2,1)S(1)}, bf16[24,2048]{1,0:T(8,128)(2,1)S(1)}, u32[]{:S(2)}, u32[]{:S(2)}) collective-permute-start(bf16[24,2048]{1,0:T(8,128)(2,1)S(1)} %get-tuple-element.27), channel_id=1, source_target_pairs={{0,8},{4,12},{8,0},{12,4},{1,9},{5,13},{9,1},{13,5},{2,10},{6,14},... | collective-permute-start | bytes 294920 | tf_op jit(solution)/shard_map/ppermute | solution.py:457
  12.7 11.4 %collective-permute-start.4 = (bf16[24,2048]{1,0:T(8,128)(2,1)S(1)}, bf16[24,2048]{1,0:T(8,128)(2,1)S(1)}, u32[]{:S(2)}, u32[]{:S(2)}) collective-permute-start(bf16[24,2048]{1,0:T(8,128)(2,1)S(1)} %get-tuple-element.28), channel_id=1, source_target_pairs={{0,12},{4,8},{8,4},{12,0},{1,13},{5,9},{9,5},{13,1},{2,14},{6,10},... | collective-permute-start | bytes 294920 | tf_op jit(solution)/shard_map/ppermute | solution.py:457
  18.1 11.3 %collective-permute-start.5 = (bf16[24,2048]{1,0:T(8,128)(2,1)S(1)}, bf16[24,2048]{1,0:T(8,128)(2,1)S(1)}, u32[]{:S(2)}, u32[]{:S(2)}) collective-permute-start(bf16[24,2048]{1,0:T(8,128)(2,1)S(1)} %get-tuple-element.29.refs_4_), channel_id=1, source_target_pairs={{0,8},{4,12},{8,0},{12,4},{1,9},{5,13},{9,1},{13,5},{2,10},{6,14},... | collective-permute-start | bytes 294920 | tf_op jit(solution)/shard_map/ppermute | solution.py:457
  21.6 7.8 %collective-permute-start.6 = (bf16[24,2048]{1,0:T(8,128)(2,1)S(1)}, bf16[24,2048]{1,0:T(8,128)(2,1)S(1)}, u32[]{:S(2)}, u32[]{:S(2)}) collective-permute-start(bf16[24,2048]{1,0:T(8,128)(2,1)S(1)} %get-tuple-element.30), channel_id=1, source_target_pairs={{0,12},{4,8},{8,4},{12,0},{1,13},{5,9},{9,5},{13,1},{2,14},{6,10},... | collective-permute-start | bytes 294920 | tf_op jit(solution)/shard_map/ppermute | solution.py:457
  25.4 4.6 %collective-permute-start.10 = (f32[96,128]{1,0:T(8,128)S(1)}, f32[96,128]{1,0:T(8,128)S(1)}, u32[]{:S(2)}, u32[]{:S(2)}) collective-permute-start(f32[96,128]{1,0:T(8,128)S(1)} %down.1), channel_id=1, source_target_pairs={{0,2},{2,0},{1,3},{3,1},{4,6},{6,4},{5,7},{7,5},{8,10},{10,8},{9,1... | collective-permute-start | bytes 147464 | tf_op jit(solution)/shard_map/ppermute | solution.py:457
  26.9 3.1 %collective-permute-start.11 = (f32[96,128]{1,0:T(8,128)S(1)}, f32[96,128]{1,0:T(8,128)S(1)}, u32[]{:S(2)}, u32[]{:S(2)}) collective-permute-start(f32[96,128]{1,0:T(8,128)S(1)} %down.1), channel_id=1, source_target_pairs={{0,1},{1,0},{2,3},{3,2},{4,5},{5,4},{6,7},{7,6},{8,9},{9,8},{10,11... | collective-permute-start | bytes 147464 | tf_op jit(solution)/shard_map/ppermute | solution.py:457
  26.9 3.5 %collective-permute-start.12 = (f32[96,128]{1,0:T(8,128)S(1)}, f32[96,128]{1,0:T(8,128)S(1)}, u32[]{:S(2)}, u32[]{:S(2)}) collective-permute-start(f32[96,128]{1,0:T(8,128)S(1)} %down.1), channel_id=1, source_target_pairs={{0,3},{1,2},{2,1},{3,0},{4,7},{5,6},{6,5},{7,4},{8,11},{9,10},{10,... | collective-permute-start | bytes 147464 | tf_op jit(solution)/shard_map/ppermute | solution.py:499
  29.4 4.3 %collective-permute-start.7 = (bf16[2,24,2048]{2,1,0:T(8,128)(2,1)S(1)}, bf16[2,24,2048]{2,1,0:T(8,128)(2,1)S(1)}, u32[]{:S(2)}, u32[]{:S(2)}) collective-permute-start(bf16[2,24,2048]{2,1,0:T(8,128)(2,1)S(1)} %join.2.refs_0_), channel_id=1, source_target_pairs={{0,1},{1,0},{2,3},{3,2},{4,5},{5,4},{6,7},{7,6},{8,9},{9,8},{10,11... | collective-permute-start | bytes 589832 | tf_op jit(solution)/shard_map/ppermute | solution.py:457
  29.4 5.5 %collective-permute-start.8 = (bf16[2,24,2048]{2,1,0:T(8,128)(2,1)S(1)}, bf16[2,24,2048]{2,1,0:T(8,128)(2,1)S(1)}, u32[]{:S(2)}, u32[]{:S(2)}) collective-permute-start(bf16[2,24,2048]{2,1,0:T(8,128)(2,1)S(1)} %join.3.refs_1_), channel_id=1, source_target_pairs={{0,1},{1,0},{2,3},{3,2},{4,5},{5,4},{6,7},{7,6},{8,9},{9,8},{10,11... | collective-permute-start | bytes 589832 | tf_op jit(solution)/shard_map/ppermute | solution.py:457
  30.0 5.8 %collective-permute-start.13 = (bf16[48,2048]{1,0:T(8,128)(2,1)S(1)}, bf16[48,2048]{1,0:T(8,128)(2,1)S(1)}, u32[]{:S(2)}, u32[]{:S(2)}) collective-permute-start(bf16[48,2048]{1,0:T(8,128)(2,1)S(1)} %collective-permute-done.2.refs_1_), channel_id=1, source_target_pairs={{0,1},{1,0},{2,3},{3,2},{4,5},{5,4},{6,7},{7,6},{8,9},{9,8},{10,11... | collective-permute-start | bytes 589832 | tf_op jit(solution)/shard_map/ppermute | solution.py:457
  30.5 7.2 %collective-permute-start.14 = (bf16[96,128]{1,0:T(8,128)(2,1)S(1)}, bf16[96,128]{1,0:T(8,128)(2,1)S(1)}, u32[]{:S(2)}, u32[]{:S(2)}) collective-permute-start(bf16[96,128]{1,0:T(8,128)(2,1)S(1)} %add_convert_fusion.refs_4_.refs_0_), channel_id=1, source_target_pairs={{0,12},{4,8},{8,4},{12,0},{1,13},{5,9},{9,5},{13,1},{2,14},{6,10},... | collective-permute-start | bytes 73736 | tf_op jit(solution)/shard_map/ppermute | solution.py:457
  32.7 5.0 %collective-permute-start.15 = (bf16[96,128]{1,0:T(8,128)(2,1)S(1)}, bf16[96,128]{1,0:T(8,128)(2,1)S(1)}, u32[]{:S(2)}, u32[]{:S(2)}) collective-permute-start(bf16[96,128]{1,0:T(8,128)(2,1)S(1)} %add_convert_fusion.refs_4_.refs_0_), channel_id=1, source_target_pairs={{0,8},{4,12},{8,0},{12,4},{1,9},{5,13},{9,1},{13,5},{2,10},{6,14},... | collective-permute-start | bytes 73736 | tf_op jit(solution)/shard_map/ppermute | solution.py:457
  33.7 4.0 %collective-permute-start.16 = (bf16[96,128]{1,0:T(8,128)(2,1)S(1)}, bf16[96,128]{1,0:T(8,128)(2,1)S(1)}, u32[]{:S(2)}, u32[]{:S(2)}) collective-permute-start(bf16[96,128]{1,0:T(8,128)(2,1)S(1)} %add_convert_fusion.refs_4_.refs_0_), channel_id=1, source_target_pairs={{0,4},{4,0},{8,12},{12,8},{1,5},{5,1},{9,13},{13,9},{2,6},{6,2},{1... | collective-permute-start | bytes 73736 | tf_op jit(solution)/shard_map/ppermute | solution.py:457
  37.7 2.1 %copy-start.2 = (bf16[96,1024]{1,0:T(8,128)(2,1)S(1)}, bf16[96,1024]{1,0:T(8,128)(2,1)}, u32[]{:S(2)}) copy-start(bf16[96,1024]{1,0:T(8,128)(2,1)} %refs_4_.1) | copy-start | bytes 589828
  38.2 6.5 %collective-permute-start.17 = (bf16[96,1024]{1,0:T(8,128)(2,1)S(1)}, bf16[96,1024]{1,0:T(8,128)(2,1)S(1)}, u32[]{:S(2)}, u32[]{:S(2)}) collective-permute-start(bf16[96,1024]{1,0:T(8,128)(2,1)S(1)} %up.3), channel_id=1, source_target_pairs={{0,2},{2,0},{1,3},{3,1},{4,6},{6,4},{5,7},{7,5},{8,10},{10,8},{9,1... | collective-permute-start | bytes 589832 | tf_op jit(solution)/shard_map/ppermute | solution.py:457
  (1 other events, 1.9 us)
